TPU v7x, 512 devices: a whole 4x8x8 slice. The times are simulated.
512 devices in a mesh: sess: 32 (over y, x), tensor: 16 (over z, core).
Axes of the slice: x: 4, y: 8, z: 8, core: 2. Of those that a mesh axis runs over, the one named last changes fastest.
Arguments:
- hidden: bfloat16 [32, 8192], P('sess'), may hold values from -6 to 6
- key_value_weight: bfloat16 [8192, 2048], P(None, 'tensor'), may hold values from -0.0625 to 0.0625
- adapter_down_maps: bfloat16 [64, 2, 64, 8192], P('sess', None, 'tensor'), may hold values from -0.0625 to 0.0625
- adapter_up_maps: bfloat16 [64, 2, 64, 1024], P('sess', None, 'tensor'), may hold values from -0.75 to 0.75
- session_slot: int32 [32], replicated, may hold values from 0 to 63, as said below
- lengths: int32 [32], P('sess'), may hold values from 2048 to 4095, as said below
- queries: bfloat16 [32, 8192], P('sess', 'tensor'), may hold values from -400 to 400
- cached_key_rows: bfloat16 [32, 4096, 1024], P('sess', 'tensor'), may hold values from -12 to 12
- cached_value_rows: bfloat16 [32, 4096, 1024], P('sess', 'tensor'), may hold values from -6 to 6
Outputs:
- new_key_value: bfloat16 [32, 2048], P('sess', 'tensor')
- attended: bfloat16 [32, 8192], P('sess', 'tensor')
Inputs may be any that keep to these rules, and one draw needn't show every extreme that they name: `session_slot`: the sessions' slots are distinct; slot q lives on index q // 2 of sess; in every draw some index of sess holds the adapters of 2 sessions. The new token takes position lengths[s]; some session has 4095.
All inputs are finite; a program needn't handle non-finite values.
Results may differ from a plain program's by a relative error of at most 0.014.
Values may be sent and summed in bfloat16 or wider, within the bound.
No kernel may reach another device: no remote copies, remote signals or barrier semaphores. Data moves between devices by JAX's collectives and lax.ppermute only.
A program may use at most 64 MiB of HBM per device.

v0:
```python
import math

import jax
import jax.numpy as jnp
from jax import lax
from jax.sharding import PartitionSpec as P

QH = 64
KVH = 8
HD = 128


ADAPTER_SCALE = 0.5
ROPE_BASE = 500000.0
MASKED = -1e30


def combined_all(x, axis, combine):
    everything = jax.tree.map(lambda part: lax.all_gather(part, axis), x)
    leading = jax.tree.map(lambda part: part[0], everything)

    def step(k, so_far):
        return combine(so_far, jax.tree.map(lambda part: part[k], everything))

    return lax.fori_loop(1, lax.axis_size(axis), step, leading)


def apply_rotation(columns_in, lengths, first_column):
    row_count = columns_in.shape[0]
    column_count = columns_in.shape[1]
    head_count = column_count // HD
    half_width = HD // 2
    shaped = columns_in.reshape(row_count, head_count, 2, half_width)
    indices = jnp.arange(half_width, dtype=jnp.float32)
    inverse = jnp.exp(-(2.0 * indices / HD) * math.log(ROPE_BASE))
    angles = lengths.astype(jnp.float32)[:, None] * inverse[None, :]
    cosine = jnp.cos(angles)[:, None, :]
    sine_part = jnp.sin(angles)[:, None, :]
    former = shaped[:, :, 0, :]
    latter = shaped[:, :, 1, :]
    turned = jnp.stack(
        [former * cosine - latter * sine_part, latter * cosine + former * sine_part], axis=2
    )
    head_ids = first_column // HD + jnp.arange(head_count, dtype=jnp.int32)
    is_keyed = (head_ids < KVH)[None, :, None, None]
    return jnp.where(is_keyed, turned, shaped).reshape(row_count, column_count)


def combine_parts(earlier, later):
    top_early, total_early, accum_early = earlier
    top_late, total_late, accum_late = later
    highest = jnp.maximum(top_early, top_late)
    factor_early = jnp.exp(top_early - highest)
    factor_late = jnp.exp(top_late - highest)
    total = total_early * factor_early + total_late * factor_late
    accum = accum_early * factor_early[..., None] + accum_late * factor_late[..., None]
    return (highest, total, accum)


def local(
    hidden,
    key_value_weight,
    adapter_down_maps,
    adapter_up_maps,
    session_slot,
    lengths,
    queries,
    cached_key_rows,
    cached_value_rows,
):
    sess_count = lax.axis_size("sess")
    tensor_count = lax.axis_size("tensor")
    sess_index = lax.axis_index("sess")
    tensor_index = lax.axis_index("tensor")
    local_rows = hidden.shape[0]
    number_of_slots = adapter_down_maps.shape[0]
    block_width = key_value_weight.shape[1]
    kv_width = KVH * HD
    group = QH // KVH
    slot_ids = sess_index * number_of_slots + jnp.arange(number_of_slots, dtype=jnp.int32)
    chooser = (session_slot[None, :] == slot_ids[:, None]).astype(jnp.bfloat16)
    selected_maps = jnp.dot(
        chooser,
        lax.all_gather(hidden, "sess", axis=0, tiled=True),
        preferred_element_type=jnp.float32,
    )
    lowrank_input = jnp.einsum(
        "sv,stzv->stz",
        selected_maps.astype(jnp.bfloat16),
        adapter_down_maps,
        preferred_element_type=jnp.float32,
    ).astype(jnp.bfloat16)
    lifted = (
        jnp.einsum(
            "meo,meob->meb", lowrank_input, adapter_up_maps, preferred_element_type=jnp.float32
        )
        * ADAPTER_SCALE
    )
    lifted = lifted.reshape(number_of_slots, 2 * kv_width)
    base_block = jnp.dot(hidden, key_value_weight, preferred_element_type=jnp.float32)
    chooser_wide = chooser.astype(jnp.float32)
    placed = jnp.einsum(
        "qij,qtc->itjc",
        chooser_wide.reshape(number_of_slots, sess_count, local_rows),
        lifted.reshape(number_of_slots, tensor_count, block_width),
        precision=lax.Precision.HIGHEST,
    )
    summed = lax.psum_scatter(
        placed.reshape(sess_count * tensor_count, local_rows, block_width),
        ("sess", "tensor"),
        scatter_dimension=0,
        tiled=True,
    )[0]
    fresh = apply_rotation(base_block + summed, lengths, tensor_index * block_width).astype(
        jnp.bfloat16
    )
    query_all, fresh_all = (
        lax.all_gather(queries, "tensor", axis=1, tiled=True),
        lax.all_gather(fresh, "tensor", axis=1, tiled=True),
    )
    span = cached_key_rows.shape[1]
    positions = tensor_index * span + jnp.arange(span, dtype=jnp.int32)
    landing = (positions[None, :] == lengths[:, None])[:, :, None]
    keys_here = jnp.where(landing, fresh_all[:, None, :kv_width], cached_key_rows)
    values_here = jnp.where(landing, fresh_all[:, None, kv_width:], cached_value_rows)
    query_heads = query_all.reshape(local_rows, KVH, group, HD)
    scores = jnp.einsum(
        "sgjd,spgd->sgjp",
        query_heads,
        keys_here.reshape(local_rows, span, KVH, HD),
        preferred_element_type=jnp.float32,
    ) * (1.0 / math.sqrt(HD))
    live = (positions[None, :] <= lengths[:, None])[:, None, None, :]
    scores = jnp.where(live, scores, MASKED)
    local_top = jnp.max(scores, axis=3)
    weights = jnp.where(live, jnp.exp(scores - local_top[..., None]), 0.0)
    local_total = jnp.sum(weights, axis=3)
    local_accum = jnp.einsum(
        "sgjp,spgd->sgjd",
        weights.astype(jnp.bfloat16),
        values_here.reshape(local_rows, span, KVH, HD),
        preferred_element_type=jnp.float32,
    )
    merged = combined_all((local_top, local_total, local_accum), "tensor", combine_parts)
    accum_all = merged[2]
    total_all = merged[1]
    attended = (accum_all / total_all[..., None]).reshape(local_rows, QH * HD)
    width_here = queries.shape[1]
    attended = lax.dynamic_slice_in_dim(attended, tensor_index * width_here, width_here, 1).astype(
        jnp.bfloat16
    )
    return (fresh, attended)


def solution(mesh):
    return jax.shard_map(
        local,
        mesh=mesh,
        in_specs=(
            P("sess", None),
            P(None, "tensor"),
            P("sess", None, "tensor", None),
            P("sess", None, "tensor", None),
            P(),
            P("sess"),
            P("sess", "tensor"),
            P("sess", "tensor", None),
            P("sess", "tensor", None),
        ),
        out_specs=(P("sess", "tensor"), P("sess", "tensor")),
        check_vma=False,
    )
```

profile of v0, /device:TPU:1, one launch (start us, length us, event | category | flops | bytes accessed | tf_op | source)
XLA Modules:
  0.0 410.7 jit_solution(7769299192015443371)
XLA Ops:
  7.3 40.9 %all-gather.4 = bf16[32,1,8192]{2,1,0:T(2,128)(2,1)S(1)} all-gather(bf16[1,1,8192]{2,1,0:T(2,128)(2,1)} %bitcast.113), channel_id=1, replica_groups=mesh['sess'=32,'tensor'=16] {'sess'}, dimensions={0}, use_global_device_ids=true | all-gather | bytes 540672 | tf_op jit(solution)/shard_map/all_gather | solution.py:84
  48.2 1.3 fusion.5
  49.5 2.3 fusion.14
  51.8 0.2 fusion.28
  52.0 0.4 convolution_bitcast_fusion
  52.4 0.9 copy.24
  53.9 35.0 %all_gather.29 = bf16[1,8192]{1,0:T(2,128)(2,1)S(1)} all-gather(bf16[1,512]{1,0:T(2,128)(2,1)S(1)} %copy-done.4), channel_id=1, replica_groups=mesh['sess'=32,'tensor'=16] {'tensor'}, dimensions={1}, use_global_device_ids=true | all-gather | bytes 17408 | tf_op jit(solution)/shard_map/all_gather | solution.py:118
  88.9 0.1 reduce.5
  89.0 244.5 %all-reduce.3.cloned.1.call-done = f32[512,1,128]{2,0,1:T(8,128)} async-done(((f32[512,1,128]{2,0,1:T(8,128)}), f32[512,1,128]{2,0,1:T(8,128)}) %all-reduce.3.cloned.1.call-update) | async-done | bytes 262160
  333.6 1.0 fusion.8
  334.9 0.5 fusion.40
  335.4 16.4 %all-gather.5 = bf16[16,1,128]{2,1,0:T(2,128)(2,1)S(1)} all-gather(bf16[1,1,128]{2,1,0:T(2,128)(2,1)S(1)} %get-tuple-element.222), channel_id=2, replica_groups=mesh['sess'=32,'tensor'=16] {'tensor'}, dimensions={0}, use_global_device_ids=true | all-gather | bytes 4352 | tf_op jit(solution)/shard_map/all_gather | solution.py:119
  351.9 0.1 select_bitcast_fusion
  352.0 0.1 copy.37
  352.1 0.1 copy.38
  352.2 0.3 fusion.42
  352.5 14.6 %all-gather.1 = f32[128,8]{1,0:T(8,128)S(1)} all-gather(f32[8,8]{1,0:T(8,128)S(1)} %get-tuple-element.228), channel_id=3, replica_groups=mesh['sess'=32,'tensor'=16] {'tensor'}, dimensions={0}, use_global_device_ids=true | all-gather | bytes 4352 | tf_op jit(solution)/shard_map/all_gather | solution.py:19
  367.2 0.2 fusion.17
  367.3 0.2 fusion.11
  367.6 18.5 %all-gather.3 = f32[128,8,128]{2,1,0:T(8,128)S(1)} all-gather(f32[8,8,128]{2,1,0:T(8,128)S(1)} %fusion.11), channel_id=5, replica_groups=mesh['sess'=32,'tensor'=16] {'tensor'}, dimensions={0}, use_global_device_ids=true | all-gather | bytes 557056 | tf_op jit(solution)/shard_map/all_gather | solution.py:19
  386.0 14.6 %all-gather.2 = f32[128,8]{1,0:T(8,128)S(1)} all-gather(f32[8,8]{1,0:T(8,128)S(1)} %fusion.17), channel_id=4, replica_groups=mesh['sess'=32,'tensor'=16] {'tensor'}, dimensions={0}, use_global_device_ids=true | all-gather | bytes 4352 | tf_op jit(solution)/shard_map/all_gather | solution.py:19
  400.7 2.5 while.19
  400.7 0.1 fusion.51
  400.9 0.1 fusion.51
  401.0 0.1 fusion.51
  401.2 0.1 fusion.51
  401.4 0.1 fusion.51
  401.5 0.1 fusion.51
  401.7 0.1 fusion.51
  401.9 0.1 fusion.51
  402.1 0.1 fusion.51
  403.3 0.6 dynamic-slice_convert_fusion
  (82 shorter events, 1.6 us)
Async XLA Ops:
  7.2 326.4 %copy-start = (bf16[8192,128]{1,0:T(8,128)(2,1)S(1)}, bf16[8192,128]{1,0:T(8,128)(2,1)}, u32[]{:S(2)}) copy-start(bf16[8192,128]{1,0:T(8,128)(2,1)} %param.12) | copy-start | bytes 6291460
  7.2 326.4 %copy-start.3 = (bf16[1,8192]{1,0:T(2,128)(2,1)S(1)}, bf16[1,8192]{1,0:T(2,128)(2,1)}, u32[]{:S(2)}) copy-start(bf16[1,8192]{1,0:T(2,128)(2,1)} %param.11) | copy-start | bytes 49156
  7.2 44.8 %copy-start.5 = (s32[32]{0:T(128)S(1)}, s32[32]{0:T(128)}, u32[]{:S(2)}) copy-start(s32[32]{0:T(128)} %param.15) | copy-start | bytes 388
  7.2 44.6 %copy-start.6 = (bf16[2,2,4,1024]{3,2,1,0:T(4,128)(2,1)S(1)}, bf16[2,2,4,1024]{3,2,1,0:T(4,128)(2,1)}, u32[]{:S(2)}) copy-start(bf16[2,2,4,1024]{3,2,1,0:T(4,128)(2,1)} %param.14) | copy-start | bytes 98308
  7.2 46.7 %copy-start.4 = (bf16[1,512]{1,0:T(2,128)(2,1)S(1)}, bf16[1,512]{1,0:T(2,128)(2,1)}, u32[]{:S(2)}) copy-start(bf16[1,512]{1,0:T(2,128)(2,1)} %param.17) | copy-start | bytes 3076
  7.2 326.3 %all-reduce.3.cloned.1.call-start = ((), (), s32[]{:S(2)}) async-start(), calls=%async_computation | async-start | bytes 524288
  49.5 302.4 %copy-start.1 = (bf16[1,256,1024]{2,1,0:T(8,128)(2,1)S(1)}, bf16[1,256,1024]{2,1,0:T(8,128)(2,1)}, u32[]{:S(2)}) copy-start(bf16[1,256,1024]{2,1,0:T(8,128)(2,1)} %param.19) | copy-start | bytes 1572868
  49.5 302.4 %copy-start.2 = (bf16[1,256,1024]{2,1,0:T(8,128)(2,1)S(1)}, bf16[1,256,1024]{2,1,0:T(8,128)(2,1)}, u32[]{:S(2)}) copy-start(bf16[1,256,1024]{2,1,0:T(8,128)(2,1)} %param.18) | copy-start | bytes 1572868
Sparse Core Ops, SparseCore 0:
  53.4 280.1 all-reduce.2
where the time goes:
time: 411 us
  waiting for transfers between devices  245 us (60%)
  blocking collectives  140 us (34%)
  between operations  14.9 us (4%)
  matrix products  5.72 us (1%)
    unnamed x2, waiting for transfers between devices  245 us
    all_gather x3, blocking collectives, combined_all(): everything = jax.tree.map(lambda part: lax.all_gather(part, axis), x)  47.7 us
    all_gather x1, blocking collectives, local(): lax.all_gather(hidden, 'sess', axis=0, tiled=True)  40.9 us
    all_gather x1, blocking collectives, local(): lax.all_gather(queries, 'tensor', axis=1, tiled=True)  35 us
    all_gather x1, blocking collectives, local(): lax.all_gather(fresh, 'tensor', axis=1, tiled=True)  16.4 us
  transfers between devices with their start and end apart: 1, of which 1 were waited for; matrix products, arithmetic and copies ran while one was open for 0% of the time, Pallas kernels for 0%

commit v1 on v0

v1 whole, which is shorter than its diff:
```python
import math

import jax
import jax.numpy as jnp
from jax import lax
from jax.sharding import PartitionSpec as P

QH = 64
KVH = 8
HD = 128
ADAPTER_SCALE = 0.5
ROPE_BASE = 500000.0
MASKED = -1e30


def rotate_head(row, cosine, sine):
    half = HD // 2
    a = row[:half]
    b = row[half:]
    return jnp.concatenate([a * cosine - b * sine, b * cosine + a * sine])


def local(
    hidden,
    key_value_weight,
    adapter_down_maps,
    adapter_up_maps,
    session_slot,
    lengths,
    queries,
    cached_key_rows,
    cached_value_rows,
):
    f32 = jnp.float32
    bf16 = jnp.bfloat16
    n_sess = lax.axis_size("sess")
    n_tensor = lax.axis_size("tensor")
    o = lax.axis_index("sess")
    t = lax.axis_index("tensor")
    slots, two, ranks, width = adapter_down_maps.shape
    kv_width = KVH * HD
    group = QH // KVH
    own_heads = QH // n_tensor
    span = cached_key_rows.shape[1]
    length = lengths[0]

    hidden_all = lax.all_to_all(
        jnp.broadcast_to(hidden, (n_sess, width)), "sess", 0, 0, tiled=True
    )
    query_all = lax.all_to_all(
        jnp.broadcast_to(queries, (n_tensor, queries.shape[1])), "tensor", 0, 0, tiled=True
    )

    down = adapter_down_maps.transpose(1, 0, 2, 3).reshape(two * slots * ranks, width)
    reduced = lax.dot_general(
        hidden_all, down, (((1,), (1,)), ((), ())), preferred_element_type=f32
    ).astype(bf16)
    slot_of_column = o * slots + jnp.arange(slots, dtype=jnp.int32)
    chosen = (session_slot[:, None] == slot_of_column[None, :])[:, None, :, None]
    reduced = jnp.where(
        chosen, reduced.reshape(n_sess, two, slots, ranks), jnp.zeros((), bf16)
    ).reshape(n_sess, two, slots * ranks)
    up = adapter_up_maps.transpose(1, 0, 2, 3).reshape(two, slots * ranks, kv_width)
    lifted = jnp.concatenate(
        [
            jnp.dot(reduced[:, k], up[k], preferred_element_type=f32)
            for k in range(two)
        ],
        axis=1,
    )
    partial = jnp.sum(
        lax.all_to_all(lifted, "sess", 0, 0, tiled=True), axis=0
    ).reshape(2 * KVH, HD)
    base = jnp.dot(hidden, key_value_weight, preferred_element_type=f32)
    blocks = jnp.arange(2 * KVH, dtype=jnp.int32)
    partial = partial * ADAPTER_SCALE + jnp.where(
        (blocks == t)[:, None], base.reshape(1, HD), 0.0
    )

    q = query_all.reshape(KVH, group, HD)
    k = cached_key_rows.reshape(span, KVH, HD)
    v = cached_value_rows.reshape(span, KVH, HD)
    positions = t * span + jnp.arange(span, dtype=jnp.int32)
    live = (positions < length)[None, None, :]
    scores = jnp.einsum("gjd,pgd->gjp", q, k, preferred_element_type=f32) * (
        1.0 / math.sqrt(HD)
    )
    scores = jnp.where(live, scores, MASKED)
    top = jnp.max(scores, axis=2)
    weights = jnp.where(live, jnp.exp(scores - top[..., None]), 0.0)
    total = jnp.sum(weights, axis=2)
    accum = jnp.einsum("gjp,pgd->gjd", weights.astype(bf16), v, preferred_element_type=f32)

    dest = jnp.arange(n_tensor, dtype=jnp.int32)
    outgoing = jnp.concatenate(
        [
            accum.reshape(n_tensor, own_heads, HD),
            jnp.broadcast_to(top.reshape(n_tensor, own_heads, 1), (n_tensor, own_heads, HD)),
            jnp.broadcast_to(total.reshape(n_tensor, own_heads, 1), (n_tensor, own_heads, HD)),
            partial[:, None],
            jnp.repeat(partial[:KVH], 2, axis=0)[:, None],
            jnp.repeat(partial[KVH:], 2, axis=0)[:, None],
            jnp.zeros((n_tensor, 1, HD), f32),
        ],
        axis=1,
    )
    incoming = lax.all_to_all(outgoing, "tensor", 0, 0, tiled=True)

    h = own_heads
    rows = jnp.sum(incoming[:, 3 * h : 3 * h + 3], axis=0)
    half = HD // 2
    inverse = jnp.exp(
        -(2.0 * jnp.arange(half, dtype=f32) / HD) * math.log(ROPE_BASE)
    )
    angles = length.astype(f32) * inverse
    cosine, sine = jnp.cos(angles), jnp.sin(angles)
    own = jnp.where(t < KVH, rotate_head(rows[0], cosine, sine), rows[0]).astype(bf16)
    new_key = rotate_head(rows[1], cosine, sine).astype(bf16)
    new_value = rows[2].astype(bf16)

    new_score = jnp.sum(
        queries.reshape(h, HD).astype(f32) * new_key.astype(f32)[None], axis=1
    ) * (1.0 / math.sqrt(HD))
    tops = incoming[:, h : 2 * h]
    new_score = jnp.broadcast_to(new_score[:, None], (h, HD))
    highest = jnp.maximum(jnp.max(tops, axis=0), new_score)
    factors = jnp.exp(tops - highest[None])
    new_weight = jnp.exp(new_score - highest)
    denom = jnp.sum(factors * incoming[:, 2 * h : 3 * h], axis=0) + new_weight
    summed = jnp.sum(factors * incoming[:, :h], axis=0) + new_weight.astype(bf16).astype(
        f32
    ) * new_value.astype(f32)[None]
    attended = (summed / denom).astype(bf16).reshape(1, h * HD)
    return (own.reshape(1, HD), attended)


def solution(mesh):
    return jax.shard_map(
        local,
        mesh=mesh,
        in_specs=(
            P("sess", None),
            P(None, "tensor"),
            P("sess", None, "tensor", None),
            P("sess", None, "tensor", None),
            P(),
            P("sess"),
            P("sess", "tensor"),
            P("sess", "tensor", None),
            P("sess", "tensor", None),
        ),
        out_specs=(P("sess", "tensor"), P("sess", "tensor")),
        check_vma=False,
    )
```

time: 411 us -> 95.1 us (0.23)
  waiting for transfers between devices: 245 us -> 30.2 us
  blocking collectives: 140 us -> 0 us
  starting transfers between devices: 0.04 us -> 37.1 us
  between operations: 14.9 us -> 1.51 us
  local copies, waits for them, and re-layouts: 1.93 us -> 12.8 us
  other arithmetic: 2.91 us -> 9.48 us
    unnamed x2 -> x0, waiting for transfers between devices: 245 us -> none
    all_gather x6 -> x0, blocking collectives: 140 us -> none  [the longest x3 47.7 us: combined_all(): everything = jax.tree.map(lambda part: lax.all_gather(part, axis), x)]
    all_to_all x0 -> x4, starting transfers between devices: none -> 37.1 us  [the longest x1 11.8 us: local(): lax.all_to_all(jnp.broadcast_to(queries, (n_tensor, queries.shape[1])), '...]
    all_to_all x0 -> x4, waiting for transfers between devices: none -> 30.2 us  [the longest x1 11.5 us: local(): lax.all_to_all(jnp.broadcast_to(hidden, (n_sess, width)), 'sess', 0, 0, t...]
    unnamed x16 -> x20, local copies, waits for them, and re-layouts: 0.23 us -> 6.79 us
    broadcast_in_dim x0 -> x2, other arithmetic: none -> 5.36 us  [the longest x1 4.63 us: local(): jnp.broadcast_to(hidden, (n_sess, width))]
  transfers between devices with their start and end apart: 1 -> 4, of which waited for: 1 -> 3; matrix products, arithmetic and copies ran while one was open for 0% -> 15% of each run, Pallas kernels for 0% -> 0%
where the time goes in v1:
time: 95.1 us; the launch traced here: 94.4 us
  starting transfers between devices  37.1 us (39%)
  waiting for transfers between devices  30.2 us (32%)
  local copies, waits for them, and re-layouts  12.8 us (13%)
  other arithmetic  9.48 us (10%)
  matrix products  3.32 us (3%)
  between operations  1.51 us (2%)
    all_to_all x1, starting transfers between devices, local(): lax.all_to_all(jnp.broadcast_to(queries, (n_tensor, queries.shape[1])), '...  11.8 us
    all_to_all x1, waiting for transfers between devices, local(): lax.all_to_all(jnp.broadcast_to(hidden, (n_sess, width)), 'sess', 0, 0, t...  11.5 us
    all_to_all x1, starting transfers between devices, local(): incoming = lax.all_to_all(outgoing, 'tensor', 0, 0, tiled=True)  10.4 us
    all_to_all x1, starting transfers between devices, local(): lax.all_to_all(jnp.broadcast_to(hidden, (n_sess, width)), 'sess', 0, 0, t...  9.83 us
    all_to_all x1, waiting for transfers between devices, local(): lax.all_to_all(lifted, 'sess', 0, 0, tiled=True)  9.53 us
    all_to_all x1, waiting for transfers between devices, local(): incoming = lax.all_to_all(outgoing, 'tensor', 0, 0, tiled=True)  9.17 us
    unnamed x20, local copies, waits for them, and re-layouts  6.79 us
    all_to_all x1, starting transfers between devices, local(): lax.all_to_all(lifted, 'sess', 0, 0, tiled=True)  4.99 us
  transfers between devices with their start and end apart: 4, of which 3 were waited for; matrix products, arithmetic and copies ran while one was open for 15% of the time, Pallas kernels for 0%

profile of v1, /device:TPU:1, one launch (start us, length us, event | category | flops | bytes accessed | tf_op | source)
XLA Modules:
  0.0 94.4 jit_solution(4267768440478477080)
XLA Ops:
  0.6 0.9 fusion.28
  1.5 0.5 broadcast.162
  2.1 0.7 reduce.5
  2.8 0.6 reshape.309
  3.4 11.8 %all-to-all-start = ((bf16[16,2,256]{2,1,0:T(2,128)(2,1)}), bf16[16,2,256]{2,1,0:T(2,128)(2,1)S(1)}, u32[]{:S(2)}, u32[]{:S(2)}) async-start(bf16[16,2,256]{2,1,0:T(2,128)(2,1)} %reshape.309), calls=%async_computation | async-start | bytes 32768 | tf_op jit(solution)/shard_map/all_to_all | solution.py:50
  15.2 0.8 reduce.3
  16.1 0.9 broadcast_in_dim.120
  17.0 4.6 %reduce.6 = bf16[32,8192]{1,0:T(8,128)(2,1)} reduce(bf16[32,1,8192]{2,1,0:T(2,128)(2,1)S(1)} %broadcast_in_dim.120, bf16[]{:T(256)} %broadcast.162), dimensions={1}, to_apply=%broadcast_in_dim.120.reduce_sub_computation | reduce | bytes 1048578 | tf_op jit(solution)/shard_map/broadcast_in_dim | solution.py:48
  21.7 2.3 %reshape.311 = bf16[32,2,4096]{2,1,0:T(2,128)(2,1)} reshape(bf16[32,8192]{1,0:T(8,128)(2,1)} %reduce.6) | data formatting | bytes 1048576
  23.9 9.8 %all-to-all-start.1 = ((bf16[32,2,4096]{2,1,0:T(2,128)(2,1)}), bf16[32,2,4096]{2,1,0:T(2,128)(2,1)S(1)}, u32[]{:S(2)}, u32[]{:S(2)}) async-start(bf16[32,2,4096]{2,1,0:T(2,128)(2,1)} %reshape.311), calls=%async_computation.1 | async-start | bytes 1048576 | tf_op jit(solution)/shard_map/all_to_all | solution.py:47
  34.4 0.9 copy.25
  35.4 1.1 %copy.26 = bf16[32,8,8,128]{3,2,1,0:T(8,128)(2,1)S(1)} copy(bf16[32,8,8,128]{3,1,2,0:T(8,128)(2,1)} %bitcast.63) | data formatting | bytes 1048576
  36.5 1.0 %copy.22 = bf16[2,2,4,8192]{3,2,1,0:T(4,128)(2,1)S(1)} copy(bf16[2,2,4,8192]{3,2,0,1:T(4,128)(2,1)} %bitcast.64) | data formatting | bytes 524288 | tf_op jit(solution)/shard_map/transpose | solution.py:54
  37.6 0.8 reshape.299
  38.4 0.4 convolution_bitcast_fusion
  39.1 11.5 %all-to-all-done.1 = bf16[32,2,4096]{2,1,0:T(2,128)(2,1)S(1)} async-done(((bf16[32,2,4096]{2,1,0:T(2,128)(2,1)}), bf16[32,2,4096]{2,1,0:T(2,128)(2,1)S(1)}, u32[]{:S(2)}, u32[]{:S(2)}) %all-to-all-start.1) | async-done | bytes 524320 | tf_op jit(solution)/shard_map/all_to_all | solution.py:47
  50.5 1.8 %reshape.312 = bf16[32,1,8192]{2,1,0:T(2,128)(2,1)} reshape(bf16[32,2,4096]{2,1,0:T(2,128)(2,1)S(1)} %all-to-all-done.1) | data formatting | bytes 1048576
  52.3 2.0 %fusion.2 = bf16[32,2,8]{0,2,1:T(8,128)(2,1)S(1)} fusion(bf16[16,8192]{1,0:T(8,128)(2,1)S(1)} %copy-done.3, bf16[32,1,8192]{2,1,0:T(2,128)(2,1)} %reshape.312, pred[32,8]{0,1:T(8,128)(4,1)S(1)} %bitcast.76), kind=kOutput, calls=%fused_computation.4 | convolution fusion | flops 8389632 | bytes 787712 | tf_op jit(solution)/shard_map/dot_general | solution.py:55
  54.3 0.2 fusion.19
  54.5 0.2 fusion.20
  54.8 1.0 %copy.23 = f32[32,1,2048]{2,1,0:T(1,128)} copy(f32[32,1,2048]{2,0,1:T(8,128)S(1)} %maximum_bitcast_fusion) | data formatting | bytes 524288 | tf_op jit(solution)/shard_map/all_to_all | solution.py:72
  55.7 5.0 %all-to-all-start.2 = ((f32[32,1,2048]{2,1,0:T(1,128)}), f32[32,1,2048]{2,1,0:T(1,128)S(1)}, u32[]{:S(2)}, u32[]{:S(2)}) async-start(f32[32,1,2048]{2,1,0:T(1,128)} %copy.23), calls=%async_computation.2 | async-start | bytes 524288 | tf_op jit(solution)/shard_map/all_to_all | solution.py:72
  60.7 0.3 fusion.29
  61.1 0.2 fusion.8
  61.4 0.2 fusion.5
  61.6 9.5 %all-to-all-done.2 = f32[32,1,2048]{2,1,0:T(1,128)S(1)} async-done(((f32[32,1,2048]{2,1,0:T(1,128)}), f32[32,1,2048]{2,1,0:T(1,128)S(1)}, u32[]{:S(2)}, u32[]{:S(2)}) %all-to-all-start.2) | async-done | bytes 262176 | tf_op jit(solution)/shard_map/all_to_all | solution.py:72
  71.1 0.2 reduce_sum.59
  71.7 1.3 %concatenate.23 = f32[16,16,128]{2,1,0:T(8,128)} concatenate(f32[16,4,128]{2,1,0:T(4,128)S(1)} %bitcast.65, f32[16,4,128]{2,1,0:T(4,128)S(1)} %broadcast_in_dim.114, f32[16,4,128]{2,1,0:T(4,128)S(1)} %broadcast_in_dim.116, f32[16,1,128]{2,1,0:T(1,128)S(1)} %fusion.17, f32[16,1,128]{2,1,0:T(1,128)S(1)} %bitcast.66, f32[16,1,128]{2,1,0:T(1,128)S(1)} %bitcast.67, ...), dimensions={1} | concatenate | bytes 262144 | tf_op jit(solution)/shard_map/concatenate | solution.py:95
  73.0 10.4 %all-to-all-start.3 = ((f32[16,16,128]{2,1,0:T(8,128)}), f32[16,16,128]{2,1,0:T(8,128)S(1)}, u32[]{:S(2)}, u32[]{:S(2)}) async-start(f32[16,16,128]{2,1,0:T(8,128)} %concatenate.23), calls=%async_computation.3 | async-start | bytes 262144 | tf_op jit(solution)/shard_map/all_to_all | solution.py:107
  83.5 9.2 %all-to-all-done.3 = f32[16,16,128]{2,1,0:T(8,128)S(1)} async-done(((f32[16,16,128]{2,1,0:T(8,128)}), f32[16,16,128]{2,1,0:T(8,128)S(1)}, u32[]{:S(2)}, u32[]{:S(2)}) %all-to-all-start.3) | async-done | bytes 131104 | tf_op jit(solution)/shard_map/all_to_all | solution.py:107
  93.1 0.6 fusion.22
  93.8 0.6 fusion.21
  (52 shorter events, 1.4 us)
Async XLA Ops:
  0.6 37.8 %copy-start = (bf16[8192,128]{1,0:T(8,128)(2,1)S(1)}, bf16[8192,128]{1,0:T(8,128)(2,1)}, u32[]{:S(2)}) copy-start(bf16[8192,128]{1,0:T(8,128)(2,1)} %param.10) | copy-start | bytes 6291460
  3.4 20.5 %all-to-all-start = ((bf16[16,2,256]{2,1,0:T(2,128)(2,1)}), bf16[16,2,256]{2,1,0:T(2,128)(2,1)S(1)}, u32[]{:S(2)}, u32[]{:S(2)}) async-start(bf16[16,2,256]{2,1,0:T(2,128)(2,1)} %reshape.309), calls=%async_computation | async-start | bytes 32768 | tf_op jit(solution)/shard_map/all_to_all | solution.py:50
  21.7 12.8 %copy-start.2 = (bf16[1,256,1024]{2,1,0:T(8,128)(2,1)S(1)}, bf16[1,256,1024]{2,1,0:T(8,128)(2,1)}, u32[]{:S(2)}) copy-start(bf16[1,256,1024]{2,1,0:T(8,128)(2,1)} %param.16) | copy-start | bytes 1572868
  23.9 14.4 %copy-start.5 = (bf16[2,2,4,1024]{3,2,1,0:T(4,128)(2,1)S(1)}, bf16[2,2,4,1024]{3,2,1,0:T(4,128)(2,1)}, u32[]{:S(2)}) copy-start(bf16[2,2,4,1024]{3,2,1,0:T(4,128)(2,1)} %param.12) | copy-start | bytes 98308
  23.9 14.5 %copy-start.4 = (bf16[1,8192]{1,0:T(2,128)(2,1)S(1)}, bf16[1,8192]{1,0:T(2,128)(2,1)}, u32[]{:S(2)}) copy-start(bf16[1,8192]{1,0:T(2,128)(2,1)} %param.9) | copy-start | bytes 49156
  23.9 26.6 %all-to-all-start.1 = ((bf16[32,2,4096]{2,1,0:T(2,128)(2,1)}), bf16[32,2,4096]{2,1,0:T(2,128)(2,1)S(1)}, u32[]{:S(2)}, u32[]{:S(2)}) async-start(bf16[32,2,4096]{2,1,0:T(2,128)(2,1)} %reshape.311), calls=%async_computation.1 | async-start | bytes 1048576 | tf_op jit(solution)/shard_map/all_to_all | solution.py:47
  35.4 3.5 %copy-start.6 = (s32[32]{0:T(128)S(1)}, s32[32]{0:T(128)}, u32[]{:S(2)}) copy-start(s32[32]{0:T(128)} %param.13) | copy-start | bytes 388
  38.3 14.0 %copy-start.3 = (bf16[16,8192]{1,0:T(8,128)(2,1)S(1)}, bf16[16,8192]{1,0:T(8,128)(2,1)}, u32[]{:S(2)}) copy-start(bf16[16,8192]{1,0:T(8,128)(2,1)} %reshape.299) | copy-start | bytes 786436
  52.3 8.4 %copy-start.1 = (bf16[32,8,8,128]{3,2,1,0:T(8,128)(2,1)S(1)}, bf16[32,8,8,128]{3,2,1,0:T(8,128)(2,1)}, u32[]{:S(2)}) copy-start(bf16[32,8,8,128]{3,2,1,0:T(8,128)(2,1)} %copy.25) | copy-start | bytes 1572868
  55.7 15.4 %all-to-all-start.2 = ((f32[32,1,2048]{2,1,0:T(1,128)}), f32[32,1,2048]{2,1,0:T(1,128)S(1)}, u32[]{:S(2)}, u32[]{:S(2)}) async-start(f32[32,1,2048]{2,1,0:T(1,128)} %copy.23), calls=%async_computation.2 | async-start | bytes 524288 | tf_op jit(solution)/shard_map/all_to_all | solution.py:72
  73.0 19.6 %all-to-all-start.3 = ((f32[16,16,128]{2,1,0:T(8,128)}), f32[16,16,128]{2,1,0:T(8,128)S(1)}, u32[]{:S(2)}, u32[]{:S(2)}) async-start(f32[16,16,128]{2,1,0:T(8,128)} %concatenate.23), calls=%async_computation.3 | async-start | bytes 262144 | tf_op jit(solution)/shard_map/all_to_all | solution.py:107

commit v2 on v1

v2 whole, which is shorter than its diff:
```python
import math

import jax
import jax.numpy as jnp
from jax import lax
from jax.experimental import pallas as pl
from jax.experimental.pallas import tpu as pltpu
from jax.sharding import PartitionSpec as P

QH = 64
KVH = 8
HD = 128
GROUP = QH // KVH
ADAPTER_SCALE = 0.5
ROPE_BASE = 500000.0
MASKED = -1e30
F32 = jnp.float32
BF16 = jnp.bfloat16

VMEM = pl.BlockSpec(memory_space=pltpu.VMEM)
SMEM = pl.BlockSpec(memory_space=pltpu.SMEM)


def call(body, out_shape, specs, args, cost):
    return pl.pallas_call(
        body,
        out_shape=out_shape,
        in_specs=specs,
        out_specs=jax.tree.map(lambda _: VMEM, out_shape),
        cost_estimate=pl.CostEstimate(flops=cost, bytes_accessed=cost, transcendentals=0),
        compiler_params=pltpu.CompilerParams(vmem_limit_bytes=24 * 1024 * 1024),
    )(*args)


def holder(slot_ref, slot, n_sess):
    index = jnp.int32(0)
    found = jnp.int32(0)
    for s in range(n_sess):
        hit = slot_ref[s] == slot
        index = jnp.where(hit, jnp.int32(s), index)
        found = jnp.where(hit, jnp.int32(1), found)
    return index, found


def spread_kernel(hidden_ref, out_ref):
    n, rows, lanes = out_ref.shape
    part = rows * lanes
    start = pl.multiple_of(lax.axis_index("tensor") * part, part)
    x = hidden_ref[:, pl.ds(start, part)].astype(F32)
    x = jnp.concatenate([x[:, j * lanes : (j + 1) * lanes] for j in range(rows)], axis=0)
    out_ref[...] = jnp.broadcast_to(x[None], out_ref.shape)


def select_kernel(slot_ref, arrived_ref, query_ref, out_ref):
    n_sess = arrived_ref.shape[0]
    o = lax.axis_index("sess")
    t = lax.axis_index("tensor")
    first, _ = holder(slot_ref, 2 * o, n_sess)
    second, _ = holder(slot_ref, 2 * o + 1, n_sess)
    q = query_ref[...].astype(F32)
    q = jnp.concatenate([q[:, j * HD : (j + 1) * HD] for j in range(4)], axis=0)
    even = jnp.bitwise_and(t, 1) == 0
    zero = jnp.zeros_like(q)
    block = jnp.concatenate(
        [
            jnp.where(even, q, zero),
            jnp.where(even, zero, q),
            arrived_ref[first],
            arrived_ref[second],
        ],
        axis=0,
    ).astype(BF16)
    out_ref[...] = jnp.broadcast_to(block[None], out_ref.shape)


def adapter_kernel(slot_ref, arrived_ref, down_ref, up_ref, out_ref):
    n_sess = out_ref.shape[0]
    n_tensor = arrived_ref.shape[0]
    ranks = down_ref.shape[0] // 2
    o = lax.axis_index("sess")
    x = arrived_ref[...].astype(F32)[:, 8:, :]
    upper = lax.broadcasted_iota(jnp.int32, (8, HD), 0) < 4
    reduced = [[], []]
    for row in range(2 * ranks):
        d = down_ref[row].astype(F32).reshape(n_tensor, 8, HD)
        total = jnp.sum(x * d, axis=0)
        for a in range(2):
            kept = jnp.where(upper if a == 0 else ~upper, total, 0.0)
            value = jnp.sum(jnp.sum(kept, axis=0, keepdims=True), axis=1, keepdims=True)
            reduced[a].append(value.astype(BF16).astype(F32))
    out_ref[...] = jnp.zeros(out_ref.shape, out_ref.dtype)
    for a in range(2):
        lifted = []
        for k in range(2):
            acc = None
            for r in range(ranks):
                term = reduced[a][k * ranks + r] * up_ref[(a * 2 + k) * ranks + r]
                acc = term if acc is None else acc + term
            lifted.append(acc)
        lifted = (jnp.concatenate(lifted, axis=0) * ADAPTER_SCALE).astype(out_ref.dtype)
        index, found = holder(slot_ref, 2 * o + a, n_sess)

        @pl.when(found == 1)
        def _():
            out_ref[index] = lifted


def attention_kernel(length_ref, arrived_ref, key_ref, value_ref, out_ref):
    span = key_ref.shape[1]
    t = lax.axis_index("tensor")
    length = length_ref[0]
    k = key_ref[0]
    v = value_ref[0]
    scores = []
    for g in range(KVH):
        q = (
            arrived_ref[2 * g].astype(F32)[:8] + arrived_ref[2 * g + 1].astype(F32)[:8]
        ).astype(BF16)
        scores.append(
            lax.dot_general(
                q,
                k[:, g * HD : (g + 1) * HD],
                (((1,), (1,)), ((), ())),
                preferred_element_type=F32,
            )
        )
    s = jnp.concatenate(scores, axis=0) * (1.0 / math.sqrt(HD))
    live = (t * span + lax.broadcasted_iota(jnp.int32, s.shape, 1)) < length
    s = jnp.where(live, s, MASKED)
    top = jnp.max(s, axis=1, keepdims=True)
    w = jnp.where(live, jnp.exp(s - top), 0.0)
    total = jnp.sum(w, axis=1, keepdims=True)
    wb = w.astype(BF16)
    lane = lax.broadcasted_iota(jnp.int32, (QH, HD), 1)
    head = jnp.bitwise_and(lax.broadcasted_iota(jnp.int32, (QH, HD), 0), 3)
    stats = jnp.where(lane == head, top, 0.0) + jnp.where(lane == head + 4, total, 0.0)
    zero = jnp.zeros((3, HD), F32)
    for g in range(KVH):
        acc = jnp.dot(
            wb[g * GROUP : (g + 1) * GROUP],
            v[:, g * HD : (g + 1) * HD],
            preferred_element_type=F32,
        )
        for half in range(2):
            rows = slice(4 * half, 4 * half + 4)
            stat = jnp.sum(stats[g * GROUP : (g + 1) * GROUP][rows], axis=0, keepdims=True)
            out_ref[2 * g + half] = jnp.concatenate([acc[rows], zero, stat], axis=0)


def pack_kernel(slot_ref, arrived_ref, base_ref, partial_ref, out_ref):
    s = lax.axis_index("sess")
    t = lax.axis_index("tensor")
    owner = lax.shift_right_logical(slot_ref[s], 1)
    row = lax.broadcasted_iota(jnp.int32, (2 * KVH, HD), 0)
    p = arrived_ref[owner].astype(F32) + jnp.where(row == t, base_ref[...], 0.0)
    out_ref[...] = partial_ref[...]
    for d in range(out_ref.shape[0]):
        g = d // 2
        out_ref[d, 4:7, :] = jnp.concatenate(
            [p[d : d + 1], p[g : g + 1], p[KVH + g : KVH + g + 1]], axis=0
        )


def merge_kernel(rot_ref, query_ref, arrived_ref, fresh_ref, attended_ref):
    r = arrived_ref[...]
    n = r.shape[0]
    sums = jnp.sum(r, axis=0)
    own, key, value = sums[4:5], sums[5:6], sums[6:7]
    half = HD // 2
    own = own * rot_ref[2:3] + pltpu.roll(own, half, 1) * rot_ref[3:4]
    key = key * rot_ref[0:1] + pltpu.roll(key, half, 1) * rot_ref[1:2]
    fresh_ref[...] = own.astype(BF16)
    key = key.astype(BF16).astype(F32)
    value = value.astype(BF16).astype(F32)
    q = query_ref[...].astype(F32)
    q = jnp.concatenate([q[:, j * HD : (j + 1) * HD] for j in range(4)], axis=0)
    new_score = jnp.sum(q * key, axis=1, keepdims=True) * (1.0 / math.sqrt(HD))
    shape = (n, 8, HD)
    picked = lax.broadcasted_iota(jnp.int32, shape, 1) == lax.broadcasted_iota(
        jnp.int32, shape, 2
    )
    stats = jnp.sum(
        jnp.where(picked, jnp.broadcast_to(r[:, 7:8, :], shape), 0.0), axis=2, keepdims=True
    )
    tops, totals = stats[:, :4], stats[:, 4:]
    highest = jnp.maximum(jnp.max(tops, axis=0), new_score)
    factors = jnp.exp(tops - highest[None])
    weight = jnp.exp(new_score - highest)
    denom = jnp.sum(factors * totals, axis=0) + weight
    summed = jnp.sum(factors * r[:, :4, :], axis=0) + weight.astype(BF16).astype(F32) * value
    result = (summed / denom).astype(BF16).astype(F32)
    for j in range(4):
        attended_ref[:, j * HD : (j + 1) * HD] = result[j : j + 1].astype(BF16)


def local(
    hidden,
    key_value_weight,
    adapter_down_maps,
    adapter_up_maps,
    session_slot,
    lengths,
    queries,
    cached_key_rows,
    cached_value_rows,
):
    n_sess = lax.axis_size("sess")
    n_tensor = lax.axis_size("tensor")
    t = lax.axis_index("tensor")
    slots, two, ranks, width = adapter_down_maps.shape
    part = width // n_tensor // HD
    shape = jax.ShapeDtypeStruct

    parts = call(spread_kernel, shape((n_sess, part, HD), F32), [VMEM], [hidden], 10**5)
    parts = lax.all_to_all(parts, "sess", 0, 0, tiled=True)

    block = call(
        select_kernel,
        shape((n_tensor, 16, HD), BF16),
        [SMEM, VMEM, VMEM],
        [session_slot, parts, queries],
        10**5,
    )
    block = lax.all_to_all(block, "tensor", 0, 0, tiled=True)

    down = (
        adapter_down_maps.reshape(slots, two, ranks, n_tensor, part, HD)
        .transpose(1, 2, 3, 0, 4, 5)
        .reshape(two * ranks, n_tensor * slots * part, HD)
    )
    up = adapter_up_maps.reshape(slots * two * ranks, KVH, HD).astype(F32)
    terms = call(
        adapter_kernel,
        shape((n_sess, 2 * KVH, HD), BF16),
        [SMEM, VMEM, VMEM, VMEM],
        [session_slot, block, down, up],
        10**6,
    )
    terms = lax.all_to_all(terms, "sess", 0, 0, tiled=True)

    partial = call(
        attention_kernel,
        shape((n_tensor, 8, HD), F32),
        [SMEM, VMEM, VMEM, VMEM],
        [lengths, block, cached_key_rows, cached_value_rows],
        10**7,
    )
    base = jnp.dot(hidden, key_value_weight, preferred_element_type=F32)
    packed = call(
        pack_kernel,
        shape((n_tensor, 8, HD), F32),
        [SMEM, VMEM, VMEM, VMEM],
        [session_slot, terms, base, partial],
        10**5,
    )
    packed = lax.all_to_all(packed, "tensor", 0, 0, tiled=True)

    half = HD // 2
    inverse = jnp.exp(-(2.0 * jnp.arange(half, dtype=F32) / HD) * math.log(ROPE_BASE))
    angles = lengths[0].astype(F32) * inverse
    cosine, sine = jnp.cos(angles), jnp.sin(angles)
    cosine = jnp.concatenate([cosine, cosine])
    sine = jnp.concatenate([-sine, sine])
    keyed = t < KVH
    rot = jnp.stack(
        [cosine, sine, jnp.where(keyed, cosine, 1.0), jnp.where(keyed, sine, 0.0)]
    )
    return call(
        merge_kernel,
        (shape((1, HD), BF16), shape((1, 4 * HD), BF16)),
        [VMEM, VMEM, VMEM],
        [rot, queries, packed],
        10**5,
    )


def solution(mesh):
    return jax.shard_map(
        local,
        mesh=mesh,
        in_specs=(
            P("sess", None),
            P(None, "tensor"),
            P("sess", None, "tensor", None),
            P("sess", None, "tensor", None),
            P(),
            P("sess"),
            P("sess", "tensor"),
            P("sess", "tensor", None),
            P("sess", "tensor", None),
        ),
        out_specs=(P("sess", "tensor"), P("sess", "tensor")),
        check_vma=False,
    )
```

time: 95.1 us -> 76.7 us (0.81)
  local copies, waits for them, and re-layouts: 12.8 us -> 6.67 us
  waiting for transfers between devices: 30.2 us -> 24.4 us
  Pallas kernels: 0 us -> 5.75 us
  other arithmetic: 9.48 us -> 3.86 us
  starting transfers between devices: 37.1 us -> 32.9 us
  matrix products: 3.32 us -> 1.13 us
    all_to_all x4, waiting for transfers between devices: 30.2 us -> 24.4 us  [the longest x1 8.27 us: local(): terms = lax.all_to_all(terms, 'sess', 0, 0, tiled=True)]
    pallas_call x0 -> x6, Pallas kernels: none -> 5.75 us  [call(): pl.pallas_call(body, out_shape=out_shape, in_specs=specs, out_specs=jax.t...]
    broadcast_in_dim x2 -> x0, other arithmetic: 5.36 us -> none  [the longest x1 4.63 us: local(): jnp.broadcast_to(hidden, (n_sess, width))]
    all_to_all x4, starting transfers between devices: 37.1 us -> 32.9 us  [the longest x1 12.6 us: local(): block = lax.all_to_all(block, 'tensor', 0, 0, tiled=True)]
    unnamed x20 -> x24, local copies, waits for them, and re-layouts: 6.79 us -> 2.93 us
    dot_general x6 -> x1, matrix products: 3.32 us -> 1.13 us  [local(): base = jnp.dot(hidden, key_value_weight, preferred_element_type=F32)]
    reshape x2, local copies, waits for them, and re-layouts: 0.79 us -> 2.97 us  [local(): adapter_down_maps.reshape(slots, two, ranks, n_tensor, part, HD)]
    convert_element_type x4 -> x0, other arithmetic: 2.13 us -> none  [the longest x1 0.87 us: local(): queries.reshape(h, HD).astype(f32) * new_key.astype(f32)[None]]
  transfers between devices with their start and end apart: 4 -> 4, of which waited for: 3 -> 4; matrix products, arithmetic and copies ran while one was open for 15% -> 11% of each run, Pallas kernels for 0% -> 1%
where the time goes in v2:
time: 76.7 us; the launch traced here: 76.1 us
  starting transfers between devices  32.9 us (43%)
  waiting for transfers between devices  24.4 us (32%)
  local copies, waits for them, and re-layouts  6.67 us (9%)
  Pallas kernels  5.75 us (7%)
  other arithmetic  3.86 us (5%)
  between operations  1.39 us (2%)
  matrix products  1.13 us (1%)
    all_to_all x1, starting transfers between devices, local(): block = lax.all_to_all(block, 'tensor', 0, 0, tiled=True)  12.6 us
    all_to_all x1, starting transfers between devices, local(): parts = lax.all_to_all(parts, 'sess', 0, 0, tiled=True)  10.5 us
    all_to_all x1, waiting for transfers between devices, local(): terms = lax.all_to_all(terms, 'sess', 0, 0, tiled=True)  8.27 us
    all_to_all x1, waiting for transfers between devices, local(): packed = lax.all_to_all(packed, 'tensor', 0, 0, tiled=True)  7.7 us
    all_to_all x1, starting transfers between devices, local(): packed = lax.all_to_all(packed, 'tensor', 0, 0, tiled=True)  5.82 us
    all_to_all x1, waiting for transfers between devices, local(): parts = lax.all_to_all(parts, 'sess', 0, 0, tiled=True)  5.77 us
    pallas_call x6, Pallas kernels, call(): pl.pallas_call(body, out_shape=out_shape, in_specs=specs, out_specs=jax.t...  5.75 us
    all_to_all x1, starting transfers between devices, local(): terms = lax.all_to_all(terms, 'sess', 0, 0, tiled=True)  3.99 us
  transfers between devices with their start and end apart: 4, of which 4 were waited for; matrix products, arithmetic and copies ran while one was open for 11% of the time, Pallas kernels for 1%

profile of v2, /device:TPU:1, one launch (start us, length us, event | category | flops | bytes accessed | tf_op | source)
XLA Modules:
  0.0 76.1 jit_solution(4199078916524292001)
XLA Ops:
  0.6 0.0 copy-start
  0.7 0.9 %copy-done.3 = bf16[1,8192]{1,0:T(2,128)(2,1)S(1)} copy-done((bf16[1,8192]{1,0:T(2,128)(2,1)S(1)}, bf16[1,8192]{1,0:T(2,128)(2,1)}, u32[]{:S(2)}) %copy-start.3) | copy-done | bytes 16408
  1.6 0.6 shard_map.104
  2.2 10.5 %all-to-all-start = ((f32[32,4,128]{2,1,0:T(4,128)}), f32[32,4,128]{2,1,0:T(4,128)S(1)}, u32[]{:S(2)}, u32[]{:S(2)}) async-start(f32[32,4,128]{2,1,0:T(4,128)} %shard_map.104), calls=%async_computation | async-start | bytes 131072 | tf_op jit(solution)/shard_map/all_to_all | solution.py:215
  13.3 0.1 fusion.5
  13.4 0.6 negate_bitcast_fusion
  14.0 0.6 fusion.4
  14.6 0.6 fusion.6
  15.2 0.6 fusion.2
  15.8 5.8 %all-to-all-done.arrived_ref = f32[32,4,128]{2,1,0:T(4,128)S(1)} async-done(((f32[32,4,128]{2,1,0:T(4,128)}), f32[32,4,128]{2,1,0:T(4,128)S(1)}, u32[]{:S(2)}, u32[]{:S(2)}) %all-to-all-start) | async-done | bytes 65568 | tf_op jit(solution)/shard_map/all_to_all | solution.py:215
  21.5 0.7 copy-done.4
  22.2 0.7 copy-done.6
  22.9 1.2 %shard_map.105 = bf16[16,16,128]{2,1,0:T(8,128)(2,1)} custom-call(s32[32]{0:T(128)S(1)} %copy-done.6, f32[32,4,128]{2,1,0:T(4,128)S(1)} %all-to-all-done.arrived_ref, bf16[1,512]{1,0:T(2,128)(2,1)S(1)} %copy-done.4), custom_call_target="tpu_custom_call" | custom-call | flops 100000 | bytes 100000 | tf_op jit(solution)/shard_map/pallas_call | solution.py:25
  24.1 12.6 %all-to-all-start.1 = ((bf16[16,16,128]{2,1,0:T(8,128)(2,1)}), bf16[16,16,128]{2,1,0:T(8,128)(2,1)S(1)}, u32[]{:S(2)}, u32[]{:S(2)}) async-start(bf16[16,16,128]{2,1,0:T(8,128)(2,1)} %shard_map.105), calls=%async_computation.1 | async-start | bytes 131072 | tf_op jit(solution)/shard_map/all_to_all | solution.py:224
  36.6 0.6 maximum_bitcast_fusion
  37.2 1.9 %reshape.61 = bf16[2,2,4,16,4,128]{5,4,3,2,1,0:T(4,128)(2,1)} reshape(bf16[2,2,4,8192]{3,2,1,0:T(4,128)(2,1)} %param.11) | data formatting | bytes 524288 | tf_op jit(solution)/shard_map/reshape | solution.py:227
  39.2 1.0 %copy.11 = bf16[2,2,4,16,4,128]{5,4,0,3,2,1:T(4,128)(2,1)S(1)} copy(bf16[2,2,4,16,4,128]{5,4,3,2,1,0:T(4,128)(2,1)} %reshape.61) | data formatting | bytes 524288 | tf_op jit(solution)/shard_map/reshape | solution.py:227
  40.2 0.0 copy-start.8
  40.2 0.8 %reshape.64.up_ref = f32[16,8,128]{2,1,0:T(8,128)S(1)} reshape(bf16[2,2,4,1024]{3,2,1,0:T(4,128)(2,1)} %param.12) | data formatting | bytes 98304 | tf_op jit(solution)/shard_map/convert_element_type | solution.py:231
  41.0 0.8 %broadcast_select_fusion = (f32[1,128]{1,0:T(1,128)S(1)}, f32[1,128]{1,0:T(1,128)S(1)}) fusion(pred[]{:T(512)S(6)} %lt.3, f32[1,64]{1,0:T(1,128)S(1)} %fusion.5, f32[1,64]{1,0:T(1,128)} %negate_bitcast_fusion, f32[1,64]{1,0:T(1,128)} %fusion.4), kind=kLoop, calls=%fused_computation.3 | loop fusion | flops 512 | bytes 1793 | tf_op jit(solution)/shard_map/jit(_where)/select_n | solution.py:266
  41.8 2.7 %all-to-all-done.1.arrived_ref = bf16[16,16,128]{2,1,0:T(8,128)(2,1)S(1)} async-done(((bf16[16,16,128]{2,1,0:T(8,128)(2,1)}), bf16[16,16,128]{2,1,0:T(8,128)(2,1)S(1)}, u32[]{:S(2)}, u32[]{:S(2)}) %all-to-all-start.1) | async-done | bytes 65568 | tf_op jit(solution)/shard_map/all_to_all | solution.py:224
  44.5 0.7 copy-done.7
  45.1 1.4 %shard_map.106 = bf16[32,16,128]{2,1,0:T(8,128)(2,1)} custom-call(s32[32]{0:T(128)S(1)} %copy-done.7, bf16[16,16,128]{2,1,0:T(8,128)(2,1)S(1)} %all-to-all-done.1.arrived_ref, bf16[8,128,128]{2,1,0:T(8,128)(2,1)S(1)} %bitcast.19, f32[16,8,128]{2,1,0:T(8,128)S(1)} %reshape.64.up_ref), custom_call_target="tpu_custom_call" | custom-call | flops 1000000 | bytes 1000000 | tf_op jit(solution)/shard_map/pallas_call | solution.py:25
  46.5 4.0 %all-to-all-start.2 = ((bf16[32,16,128]{2,1,0:T(8,128)(2,1)}), bf16[32,16,128]{2,1,0:T(8,128)(2,1)S(1)}, u32[]{:S(2)}, u32[]{:S(2)}) async-start(bf16[32,16,128]{2,1,0:T(8,128)(2,1)} %shard_map.106), calls=%async_computation.2 | async-start | bytes 262144 | tf_op jit(solution)/shard_map/all_to_all | solution.py:239
  50.5 1.1 %fusion.base_ref = f32[1,128]{1,0:T(1,128)S(1)} fusion(bf16[8192,128]{1,0:T(8,128)(2,1)S(1)} %copy-done, bf16[1,8192]{1,0:T(2,128)(2,1)} %hidden_ref.1), kind=kOutput, calls=%fused_computation | convolution fusion | flops 2097152 | bytes 2114048 | tf_op jit(solution)/shard_map/dot_general | solution.py:248
  51.6 0.5 shard_map.107.partial_ref
  52.1 8.3 %all-to-all-done.2.arrived_ref = bf16[32,16,128]{2,1,0:T(8,128)(2,1)S(1)} async-done(((bf16[32,16,128]{2,1,0:T(8,128)(2,1)}), bf16[32,16,128]{2,1,0:T(8,128)(2,1)S(1)}, u32[]{:S(2)}, u32[]{:S(2)}) %all-to-all-start.2) | async-done | bytes 131104 | tf_op jit(solution)/shard_map/all_to_all | solution.py:239
  60.4 1.2 %shard_map.108 = f32[16,8,128]{2,1,0:T(8,128)} custom-call(s32[32]{0:T(128)S(1)} %copy-done.8, bf16[32,16,128]{2,1,0:T(8,128)(2,1)S(1)} %all-to-all-done.2.arrived_ref, f32[1,128]{1,0:T(1,128)S(1)} %fusion.base_ref, f32[16,8,128]{2,1,0:T(8,128)S(1)} %shard_map.107.partial_ref), custom_call_target="tpu_custom_call" | custom-call | flops 100000 | bytes 100000 | tf_op jit(solution)/shard_map/pallas_call | solution.py:25
  61.6 5.8 %all-to-all-start.3 = ((f32[16,8,128]{2,1,0:T(8,128)}), f32[16,8,128]{2,1,0:T(8,128)S(1)}, u32[]{:S(2)}, u32[]{:S(2)}) async-start(f32[16,8,128]{2,1,0:T(8,128)} %shard_map.108), calls=%async_computation.3 | async-start | bytes 131072 | tf_op jit(solution)/shard_map/all_to_all | solution.py:256
  67.4 0.1 maximum_bitcast_fusion.1
  67.5 7.7 %all-to-all-done.3.arrived_ref = f32[16,8,128]{2,1,0:T(8,128)S(1)} async-done(((f32[16,8,128]{2,1,0:T(8,128)}), f32[16,8,128]{2,1,0:T(8,128)S(1)}, u32[]{:S(2)}, u32[]{:S(2)}) %all-to-all-start.3) | async-done | bytes 65568 | tf_op jit(solution)/shard_map/all_to_all | solution.py:256
  75.2 0.9 %shard_map.109 = (bf16[1,128]{1,0:T(2,128)(2,1)}, bf16[1,512]{1,0:T(2,128)(2,1)}) custom-call(f32[4,128]{1,0:T(4,128)S(1)} %pad_maximum_fusion.rot_ref, bf16[1,512]{1,0:T(2,128)(2,1)S(1)} %copy-done.5, f32[16,8,128]{2,1,0:T(8,128)S(1)} %all-to-all-done.3.arrived_ref), custom_call_target="tpu_custom_call" | custom-call | flops 100000 | bytes 100000 | tf_op jit(solution)/shard_map/pallas_call | solution.py:25
  (19 shorter events, 0.0 us)
Async XLA Ops:
  0.6 49.9 %copy-start = (bf16[8192,128]{1,0:T(8,128)(2,1)S(1)}, bf16[8192,128]{1,0:T(8,128)(2,1)}, u32[]{:S(2)}) copy-start(bf16[8192,128]{1,0:T(8,128)(2,1)} %param.10) | copy-start | bytes 6291460
  0.6 0.9 %copy-start.3 = (bf16[1,8192]{1,0:T(2,128)(2,1)S(1)}, bf16[1,8192]{1,0:T(2,128)(2,1)}, u32[]{:S(2)}) copy-start(bf16[1,8192]{1,0:T(2,128)(2,1)} %hidden_ref.1) | copy-start | bytes 49156
  2.2 19.3 %all-to-all-start = ((f32[32,4,128]{2,1,0:T(4,128)}), f32[32,4,128]{2,1,0:T(4,128)S(1)}, u32[]{:S(2)}, u32[]{:S(2)}) async-start(f32[32,4,128]{2,1,0:T(4,128)} %shard_map.104), calls=%async_computation | async-start | bytes 131072 | tf_op jit(solution)/shard_map/all_to_all | solution.py:215
  21.5 0.7 copy-start.4
  22.2 0.7 copy-start.6
  24.1 27.6 %copy-start.1 = (bf16[1,256,1024]{2,1,0:T(8,128)(2,1)S(1)}, bf16[1,256,1024]{2,1,0:T(8,128)(2,1)}, u32[]{:S(2)}) copy-start(bf16[1,256,1024]{2,1,0:T(8,128)(2,1)} %key_ref.1) | copy-start | bytes 1572868
  24.1 27.6 %copy-start.2 = (bf16[1,256,1024]{2,1,0:T(8,128)(2,1)S(1)}, bf16[1,256,1024]{2,1,0:T(8,128)(2,1)}, u32[]{:S(2)}) copy-start(bf16[1,256,1024]{2,1,0:T(8,128)(2,1)} %value_ref.1) | copy-start | bytes 1572868
  24.1 20.4 %all-to-all-start.1 = ((bf16[16,16,128]{2,1,0:T(8,128)(2,1)}), bf16[16,16,128]{2,1,0:T(8,128)(2,1)S(1)}, u32[]{:S(2)}, u32[]{:S(2)}) async-start(bf16[16,16,128]{2,1,0:T(8,128)(2,1)} %shard_map.105), calls=%async_computation.1 | async-start | bytes 131072 | tf_op jit(solution)/shard_map/all_to_all | solution.py:224
  40.2 20.2 %copy-start.8 = (s32[32]{0:T(128)S(1)}, s32[32]{0:T(128)}, u32[]{:S(2)}) copy-start(s32[32]{0:T(128)} %slot_ref.5) | copy-start | bytes 388
  44.5 0.7 copy-start.7
  46.5 20.9 %copy-start.10 = (f32[64]{0:T(128)S(1)}, f32[64]{0:T(128)}, u32[]{:S(2)}) copy-start(f32[64]{0:T(128)} %fusion.6) | copy-start | bytes 772
  46.5 20.9 %copy-start.11 = (f32[64]{0:T(128)S(1)}, f32[64]{0:T(128)}, u32[]{:S(2)}) copy-start(f32[64]{0:T(128)} %get-tuple-element.4) | copy-start | bytes 772
  46.5 21.0 %copy-start.9 = (f32[1,128]{1,0:T(1,128)S(1)}, f32[1,128]{1,0:T(1,128)}, u32[]{:S(2)}) copy-start(f32[1,128]{1,0:T(1,128)} %maximum_bitcast_fusion) | copy-start | bytes 1540
  46.5 28.7 %copy-start.5 = (bf16[1,512]{1,0:T(2,128)(2,1)S(1)}, bf16[1,512]{1,0:T(2,128)(2,1)}, u32[]{:S(2)}) copy-start(bf16[1,512]{1,0:T(2,128)(2,1)} %query_ref.3) | copy-start | bytes 3076
  46.5 13.9 %all-to-all-start.2 = ((bf16[32,16,128]{2,1,0:T(8,128)(2,1)}), bf16[32,16,128]{2,1,0:T(8,128)(2,1)S(1)}, u32[]{:S(2)}, u32[]{:S(2)}) async-start(bf16[32,16,128]{2,1,0:T(8,128)(2,1)} %shard_map.106), calls=%async_computation.2 | async-start | bytes 262144 | tf_op jit(solution)/shard_map/all_to_all | solution.py:239
  61.6 13.6 %all-to-all-start.3 = ((f32[16,8,128]{2,1,0:T(8,128)}), f32[16,8,128]{2,1,0:T(8,128)S(1)}, u32[]{:S(2)}, u32[]{:S(2)}) async-start(f32[16,8,128]{2,1,0:T(8,128)} %shard_map.108), calls=%async_computation.3 | async-start | bytes 131072 | tf_op jit(solution)/shard_map/all_to_all | solution.py:256

commit v3 on v2

--- a/solution.py
+++ b/solution.py
@@ -19,6 +19,7 @@
 
 VMEM = pl.BlockSpec(memory_space=pltpu.VMEM)
 SMEM = pl.BlockSpec(memory_space=pltpu.SMEM)
+HBM = pl.BlockSpec(memory_space=pltpu.HBM)
 
 
 def call(body, out_shape, specs, args, cost):
@@ -26,7 +27,9 @@
         body,
         out_shape=out_shape,
         in_specs=specs,
-        out_specs=jax.tree.map(lambda _: VMEM, out_shape),
+        out_specs=jax.tree.map(
+            lambda x: SMEM if getattr(x, "memory_space", None) == pltpu.SMEM else VMEM, out_shape
+        ),
         cost_estimate=pl.CostEstimate(flops=cost, bytes_accessed=cost, transcendentals=0),
         compiler_params=pltpu.CompilerParams(vmem_limit_bytes=24 * 1024 * 1024),
     )(*args)
@@ -42,70 +45,76 @@
     return index, found
 
 
-def spread_kernel(hidden_ref, out_ref):
-    n, rows, lanes = out_ref.shape
-    part = rows * lanes
-    start = pl.multiple_of(lax.axis_index("tensor") * part, part)
-    x = hidden_ref[:, pl.ds(start, part)].astype(F32)
-    x = jnp.concatenate([x[:, j * lanes : (j + 1) * lanes] for j in range(rows)], axis=0)
-    out_ref[...] = jnp.broadcast_to(x[None], out_ref.shape)
-
-
-def select_kernel(slot_ref, arrived_ref, query_ref, out_ref):
-    n_sess = arrived_ref.shape[0]
+def spread_kernel(
+    slot_hbm, hidden_hbm, query_hbm, out_hbm, query_out, index_ref, slot, hidden, query, chunks, sem, out_sem
+):
+    copies = [
+        pltpu.make_async_copy(hidden_hbm, hidden, sem.at[0]),
+        pltpu.make_async_copy(query_hbm, query, sem.at[1]),
+        pltpu.make_async_copy(slot_hbm, slot, sem.at[2]),
+    ]
+    for copy in copies:
+        copy.start()
+    n_sess, rows, lanes = out_hbm.shape
     o = lax.axis_index("sess")
     t = lax.axis_index("tensor")
-    first, _ = holder(slot_ref, 2 * o, n_sess)
-    second, _ = holder(slot_ref, 2 * o + 1, n_sess)
-    q = query_ref[...].astype(F32)
+    copies[0].wait()
+    x = hidden[...].astype(F32)
+    x = jnp.concatenate([x[:, j * lanes : (j + 1) * lanes] for j in range(rows)], axis=0)
+    x = x.astype(BF16)
+    sends = []
+    step = n_sess // 4
+    for s in range(4):
+        places = pl.ds(s * step, step)
+        chunks[places] = jnp.broadcast_to(x[None], (step, rows, lanes))
+        sends.append(pltpu.make_async_copy(chunks.at[places], out_hbm.at[places], out_sem.at[s]))
+        sends[-1].start()
+    copies[1].wait()
+    q = query[...].astype(F32)
     q = jnp.concatenate([q[:, j * HD : (j + 1) * HD] for j in range(4)], axis=0)
     even = jnp.bitwise_and(t, 1) == 0
     zero = jnp.zeros_like(q)
-    block = jnp.concatenate(
-        [
-            jnp.where(even, q, zero),
-            jnp.where(even, zero, q),
-            arrived_ref[first],
-            arrived_ref[second],
-        ],
-        axis=0,
-    ).astype(BF16)
-    out_ref[...] = jnp.broadcast_to(block[None], out_ref.shape)
-
-
-def adapter_kernel(slot_ref, arrived_ref, down_ref, up_ref, out_ref):
-    n_sess = out_ref.shape[0]
-    n_tensor = arrived_ref.shape[0]
-    ranks = down_ref.shape[0] // 2
-    o = lax.axis_index("sess")
-    x = arrived_ref[...].astype(F32)[:, 8:, :]
-    upper = lax.broadcasted_iota(jnp.int32, (8, HD), 0) < 4
-    reduced = [[], []]
-    for row in range(2 * ranks):
-        d = down_ref[row].astype(F32).reshape(n_tensor, 8, HD)
-        total = jnp.sum(x * d, axis=0)
-        for a in range(2):
-            kept = jnp.where(upper if a == 0 else ~upper, total, 0.0)
-            value = jnp.sum(jnp.sum(kept, axis=0, keepdims=True), axis=1, keepdims=True)
-            reduced[a].append(value.astype(BF16).astype(F32))
+    query_out[...] = jnp.concatenate(
+        [jnp.where(even, q, zero), jnp.where(even, zero, q)], axis=0
+    )
+    copies[2].wait()
+    for a in range(2):
+        index, found = holder(slot, 2 * o + a, n_sess)
+        index_ref[2 * a] = index
+        index_ref[2 * a + 1] = found
+    index_ref[4] = lax.shift_right_logical(slot[o], 1)
+    for send in sends:
+        send.wait()
+
+
+def adapter_kernel(index_ref, arrived_ref, down_ref, up_ref, out_ref, mark_ref):
+    ranks = down_ref.shape[2]
+    rows, lanes = arrived_ref.shape[1:]
+    mark_ref[0] = jnp.int32(0)
     out_ref[...] = jnp.zeros(out_ref.shape, out_ref.dtype)
     for a in range(2):
-        lifted = []
+        index = index_ref[2 * a]
+        x = arrived_ref[index].astype(F32)
+        heads = []
         for k in range(2):
+            d = down_ref[a, k].astype(F32)
             acc = None
-            for r in range(ranks):
-                term = reduced[a][k * ranks + r] * up_ref[(a * 2 + k) * ranks + r]
+            for i in range(rows):
+                term = d[:, i * lanes : (i + 1) * lanes] * x[i : i + 1]
                 acc = term if acc is None else acc + term
-            lifted.append(acc)
-        lifted = (jnp.concatenate(lifted, axis=0) * ADAPTER_SCALE).astype(out_ref.dtype)
-        index, found = holder(slot_ref, 2 * o + a, n_sess)
-
-        @pl.when(found == 1)
+            reduced = jnp.sum(acc, axis=1, keepdims=True).astype(BF16).astype(F32)
+            lifted = jnp.sum(reduced * up_ref[a, k].astype(F32), axis=0, keepdims=True)
+            heads += [lifted[:, h * HD : (h + 1) * HD] for h in range(KVH)]
+        lifted = (jnp.concatenate(heads, axis=0) * ADAPTER_SCALE).astype(out_ref.dtype)
+
+        @pl.when(index_ref[2 * a + 1] == 1)
         def _():
             out_ref[index] = lifted
 
 
-def attention_kernel(length_ref, arrived_ref, key_ref, value_ref, out_ref):
+def attention_kernel(
+    length_ref, mark_ref, before_ref, spread_ref, after_ref, key_ref, value_ref, out_ref
+):
     span = key_ref.shape[1]
     t = lax.axis_index("tensor")
     length = length_ref[0]
@@ -113,8 +122,13 @@
     v = value_ref[0]
     scores = []
     for g in range(KVH):
-        q = (
-            arrived_ref[2 * g].astype(F32)[:8] + arrived_ref[2 * g + 1].astype(F32)[:8]
+        place = jnp.bitwise_and(g - lax.shift_right_logical(t, 1) + 4, 7)
+        row = lax.shift_right_logical(place * 11, 5)
+        part = place - 3 * row
+        q = jnp.where(
+            part == 0,
+            before_ref[row],
+            jnp.where(part == 1, spread_ref[row], after_ref[row]),
         ).astype(BF16)
         scores.append(
             lax.dot_general(
@@ -147,10 +161,9 @@
             out_ref[2 * g + half] = jnp.concatenate([acc[rows], zero, stat], axis=0)
 
 
-def pack_kernel(slot_ref, arrived_ref, base_ref, partial_ref, out_ref):
-    s = lax.axis_index("sess")
+def pack_kernel(index_ref, arrived_ref, base_ref, partial_ref, out_ref):
     t = lax.axis_index("tensor")
-    owner = lax.shift_right_logical(slot_ref[s], 1)
+    owner = index_ref[4]
     row = lax.broadcasted_iota(jnp.int32, (2 * KVH, HD), 0)
     p = arrived_ref[owner].astype(F32) + jnp.where(row == t, base_ref[...], 0.0)
     out_ref[...] = partial_ref[...]
@@ -208,32 +221,47 @@
     n_tensor = lax.axis_size("tensor")
     t = lax.axis_index("tensor")
     slots, two, ranks, width = adapter_down_maps.shape
-    part = width // n_tensor // HD
     shape = jax.ShapeDtypeStruct
 
-    parts = call(spread_kernel, shape((n_sess, part, HD), F32), [VMEM], [hidden], 10**5)
+    parts, own_queries, index = pl.pallas_call(
+        spread_kernel,
+        out_shape=(
+            pltpu.HBM((n_sess, 16, width // 16), BF16),
+            shape((8, HD), F32),
+            pltpu.SMEM((8,), jnp.int32),
+        ),
+        in_specs=[HBM, HBM, HBM],
+        out_specs=(HBM, VMEM, SMEM),
+        scratch_shapes=[
+            pltpu.SMEM((n_sess,), jnp.int32),
+            pltpu.VMEM(hidden.shape, BF16),
+            pltpu.VMEM(queries.shape, BF16),
+            pltpu.VMEM((n_sess, 16, width // 16), BF16),
+            pltpu.SemaphoreType.DMA((3,)),
+            pltpu.SemaphoreType.DMA((4,)),
+        ],
+        cost_estimate=pl.CostEstimate(flops=10**5, bytes_accessed=10**5, transcendentals=0),
+        compiler_params=pltpu.CompilerParams(vmem_limit_bytes=24 * 1024 * 1024),
+    )(*(pltpu.with_memory_space_constraint(x, pltpu.HBM) for x in (session_slot, hidden, queries)))
     parts = lax.all_to_all(parts, "sess", 0, 0, tiled=True)
 
-    block = call(
-        select_kernel,
-        shape((n_tensor, 16, HD), BF16),
-        [SMEM, VMEM, VMEM],
-        [session_slot, parts, queries],
-        10**5,
-    )
-    block = lax.all_to_all(block, "tensor", 0, 0, tiled=True)
-
-    down = (
-        adapter_down_maps.reshape(slots, two, ranks, n_tensor, part, HD)
-        .transpose(1, 2, 3, 0, 4, 5)
-        .reshape(two * ranks, n_tensor * slots * part, HD)
-    )
-    up = adapter_up_maps.reshape(slots * two * ranks, KVH, HD).astype(F32)
-    terms = call(
+    def come(x, distance):
+        return lax.ppermute(
+            x, "tensor", [(i, (i - 2 * distance) % n_tensor) for i in range(n_tensor)]
+        )
+
+    pair = own_queries + lax.ppermute(
+        own_queries, "tensor", [(i, i ^ 1) for i in range(n_tensor)]
+    )
+    pair = pair[None]
+    spread = jnp.concatenate([come(pair, -3), pair, come(pair, 3)])
+    before, after = come(spread, -1), come(spread, 1)
+
+    terms, mark = call(
         adapter_kernel,
-        shape((n_sess, 2 * KVH, HD), BF16),
+        (shape((n_sess, 2 * KVH, HD), BF16), pltpu.SMEM((8,), jnp.int32)),
         [SMEM, VMEM, VMEM, VMEM],
-        [session_slot, block, down, up],
+        [index, parts, adapter_down_maps, adapter_up_maps],
         10**6,
     )
     terms = lax.all_to_all(terms, "sess", 0, 0, tiled=True)
@@ -241,8 +269,8 @@
     partial = call(
         attention_kernel,
         shape((n_tensor, 8, HD), F32),
-        [SMEM, VMEM, VMEM, VMEM],
-        [lengths, block, cached_key_rows, cached_value_rows],
+        [SMEM, SMEM, VMEM, VMEM, VMEM, VMEM, VMEM],
+        [lengths, mark, before, spread, after, cached_key_rows, cached_value_rows],
         10**7,
     )
     base = jnp.dot(hidden, key_value_weight, preferred_element_type=F32)
@@ -250,7 +278,7 @@
         pack_kernel,
         shape((n_tensor, 8, HD), F32),
         [SMEM, VMEM, VMEM, VMEM],
-        [session_slot, terms, base, partial],
+        [index, terms, base, partial],
         10**5,
     )
     packed = lax.all_to_all(packed, "tensor", 0, 0, tiled=True)

time: 76.7 us -> 68.6 us (0.89)
  starting transfers between devices: 32.9 us -> 50.6 us
  waiting for transfers between devices: 24.4 us -> 8.46 us
  local copies, waits for them, and re-layouts: 6.67 us -> 1.07 us
  other arithmetic: 3.86 us -> 0.51 us
  Pallas kernels: 5.75 us -> 4.69 us
    ppermute x0 -> x5, starting transfers between devices: none -> 23.7 us  [the longest x4 20.9 us: come(): lax.ppermute(x, 'tensor', [(i, (i - 2 * distance) % n_tensor) for i in ra...]
    all_to_all x1 -> x0, starting transfers between devices: 12.6 us -> none  [local(): block = lax.all_to_all(block, 'tensor', 0, 0, tiled=True)]
    all_to_all x1, waiting for transfers between devices: 8.27 us -> 0.01 us  [local(): terms = lax.all_to_all(terms, 'sess', 0, 0, tiled=True)]
    all_to_all x1, waiting for transfers between devices: 5.77 us -> 0.01 us  [local(): parts = lax.all_to_all(parts, 'sess', 0, 0, tiled=True)]
    all_to_all x1, starting transfers between devices: 3.99 us -> 9.49 us  [local(): terms = lax.all_to_all(terms, 'sess', 0, 0, tiled=True)]
    reshape x2 -> x0, local copies, waits for them, and re-layouts: 2.97 us -> none  [local(): adapter_down_maps.reshape(slots, two, ranks, n_tensor, part, HD)]
    pallas_call x6 -> x4, Pallas kernels: 5.75 us -> 2.91 us  [call(): pl.pallas_call(body, out_shape=out_shape, in_specs=specs, out_specs=jax.t...]
    all_to_all x1 -> x0, waiting for transfers between devices: 2.66 us -> none  [local(): block = lax.all_to_all(block, 'tensor', 0, 0, tiled=True)]
  transfers between devices with their start and end apart: 4 -> 8, of which waited for: 4 -> 2; matrix products, arithmetic and copies ran while one was open for 11% -> 2% of each run, Pallas kernels for 1% -> 2%
where the time goes in v3:
time: 68.6 us; the launch traced here: 68 us
  starting transfers between devices  50.6 us (74%)
  waiting for transfers between devices  8.46 us (12%)
  Pallas kernels  4.69 us (7%)
  between operations  1.49 us (2%)
  matrix products  1.14 us (2%)
  local copies, waits for them, and re-layouts  1.07 us (2%)
    ppermute x4, starting transfers between devices, come(): lax.ppermute(x, 'tensor', [(i, (i - 2 * distance) % n_tensor) for i in ra...  20.9 us
    all_to_all x1, starting transfers between devices, local(): parts = lax.all_to_all(parts, 'sess', 0, 0, tiled=True)  10.6 us
    all_to_all x1, starting transfers between devices, local(): terms = lax.all_to_all(terms, 'sess', 0, 0, tiled=True)  9.49 us
    all_to_all x1, waiting for transfers between devices, local(): packed = lax.all_to_all(packed, 'tensor', 0, 0, tiled=True)  7.72 us
    all_to_all x1, starting transfers between devices, local(): packed = lax.all_to_all(packed, 'tensor', 0, 0, tiled=True)  6.75 us
    pallas_call x4, Pallas kernels, call(): pl.pallas_call(body, out_shape=out_shape, in_specs=specs, out_specs=jax.t...  2.91 us
    ppermute x1, starting transfers between devices, local(): lax.ppermute(own_queries, 'tensor', [(i, i ^ 1) for i in range(n_tensor)])  2.86 us
    pallas_call x1, Pallas kernels, local(): pl.pallas_call(spread_kernel, out_shape=(pltpu.HBM((n_sess, 16, width //...  1.79 us
  transfers between devices with their start and end apart: 8, of which 2 were waited for; matrix products, arithmetic and copies ran while one was open for 2% of the time, Pallas kernels for 2%

profile of v3, /device:TPU:1, one launch (start us, length us, event | category | flops | bytes accessed | tf_op | source)
XLA Modules:
  0.0 68.0 jit_solution(15092746758186203588)
XLA Ops:
  0.6 0.0 copy-start
  0.7 1.8 %shard_map.104 = (bf16[32,16,512]{2,1,0:T(8,128)(2,1)}, f32[8,128]{1,0:T(8,128)S(1)}, s32[8]{0:T(128)S(4)}) custom-call(s32[32]{0:T(128)} %slot_hbm.1, bf16[1,8192]{1,0:T(2,128)(2,1)} %hidden_hbm.1, bf16[1,512]{1,0:T(2,128)(2,1)} %query_ref.1), custom_call_target="tpu_custom_call" | custom-call | flops 100000 | bytes 100000 | tf_op jit(solution)/shard_map/pallas_call | solution.py:226
  2.5 0.0 copy-start.1
  2.5 10.6 %all-to-all-start = ((bf16[32,16,512]{2,1,0:T(8,128)(2,1)}), bf16[32,16,512]{2,1,0:T(8,128)(2,1)S(1)}, u32[]{:S(2)}, u32[]{:S(2)}) async-start(bf16[32,16,512]{2,1,0:T(8,128)(2,1)} %get-tuple-element.8), calls=%async_computation | async-start | bytes 1048576 | tf_op jit(solution)/shard_map/all_to_all | solution.py:246
  13.1 2.9 %collective-permute-start = (f32[8,128]{1,0:T(8,128)S(1)}, f32[8,128]{1,0:T(8,128)S(1)}, u32[]{:S(2)}, u32[]{:S(2)}) collective-permute-start(f32[8,128]{1,0:T(8,128)S(1)} %get-tuple-element.11), channel_id=1, source_target_pairs={{0,1},{1,0},{2,3},{3,2},{4,5},{5,4},{6,7},{7,6},{8,9},{9,8},{10,11... | collective-permute-start | bytes 12296 | tf_op jit(solution)/shard_map/ppermute | solution.py:253
  16.6 0.1 fusion.5
  16.7 0.1 negate_bitcast_fusion
  16.8 0.1 fusion.4
  16.8 0.1 fusion.2
  16.9 0.0 copy-start.5
  16.9 1.1 %fusion.base_ref = f32[1,128]{1,0:T(1,128)S(1)} fusion(bf16[8192,128]{1,0:T(8,128)(2,1)S(1)} %copy-done, bf16[1,8192]{1,0:T(2,128)(2,1)} %hidden_hbm.1), kind=kOutput, calls=%fused_computation | convolution fusion | flops 2097152 | bytes 2114048 | tf_op jit(solution)/shard_map/dot_general | solution.py:276
  18.0 0.1 broadcast_select_fusion
  18.1 0.0 collective-permute-done
  18.1 10.6 %collective-permute-start.2 = (f32[1,8,128]{2,1,0:T(8,128)S(1)}, f32[1,8,128]{2,1,0:T(8,128)S(1)}, u32[]{:S(2)}, u32[]{:S(2)}) collective-permute-start(f32[1,8,128]{2,1,0:T(8,128)S(1)} %add_bitcast_fusion), channel_id=1, source_target_pairs={{0,10},{1,11},{2,12},{3,13},{4,14},{5,15},{6,0},{7,1},{8,2},{9,3},... | collective-permute-start | bytes 12296 | tf_op jit(solution)/shard_map/ppermute | solution.py:249
  28.8 1.9 %collective-permute-start.1 = (f32[1,8,128]{2,1,0:T(8,128)S(1)}, f32[1,8,128]{2,1,0:T(8,128)S(1)}, u32[]{:S(2)}, u32[]{:S(2)}) collective-permute-start(f32[1,8,128]{2,1,0:T(8,128)S(1)} %add_bitcast_fusion), channel_id=1, source_target_pairs={{0,6},{1,7},{2,8},{3,9},{4,10},{5,11},{6,12},{7,13},{8,14},{9,15},... | collective-permute-start | bytes 12296 | tf_op jit(solution)/shard_map/ppermute | solution.py:249
  30.7 0.0 all-to-all-done.arrived_ref
  30.8 0.9 %shard_map.105 = (bf16[32,16,128]{2,1,0:T(8,128)(2,1)}, s32[8]{0:T(128)S(4)}) custom-call(s32[8]{0:T(128)S(4)} %get-tuple-element.7.index_ref, bf16[32,16,512]{2,1,0:T(8,128)(2,1)S(1)} %all-to-all-done.arrived_ref, bf16[2,2,4,8192]{3,2,1,0:T(4,128)(2,1)S(1)} %copy-done.3, bf16[2,2,4,1024]{3,2,1,0:T(4,128)(2,1)S(1)} %copy-done.4), custom_call_target="tpu_custom_call" | custom-call | flops 1000000 | bytes 1000000 | tf_op jit(solution)/shard_map/pallas_call | solution.py:26
  31.7 9.5 %all-to-all-start.1 = ((bf16[32,16,128]{2,1,0:T(8,128)(2,1)}), bf16[32,16,128]{2,1,0:T(8,128)(2,1)S(1)}, u32[]{:S(2)}, u32[]{:S(2)}) async-start(bf16[32,16,128]{2,1,0:T(8,128)(2,1)} %get-tuple-element.9), calls=%async_computation.1 | async-start | bytes 262144 | tf_op jit(solution)/shard_map/all_to_all | solution.py:267
  41.2 0.1 fusion.6
  41.3 0.0 collective-permute-done.1
  41.3 3.1 %collective-permute-start.3 = (f32[3,8,128]{2,1,0:T(8,128)S(1)}, f32[3,8,128]{2,1,0:T(8,128)S(1)}, u32[]{:S(2)}, u32[]{:S(2)}) collective-permute-start(f32[3,8,128]{2,1,0:T(8,128)S(1)} %pad_maximum_fusion.spread_ref), channel_id=1, source_target_pairs={{0,2},{1,3},{2,4},{3,5},{4,6},{5,7},{6,8},{7,9},{8,10},{9,11},{10,... | collective-permute-start | bytes 36872 | tf_op jit(solution)/shard_map/ppermute | solution.py:249
  44.4 5.2 %collective-permute-start.4 = (f32[3,8,128]{2,1,0:T(8,128)S(1)}, f32[3,8,128]{2,1,0:T(8,128)S(1)}, u32[]{:S(2)}, u32[]{:S(2)}) collective-permute-start(f32[3,8,128]{2,1,0:T(8,128)S(1)} %pad_maximum_fusion.spread_ref), channel_id=1, source_target_pairs={{0,14},{1,15},{2,0},{3,1},{4,2},{5,3},{6,4},{7,5},{8,6},{9,7},{10,... | collective-permute-start | bytes 36872 | tf_op jit(solution)/shard_map/ppermute | solution.py:249
  49.6 0.1 maximum_bitcast_fusion
  49.7 0.0 collective-permute-done.3.before_ref
  49.7 0.7 %collective-permute-done.4.after_ref = f32[3,8,128]{2,1,0:T(8,128)S(1)} collective-permute-done((f32[3,8,128]{2,1,0:T(8,128)S(1)}, f32[3,8,128]{2,1,0:T(8,128)S(1)}, u32[]{:S(2)}, u32[]{:S(2)}) %collective-permute-start.4) | collective-permute-done | bytes 12320 | tf_op jit(solution)/shard_map/ppermute | solution.py:249
  50.4 1.0 %copy-done.2 = bf16[1,256,1024]{2,1,0:T(8,128)(2,1)S(1)} copy-done((bf16[1,256,1024]{2,1,0:T(8,128)(2,1)S(1)}, bf16[1,256,1024]{2,1,0:T(8,128)(2,1)}, u32[]{:S(2)}) %copy-start.2) | copy-done | bytes 524312
  51.5 0.5 shard_map.106.partial_ref
  51.9 0.6 shard_map.107
  52.6 6.8 %all-to-all-start.2 = ((f32[16,8,128]{2,1,0:T(8,128)}), f32[16,8,128]{2,1,0:T(8,128)S(1)}, u32[]{:S(2)}, u32[]{:S(2)}) async-start(f32[16,8,128]{2,1,0:T(8,128)} %shard_map.107), calls=%async_computation.2 | async-start | bytes 131072 | tf_op jit(solution)/shard_map/all_to_all | solution.py:284
  59.3 0.1 maximum_bitcast_fusion.1
  59.4 7.7 %all-to-all-done.2.arrived_ref = f32[16,8,128]{2,1,0:T(8,128)S(1)} async-done(((f32[16,8,128]{2,1,0:T(8,128)}), f32[16,8,128]{2,1,0:T(8,128)S(1)}, u32[]{:S(2)}, u32[]{:S(2)}) %all-to-all-start.2) | async-done | bytes 65568 | tf_op jit(solution)/shard_map/all_to_all | solution.py:284
  67.1 0.9 %shard_map.108 = (bf16[1,128]{1,0:T(2,128)(2,1)}, bf16[1,512]{1,0:T(2,128)(2,1)}) custom-call(f32[4,128]{1,0:T(4,128)S(1)} %pad_maximum_fusion.1.rot_ref, bf16[1,512]{1,0:T(2,128)(2,1)S(1)} %copy-done.5, f32[16,8,128]{2,1,0:T(8,128)S(1)} %all-to-all-done.2.arrived_ref), custom_call_target="tpu_custom_call" | custom-call | flops 100000 | bytes 100000 | tf_op jit(solution)/shard_map/pallas_call | solution.py:26
  (13 shorter events, 0.0 us)
Async XLA Ops:
  0.6 16.3 %copy-start = (bf16[8192,128]{1,0:T(8,128)(2,1)S(1)}, bf16[8192,128]{1,0:T(8,128)(2,1)}, u32[]{:S(2)}) copy-start(bf16[8192,128]{1,0:T(8,128)(2,1)} %param.10) | copy-start | bytes 6291460
  0.6 30.1 %copy-start.3 = (bf16[2,2,4,8192]{3,2,1,0:T(4,128)(2,1)S(1)}, bf16[2,2,4,8192]{3,2,1,0:T(4,128)(2,1)}, u32[]{:S(2)}) copy-start(bf16[2,2,4,8192]{3,2,1,0:T(4,128)(2,1)} %down_ref.1) | copy-start | bytes 786436
  0.7 30.1 %copy-start.4 = (bf16[2,2,4,1024]{3,2,1,0:T(4,128)(2,1)S(1)}, bf16[2,2,4,1024]{3,2,1,0:T(4,128)(2,1)}, u32[]{:S(2)}) copy-start(bf16[2,2,4,1024]{3,2,1,0:T(4,128)(2,1)} %up_ref.1) | copy-start | bytes 98308
  2.5 48.0 %copy-start.1 = (bf16[1,256,1024]{2,1,0:T(8,128)(2,1)S(1)}, bf16[1,256,1024]{2,1,0:T(8,128)(2,1)}, u32[]{:S(2)}) copy-start(bf16[1,256,1024]{2,1,0:T(8,128)(2,1)} %key_ref.1) | copy-start | bytes 1572868
  2.5 28.3 %all-to-all-start = ((bf16[32,16,512]{2,1,0:T(8,128)(2,1)}), bf16[32,16,512]{2,1,0:T(8,128)(2,1)S(1)}, u32[]{:S(2)}, u32[]{:S(2)}) async-start(bf16[32,16,512]{2,1,0:T(8,128)(2,1)} %get-tuple-element.8), calls=%async_computation | async-start | bytes 1048576 | tf_op jit(solution)/shard_map/all_to_all | solution.py:246
  13.1 5.0 %collective-permute-start = (f32[8,128]{1,0:T(8,128)S(1)}, f32[8,128]{1,0:T(8,128)S(1)}, u32[]{:S(2)}, u32[]{:S(2)}) collective-permute-start(f32[8,128]{1,0:T(8,128)S(1)} %get-tuple-element.11), channel_id=1, source_target_pairs={{0,1},{1,0},{2,3},{3,2},{4,5},{5,4},{6,7},{7,6},{8,9},{9,8},{10,11... | collective-permute-start | bytes 12296 | tf_op jit(solution)/shard_map/ppermute | solution.py:253
  16.9 50.2 %copy-start.5 = (bf16[1,512]{1,0:T(2,128)(2,1)S(1)}, bf16[1,512]{1,0:T(2,128)(2,1)}, u32[]{:S(2)}) copy-start(bf16[1,512]{1,0:T(2,128)(2,1)} %query_ref.1) | copy-start | bytes 3076
  18.1 23.1 %collective-permute-start.2 = (f32[1,8,128]{2,1,0:T(8,128)S(1)}, f32[1,8,128]{2,1,0:T(8,128)S(1)}, u32[]{:S(2)}, u32[]{:S(2)}) collective-permute-start(f32[1,8,128]{2,1,0:T(8,128)S(1)} %add_bitcast_fusion), channel_id=1, source_target_pairs={{0,10},{1,11},{2,12},{3,13},{4,14},{5,15},{6,0},{7,1},{8,2},{9,3},... | collective-permute-start | bytes 12296 | tf_op jit(solution)/shard_map/ppermute | solution.py:249
  28.8 12.5 %collective-permute-start.1 = (f32[1,8,128]{2,1,0:T(8,128)S(1)}, f32[1,8,128]{2,1,0:T(8,128)S(1)}, u32[]{:S(2)}, u32[]{:S(2)}) collective-permute-start(f32[1,8,128]{2,1,0:T(8,128)S(1)} %add_bitcast_fusion), channel_id=1, source_target_pairs={{0,6},{1,7},{2,8},{3,9},{4,10},{5,11},{6,12},{7,13},{8,14},{9,15},... | collective-permute-start | bytes 12296 | tf_op jit(solution)/shard_map/ppermute | solution.py:249
  31.7 20.2 %all-to-all-start.1 = ((bf16[32,16,128]{2,1,0:T(8,128)(2,1)}), bf16[32,16,128]{2,1,0:T(8,128)(2,1)S(1)}, u32[]{:S(2)}, u32[]{:S(2)}) async-start(bf16[32,16,128]{2,1,0:T(8,128)(2,1)} %get-tuple-element.9), calls=%async_computation.1 | async-start | bytes 262144 | tf_op jit(solution)/shard_map/all_to_all | solution.py:267
  41.3 8.4 %collective-permute-start.3 = (f32[3,8,128]{2,1,0:T(8,128)S(1)}, f32[3,8,128]{2,1,0:T(8,128)S(1)}, u32[]{:S(2)}, u32[]{:S(2)}) collective-permute-start(f32[3,8,128]{2,1,0:T(8,128)S(1)} %pad_maximum_fusion.spread_ref), channel_id=1, source_target_pairs={{0,2},{1,3},{2,4},{3,5},{4,6},{5,7},{6,8},{7,9},{8,10},{9,11},{10,... | collective-permute-start | bytes 36872 | tf_op jit(solution)/shard_map/ppermute | solution.py:249
  44.4 6.0 %collective-permute-start.4 = (f32[3,8,128]{2,1,0:T(8,128)S(1)}, f32[3,8,128]{2,1,0:T(8,128)S(1)}, u32[]{:S(2)}, u32[]{:S(2)}) collective-permute-start(f32[3,8,128]{2,1,0:T(8,128)S(1)} %pad_maximum_fusion.spread_ref), channel_id=1, source_target_pairs={{0,14},{1,15},{2,0},{3,1},{4,2},{5,3},{6,4},{7,5},{8,6},{9,7},{10,... | collective-permute-start | bytes 36872 | tf_op jit(solution)/shard_map/ppermute | solution.py:249
  50.4 1.0 %copy-start.2 = (bf16[1,256,1024]{2,1,0:T(8,128)(2,1)S(1)}, bf16[1,256,1024]{2,1,0:T(8,128)(2,1)}, u32[]{:S(2)}) copy-start(bf16[1,256,1024]{2,1,0:T(8,128)(2,1)} %value_ref.1) | copy-start | bytes 1572868
  52.6 14.6 %all-to-all-start.2 = ((f32[16,8,128]{2,1,0:T(8,128)}), f32[16,8,128]{2,1,0:T(8,128)S(1)}, u32[]{:S(2)}, u32[]{:S(2)}) async-start(f32[16,8,128]{2,1,0:T(8,128)} %shard_map.107), calls=%async_computation.2 | async-start | bytes 131072 | tf_op jit(solution)/shard_map/all_to_all | solution.py:284

commit v4 on v3

--- a/solution.py
+++ b/solution.py
@@ -259,7 +259,7 @@
 
     terms, mark = call(
         adapter_kernel,
-        (shape((n_sess, 2 * KVH, HD), BF16), pltpu.SMEM((8,), jnp.int32)),
+        (shape((n_sess, 2 * KVH, HD), F32), pltpu.SMEM((8,), jnp.int32)),
         [SMEM, VMEM, VMEM, VMEM],
         [index, parts, adapter_down_maps, adapter_up_maps],
         10**6,

time: 68.6 us -> 81.6 us (1.19)
  waiting for transfers between devices: 8.46 us -> 25.4 us
  starting transfers between devices: 50.6 us -> 46.7 us
    all_to_all x1, waiting for transfers between devices: 0.01 us -> 11.3 us  [local(): parts = lax.all_to_all(parts, 'sess', 0, 0, tiled=True)]
    ppermute x4, waiting for transfers between devices: 0.74 us -> 6.37 us  [come(): lax.ppermute(x, 'tensor', [(i, (i - 2 * distance) % n_tensor) for i in ra...]
    all_to_all x1, starting transfers between devices: 9.49 us -> 5.21 us  [local(): terms = lax.all_to_all(terms, 'sess', 0, 0, tiled=True)]
    all_to_all x1, starting transfers between devices: 6.75 us -> 8.95 us  [local(): packed = lax.all_to_all(packed, 'tensor', 0, 0, tiled=True)]
    ppermute x4, starting transfers between devices: 20.9 us -> 19 us  [come(): lax.ppermute(x, 'tensor', [(i, (i - 2 * distance) % n_tensor) for i in ra...]
  transfers between devices with their start and end apart: 8 -> 8, of which waited for: 2 -> 4; matrix products, arithmetic and copies ran while one was open for 2% -> 2% of each run, Pallas kernels for 2% -> 2%
where the time goes in v4:
time: 81.6 us; the launch traced here: 81 us
  starting transfers between devices  46.7 us (57%)
  waiting for transfers between devices  25.4 us (31%)
  Pallas kernels  4.74 us (6%)
  between operations  1.46 us (2%)
  matrix products  1.14 us (1%)
  local copies, waits for them, and re-layouts  1.07 us (1%)
    ppermute x4, starting transfers between devices, come(): lax.ppermute(x, 'tensor', [(i, (i - 2 * distance) % n_tensor) for i in ra...  19 us
    all_to_all x1, waiting for transfers between devices, local(): parts = lax.all_to_all(parts, 'sess', 0, 0, tiled=True)  11.3 us
    all_to_all x1, starting transfers between devices, local(): parts = lax.all_to_all(parts, 'sess', 0, 0, tiled=True)  10.6 us
    all_to_all x1, starting transfers between devices, local(): packed = lax.all_to_all(packed, 'tensor', 0, 0, tiled=True)  8.95 us
    all_to_all x1, waiting for transfers between devices, local(): packed = lax.all_to_all(packed, 'tensor', 0, 0, tiled=True)  7.72 us
    ppermute x4, waiting for transfers between devices, come(): lax.ppermute(x, 'tensor', [(i, (i - 2 * distance) % n_tensor) for i in ra...  6.37 us
    all_to_all x1, starting transfers between devices, local(): terms = lax.all_to_all(terms, 'sess', 0, 0, tiled=True)  5.21 us
    pallas_call x4, Pallas kernels, call(): pl.pallas_call(body, out_shape=out_shape, in_specs=specs, out_specs=jax.t...  2.95 us
  transfers between devices with their start and end apart: 8, of which 4 were waited for; matrix products, arithmetic and copies ran while one was open for 2% of the time, Pallas kernels for 2%

profile of v4, /device:TPU:1, one launch (start us, length us, event | category | flops | bytes accessed | tf_op | source)
XLA Modules:
  0.0 81.0 jit_solution(11096858568136300089)
XLA Ops:
  0.6 0.0 copy-start
  0.7 1.8 %shard_map.104 = (bf16[32,16,512]{2,1,0:T(8,128)(2,1)}, f32[8,128]{1,0:T(8,128)S(1)}, s32[8]{0:T(128)S(4)}) custom-call(s32[32]{0:T(128)} %slot_hbm.1, bf16[1,8192]{1,0:T(2,128)(2,1)} %hidden_hbm.1, bf16[1,512]{1,0:T(2,128)(2,1)} %query_ref.1), custom_call_target="tpu_custom_call" | custom-call | flops 100000 | bytes 100000 | tf_op jit(solution)/shard_map/pallas_call | solution.py:226
  2.5 0.0 copy-start.1
  2.5 10.6 %all-to-all-start = ((bf16[32,16,512]{2,1,0:T(8,128)(2,1)}), bf16[32,16,512]{2,1,0:T(8,128)(2,1)S(1)}, u32[]{:S(2)}, u32[]{:S(2)}) async-start(bf16[32,16,512]{2,1,0:T(8,128)(2,1)} %get-tuple-element.8), calls=%async_computation | async-start | bytes 1048576 | tf_op jit(solution)/shard_map/all_to_all | solution.py:246
  13.1 2.9 %collective-permute-start = (f32[8,128]{1,0:T(8,128)S(1)}, f32[8,128]{1,0:T(8,128)S(1)}, u32[]{:S(2)}, u32[]{:S(2)}) collective-permute-start(f32[8,128]{1,0:T(8,128)S(1)} %get-tuple-element.11), channel_id=1, source_target_pairs={{0,1},{1,0},{2,3},{3,2},{4,5},{5,4},{6,7},{7,6},{8,9},{9,8},{10,11... | collective-permute-start | bytes 12296 | tf_op jit(solution)/shard_map/ppermute | solution.py:253
  16.6 0.1 fusion.5
  16.7 0.1 negate_bitcast_fusion
  16.8 0.1 fusion.4
  16.8 0.1 fusion.2
  16.9 0.0 copy-start.5
  16.9 1.1 %fusion.base_ref = f32[1,128]{1,0:T(1,128)S(1)} fusion(bf16[8192,128]{1,0:T(8,128)(2,1)S(1)} %copy-done, bf16[1,8192]{1,0:T(2,128)(2,1)} %hidden_hbm.1), kind=kOutput, calls=%fused_computation | convolution fusion | flops 2097152 | bytes 2114048 | tf_op jit(solution)/shard_map/dot_general | solution.py:276
  18.0 0.1 broadcast_select_fusion
  18.1 11.3 %all-to-all-done.arrived_ref = bf16[32,16,512]{2,1,0:T(8,128)(2,1)S(1)} async-done(((bf16[32,16,512]{2,1,0:T(8,128)(2,1)}), bf16[32,16,512]{2,1,0:T(8,128)(2,1)S(1)}, u32[]{:S(2)}, u32[]{:S(2)}) %all-to-all-start) | async-done | bytes 524320 | tf_op jit(solution)/shard_map/all_to_all | solution.py:246
  29.4 1.0 %shard_map.105 = (f32[32,16,128]{2,1,0:T(8,128)}, s32[8]{0:T(128)S(4)}) custom-call(s32[8]{0:T(128)S(4)} %get-tuple-element.7.index_ref, bf16[32,16,512]{2,1,0:T(8,128)(2,1)S(1)} %all-to-all-done.arrived_ref, bf16[2,2,4,8192]{3,2,1,0:T(4,128)(2,1)S(1)} %copy-done.3, bf16[2,2,4,1024]{3,2,1,0:T(4,128)(2,1)S(1)} %copy-done.4), custom_call_target="tpu_custom_call" | custom-call | flops 1000000 | bytes 1000000 | tf_op jit(solution)/shard_map/pallas_call | solution.py:26
  30.4 5.2 %all-to-all-start.1 = ((f32[32,16,128]{2,1,0:T(8,128)}), f32[32,16,128]{2,1,0:T(8,128)S(1)}, u32[]{:S(2)}, u32[]{:S(2)}) async-start(f32[32,16,128]{2,1,0:T(8,128)} %get-tuple-element.9), calls=%async_computation.1 | async-start | bytes 524288 | tf_op jit(solution)/shard_map/all_to_all | solution.py:267
  35.6 0.0 collective-permute-done
  35.6 10.6 %collective-permute-start.2 = (f32[1,8,128]{2,1,0:T(8,128)S(1)}, f32[1,8,128]{2,1,0:T(8,128)S(1)}, u32[]{:S(2)}, u32[]{:S(2)}) collective-permute-start(f32[1,8,128]{2,1,0:T(8,128)S(1)} %add_bitcast_fusion), channel_id=1, source_target_pairs={{0,10},{1,11},{2,12},{3,13},{4,14},{5,15},{6,0},{7,1},{8,2},{9,3},... | collective-permute-start | bytes 12296 | tf_op jit(solution)/shard_map/ppermute | solution.py:249
  46.3 1.9 %collective-permute-start.1 = (f32[1,8,128]{2,1,0:T(8,128)S(1)}, f32[1,8,128]{2,1,0:T(8,128)S(1)}, u32[]{:S(2)}, u32[]{:S(2)}) collective-permute-start(f32[1,8,128]{2,1,0:T(8,128)S(1)} %add_bitcast_fusion), channel_id=1, source_target_pairs={{0,6},{1,7},{2,8},{3,9},{4,10},{5,11},{6,12},{7,13},{8,14},{9,15},... | collective-permute-start | bytes 12296 | tf_op jit(solution)/shard_map/ppermute | solution.py:249
  48.2 0.1 fusion.6
  48.3 0.0 collective-permute-done.2
  48.3 5.4 %collective-permute-done.1 = f32[1,8,128]{2,1,0:T(8,128)S(1)} collective-permute-done((f32[1,8,128]{2,1,0:T(8,128)S(1)}, f32[1,8,128]{2,1,0:T(8,128)S(1)}, u32[]{:S(2)}, u32[]{:S(2)}) %collective-permute-start.1) | collective-permute-done | bytes 4128 | tf_op jit(solution)/shard_map/ppermute | solution.py:249
  53.6 3.1 %collective-permute-start.3 = (f32[3,8,128]{2,1,0:T(8,128)S(1)}, f32[3,8,128]{2,1,0:T(8,128)S(1)}, u32[]{:S(2)}, u32[]{:S(2)}) collective-permute-start(f32[3,8,128]{2,1,0:T(8,128)S(1)} %pad_maximum_fusion.spread_ref), channel_id=1, source_target_pairs={{0,2},{1,3},{2,4},{3,5},{4,6},{5,7},{6,8},{7,9},{8,10},{9,11},{10,... | collective-permute-start | bytes 36872 | tf_op jit(solution)/shard_map/ppermute | solution.py:249
  56.8 3.4 %collective-permute-start.4 = (f32[3,8,128]{2,1,0:T(8,128)S(1)}, f32[3,8,128]{2,1,0:T(8,128)S(1)}, u32[]{:S(2)}, u32[]{:S(2)}) collective-permute-start(f32[3,8,128]{2,1,0:T(8,128)S(1)} %pad_maximum_fusion.spread_ref), channel_id=1, source_target_pairs={{0,14},{1,15},{2,0},{3,1},{4,2},{5,3},{6,4},{7,5},{8,6},{9,7},{10,... | collective-permute-start | bytes 36872 | tf_op jit(solution)/shard_map/ppermute | solution.py:249
  60.1 0.1 maximum_bitcast_fusion
  60.2 1.0 %collective-permute-done.4.after_ref = f32[3,8,128]{2,1,0:T(8,128)S(1)} collective-permute-done((f32[3,8,128]{2,1,0:T(8,128)S(1)}, f32[3,8,128]{2,1,0:T(8,128)S(1)}, u32[]{:S(2)}, u32[]{:S(2)}) %collective-permute-start.4) | collective-permute-done | bytes 12320 | tf_op jit(solution)/shard_map/ppermute | solution.py:249
  61.2 1.0 %copy-done.2 = bf16[1,256,1024]{2,1,0:T(8,128)(2,1)S(1)} copy-done((bf16[1,256,1024]{2,1,0:T(8,128)(2,1)S(1)}, bf16[1,256,1024]{2,1,0:T(8,128)(2,1)}, u32[]{:S(2)}) %copy-start.2) | copy-done | bytes 524312
  62.3 0.5 shard_map.106.partial_ref
  62.7 0.6 shard_map.107
  63.4 8.9 %all-to-all-start.2 = ((f32[16,8,128]{2,1,0:T(8,128)}), f32[16,8,128]{2,1,0:T(8,128)S(1)}, u32[]{:S(2)}, u32[]{:S(2)}) async-start(f32[16,8,128]{2,1,0:T(8,128)} %shard_map.107), calls=%async_computation.2 | async-start | bytes 131072 | tf_op jit(solution)/shard_map/all_to_all | solution.py:284
  72.3 0.1 maximum_bitcast_fusion.1
  72.4 7.7 %all-to-all-done.2.arrived_ref = f32[16,8,128]{2,1,0:T(8,128)S(1)} async-done(((f32[16,8,128]{2,1,0:T(8,128)}), f32[16,8,128]{2,1,0:T(8,128)S(1)}, u32[]{:S(2)}, u32[]{:S(2)}) %all-to-all-start.2) | async-done | bytes 65568 | tf_op jit(solution)/shard_map/all_to_all | solution.py:284
  80.1 0.9 %shard_map.108 = (bf16[1,128]{1,0:T(2,128)(2,1)}, bf16[1,512]{1,0:T(2,128)(2,1)}) custom-call(f32[4,128]{1,0:T(4,128)S(1)} %pad_maximum_fusion.1.rot_ref, bf16[1,512]{1,0:T(2,128)(2,1)S(1)} %copy-done.5, f32[16,8,128]{2,1,0:T(8,128)S(1)} %all-to-all-done.2.arrived_ref), custom_call_target="tpu_custom_call" | custom-call | flops 100000 | bytes 100000 | tf_op jit(solution)/shard_map/pallas_call | solution.py:26
  (13 shorter events, 0.0 us)
Async XLA Ops:
  0.6 16.3 %copy-start = (bf16[8192,128]{1,0:T(8,128)(2,1)S(1)}, bf16[8192,128]{1,0:T(8,128)(2,1)}, u32[]{:S(2)}) copy-start(bf16[8192,128]{1,0:T(8,128)(2,1)} %param.10) | copy-start | bytes 6291460
  0.6 28.8 %copy-start.3 = (bf16[2,2,4,8192]{3,2,1,0:T(4,128)(2,1)S(1)}, bf16[2,2,4,8192]{3,2,1,0:T(4,128)(2,1)}, u32[]{:S(2)}) copy-start(bf16[2,2,4,8192]{3,2,1,0:T(4,128)(2,1)} %down_ref.1) | copy-start | bytes 786436
  0.7 28.7 %copy-start.4 = (bf16[2,2,4,1024]{3,2,1,0:T(4,128)(2,1)S(1)}, bf16[2,2,4,1024]{3,2,1,0:T(4,128)(2,1)}, u32[]{:S(2)}) copy-start(bf16[2,2,4,1024]{3,2,1,0:T(4,128)(2,1)} %up_ref.1) | copy-start | bytes 98308
  2.5 58.8 %copy-start.1 = (bf16[1,256,1024]{2,1,0:T(8,128)(2,1)S(1)}, bf16[1,256,1024]{2,1,0:T(8,128)(2,1)}, u32[]{:S(2)}) copy-start(bf16[1,256,1024]{2,1,0:T(8,128)(2,1)} %key_ref.1) | copy-start | bytes 1572868
  2.5 26.9 %all-to-all-start = ((bf16[32,16,512]{2,1,0:T(8,128)(2,1)}), bf16[32,16,512]{2,1,0:T(8,128)(2,1)S(1)}, u32[]{:S(2)}, u32[]{:S(2)}) async-start(bf16[32,16,512]{2,1,0:T(8,128)(2,1)} %get-tuple-element.8), calls=%async_computation | async-start | bytes 1048576 | tf_op jit(solution)/shard_map/all_to_all | solution.py:246
  13.1 22.5 %collective-permute-start = (f32[8,128]{1,0:T(8,128)S(1)}, f32[8,128]{1,0:T(8,128)S(1)}, u32[]{:S(2)}, u32[]{:S(2)}) collective-permute-start(f32[8,128]{1,0:T(8,128)S(1)} %get-tuple-element.11), channel_id=1, source_target_pairs={{0,1},{1,0},{2,3},{3,2},{4,5},{5,4},{6,7},{7,6},{8,9},{9,8},{10,11... | collective-permute-start | bytes 12296 | tf_op jit(solution)/shard_map/ppermute | solution.py:253
  16.9 63.2 %copy-start.5 = (bf16[1,512]{1,0:T(2,128)(2,1)S(1)}, bf16[1,512]{1,0:T(2,128)(2,1)}, u32[]{:S(2)}) copy-start(bf16[1,512]{1,0:T(2,128)(2,1)} %query_ref.1) | copy-start | bytes 3076
  30.4 32.3 %all-to-all-start.1 = ((f32[32,16,128]{2,1,0:T(8,128)}), f32[32,16,128]{2,1,0:T(8,128)S(1)}, u32[]{:S(2)}, u32[]{:S(2)}) async-start(f32[32,16,128]{2,1,0:T(8,128)} %get-tuple-element.9), calls=%async_computation.1 | async-start | bytes 524288 | tf_op jit(solution)/shard_map/all_to_all | solution.py:267
  35.6 12.6 %collective-permute-start.2 = (f32[1,8,128]{2,1,0:T(8,128)S(1)}, f32[1,8,128]{2,1,0:T(8,128)S(1)}, u32[]{:S(2)}, u32[]{:S(2)}) collective-permute-start(f32[1,8,128]{2,1,0:T(8,128)S(1)} %add_bitcast_fusion), channel_id=1, source_target_pairs={{0,10},{1,11},{2,12},{3,13},{4,14},{5,15},{6,0},{7,1},{8,2},{9,3},... | collective-permute-start | bytes 12296 | tf_op jit(solution)/shard_map/ppermute | solution.py:249
  46.3 7.4 %collective-permute-start.1 = (f32[1,8,128]{2,1,0:T(8,128)S(1)}, f32[1,8,128]{2,1,0:T(8,128)S(1)}, u32[]{:S(2)}, u32[]{:S(2)}) collective-permute-start(f32[1,8,128]{2,1,0:T(8,128)S(1)} %add_bitcast_fusion), channel_id=1, source_target_pairs={{0,6},{1,7},{2,8},{3,9},{4,10},{5,11},{6,12},{7,13},{8,14},{9,15},... | collective-permute-start | bytes 12296 | tf_op jit(solution)/shard_map/ppermute | solution.py:249
  53.6 6.6 %collective-permute-start.3 = (f32[3,8,128]{2,1,0:T(8,128)S(1)}, f32[3,8,128]{2,1,0:T(8,128)S(1)}, u32[]{:S(2)}, u32[]{:S(2)}) collective-permute-start(f32[3,8,128]{2,1,0:T(8,128)S(1)} %pad_maximum_fusion.spread_ref), channel_id=1, source_target_pairs={{0,2},{1,3},{2,4},{3,5},{4,6},{5,7},{6,8},{7,9},{8,10},{9,11},{10,... | collective-permute-start | bytes 36872 | tf_op jit(solution)/shard_map/ppermute | solution.py:249
  56.8 4.4 %collective-permute-start.4 = (f32[3,8,128]{2,1,0:T(8,128)S(1)}, f32[3,8,128]{2,1,0:T(8,128)S(1)}, u32[]{:S(2)}, u32[]{:S(2)}) collective-permute-start(f32[3,8,128]{2,1,0:T(8,128)S(1)} %pad_maximum_fusion.spread_ref), channel_id=1, source_target_pairs={{0,14},{1,15},{2,0},{3,1},{4,2},{5,3},{6,4},{7,5},{8,6},{9,7},{10,... | collective-permute-start | bytes 36872 | tf_op jit(solution)/shard_map/ppermute | solution.py:249
  61.2 1.0 %copy-start.2 = (bf16[1,256,1024]{2,1,0:T(8,128)(2,1)S(1)}, bf16[1,256,1024]{2,1,0:T(8,128)(2,1)}, u32[]{:S(2)}) copy-start(bf16[1,256,1024]{2,1,0:T(8,128)(2,1)} %value_ref.1) | copy-start | bytes 1572868
  63.4 16.8 %all-to-all-start.2 = ((f32[16,8,128]{2,1,0:T(8,128)}), f32[16,8,128]{2,1,0:T(8,128)S(1)}, u32[]{:S(2)}, u32[]{:S(2)}) async-start(f32[16,8,128]{2,1,0:T(8,128)} %shard_map.107), calls=%async_computation.2 | async-start | bytes 131072 | tf_op jit(solution)/shard_map/all_to_all | solution.py:284

commit v5 on v4

--- a/solution.py
+++ b/solution.py
@@ -20,6 +20,7 @@
 VMEM = pl.BlockSpec(memory_space=pltpu.VMEM)
 SMEM = pl.BlockSpec(memory_space=pltpu.SMEM)
 HBM = pl.BlockSpec(memory_space=pltpu.HBM)
+ANY = pl.BlockSpec(memory_space=pl.ANY)
 
 
 def call(body, out_shape, specs, args, cost):
@@ -46,12 +47,29 @@
 
 
 def spread_kernel(
-    slot_hbm, hidden_hbm, query_hbm, out_hbm, query_out, index_ref, slot, hidden, query, chunks, sem, out_sem
+    slot_hbm,
+    hidden_hbm,
+    query_hbm,
+    down_hbm,
+    up_hbm,
+    out_hbm,
+    query_out,
+    index_ref,
+    down_out,
+    up_out,
+    slot,
+    hidden,
+    query,
+    chunks,
+    sem,
+    out_sem,
 ):
     copies = [
         pltpu.make_async_copy(hidden_hbm, hidden, sem.at[0]),
         pltpu.make_async_copy(query_hbm, query, sem.at[1]),
         pltpu.make_async_copy(slot_hbm, slot, sem.at[2]),
+        pltpu.make_async_copy(down_hbm, down_out, sem.at[3]),
+        pltpu.make_async_copy(up_hbm, up_out, sem.at[4]),
     ]
     for copy in copies:
         copy.start()
@@ -83,11 +101,13 @@
         index_ref[2 * a] = index
         index_ref[2 * a + 1] = found
     index_ref[4] = lax.shift_right_logical(slot[o], 1)
+    copies[3].wait()
+    copies[4].wait()
     for send in sends:
         send.wait()
 
 
-def adapter_kernel(index_ref, arrived_ref, down_ref, up_ref, out_ref, mark_ref):
+def adapter_kernel(index_ref, arrived_ref, down_ref, up_ref, spread_ref, out_ref, mark_ref):
     ranks = down_ref.shape[2]
     rows, lanes = arrived_ref.shape[1:]
     mark_ref[0] = jnp.int32(0)
@@ -223,26 +243,33 @@
     slots, two, ranks, width = adapter_down_maps.shape
     shape = jax.ShapeDtypeStruct
 
-    parts, own_queries, index = pl.pallas_call(
+    parts, own_queries, index, down, up = pl.pallas_call(
         spread_kernel,
         out_shape=(
             pltpu.HBM((n_sess, 16, width // 16), BF16),
             shape((8, HD), F32),
             pltpu.SMEM((8,), jnp.int32),
+            shape(adapter_down_maps.shape, BF16),
+            shape(adapter_up_maps.shape, BF16),
         ),
-        in_specs=[HBM, HBM, HBM],
-        out_specs=(HBM, VMEM, SMEM),
+        in_specs=[HBM] * 5,
+        out_specs=(HBM, VMEM, SMEM, VMEM, VMEM),
         scratch_shapes=[
             pltpu.SMEM((n_sess,), jnp.int32),
             pltpu.VMEM(hidden.shape, BF16),
             pltpu.VMEM(queries.shape, BF16),
             pltpu.VMEM((n_sess, 16, width // 16), BF16),
-            pltpu.SemaphoreType.DMA((3,)),
+            pltpu.SemaphoreType.DMA((5,)),
             pltpu.SemaphoreType.DMA((4,)),
         ],
         cost_estimate=pl.CostEstimate(flops=10**5, bytes_accessed=10**5, transcendentals=0),
         compiler_params=pltpu.CompilerParams(vmem_limit_bytes=24 * 1024 * 1024),
-    )(*(pltpu.with_memory_space_constraint(x, pltpu.HBM) for x in (session_slot, hidden, queries)))
+    )(
+        *(
+            pltpu.with_memory_space_constraint(x, pltpu.HBM)
+            for x in (session_slot, hidden, queries, adapter_down_maps, adapter_up_maps)
+        )
+    )
     parts = lax.all_to_all(parts, "sess", 0, 0, tiled=True)
 
     def come(x, distance):
@@ -259,9 +286,9 @@
 
     terms, mark = call(
         adapter_kernel,
-        (shape((n_sess, 2 * KVH, HD), F32), pltpu.SMEM((8,), jnp.int32)),
-        [SMEM, VMEM, VMEM, VMEM],
-        [index, parts, adapter_down_maps, adapter_up_maps],
+        (pltpu.HBM((n_sess, 2 * KVH, HD), F32), pltpu.SMEM((8,), jnp.int32)),
+        [SMEM, VMEM, VMEM, VMEM, ANY],
+        [index, parts, down, up, spread],
         10**6,
     )
     terms = lax.all_to_all(terms, "sess", 0, 0, tiled=True)
@@ -276,7 +303,7 @@
     base = jnp.dot(hidden, key_value_weight, preferred_element_type=F32)
     packed = call(
         pack_kernel,
-        shape((n_tensor, 8, HD), F32),
+        pltpu.HBM((n_tensor, 8, HD), F32),
         [SMEM, VMEM, VMEM, VMEM],
         [index, terms, base, partial],
         10**5,

time: 81.6 us -> 73.3 us (0.90)
  waiting for transfers between devices: 25.4 us -> 15.9 us
  starting transfers between devices: 46.7 us -> 49.7 us
  local copies, waits for them, and re-layouts: 1.07 us -> 0.03 us
    all_to_all x1, waiting for transfers between devices: 11.3 us -> 0.01 us  [local(): parts = lax.all_to_all(parts, 'sess', 0, 0, tiled=True)]
    all_to_all x1, starting transfers between devices: 5.21 us -> 9.63 us  [local(): terms = lax.all_to_all(terms, 'sess', 0, 0, tiled=True)]
    all_to_all x1, waiting for transfers between devices: 0.01 us -> 1.51 us  [local(): terms = lax.all_to_all(terms, 'sess', 0, 0, tiled=True)]
    all_to_all x1, starting transfers between devices: 8.95 us -> 7.5 us  [local(): packed = lax.all_to_all(packed, 'tensor', 0, 0, tiled=True)]
    unnamed x12 -> x10, local copies, waits for them, and re-layouts: 1.07 us -> 0.03 us
  transfers between devices with their start and end apart: 8 -> 8, of which waited for: 4 -> 4; matrix products, arithmetic and copies ran while one was open for 2% -> 1% of each run, Pallas kernels for 2% -> 1%
where the time goes in v5:
time: 73.3 us; the launch traced here: 72.7 us
  starting transfers between devices  49.7 us (68%)
  waiting for transfers between devices  15.9 us (22%)
  Pallas kernels  4.76 us (6%)
  between operations  1.44 us (2%)
    ppermute x4, starting transfers between devices, come(): lax.ppermute(x, 'tensor', [(i, (i - 2 * distance) % n_tensor) for i in ra...  19.1 us
    all_to_all x1, starting transfers between devices, local(): parts = lax.all_to_all(parts, 'sess', 0, 0, tiled=True)  10.6 us
    all_to_all x1, starting transfers between devices, local(): terms = lax.all_to_all(terms, 'sess', 0, 0, tiled=True)  9.63 us
    all_to_all x1, waiting for transfers between devices, local(): packed = lax.all_to_all(packed, 'tensor', 0, 0, tiled=True)  7.72 us
    all_to_all x1, starting transfers between devices, local(): packed = lax.all_to_all(packed, 'tensor', 0, 0, tiled=True)  7.5 us
    ppermute x4, waiting for transfers between devices, come(): lax.ppermute(x, 'tensor', [(i, (i - 2 * distance) % n_tensor) for i in ra...  6.67 us
    pallas_call x4, Pallas kernels, call(): pl.pallas_call(body, out_shape=out_shape, in_specs=specs, out_specs=jax.t...  2.95 us
    ppermute x1, starting transfers between devices, local(): lax.ppermute(own_queries, 'tensor', [(i, i ^ 1) for i in range(n_tensor)])  2.86 us
  transfers between devices with their start and end apart: 8, of which 4 were waited for; matrix products, arithmetic and copies ran while one was open for 1% of the time, Pallas kernels for 1%

profile of v5, /device:TPU:1, one launch (start us, length us, event | category | flops | bytes accessed | tf_op | source)
XLA Modules:
  0.0 72.7 jit_solution(11210584496604803591)
XLA Ops:
  0.6 0.0 copy-start
  0.7 1.8 %shard_map.104 = (bf16[32,16,512]{2,1,0:T(8,128)(2,1)}, f32[8,128]{1,0:T(8,128)S(1)}, s32[8]{0:T(128)S(4)}, bf16[2,2,4,8192]{3,2,1,0:T(4,128)(2,1)S(1)}, bf16[2,2,4,1024]{3,2,1,0:T(4,128)(2,1)S(1)}) custom-call(s32[32]{0:T(128)} %slot_hbm.1, bf16[1,8192]{1,0:T(2,128)(2,1)} %hidden_hbm.1, bf16[1,512]{1,0:T(2,128)(2,1)} %query_ref.1, ...), custom_call_target="tpu_custom_call" | custom-call | flops 100000 | bytes 100000 | tf_op jit(solution)/shard_map/pallas_call | solution.py:246
  2.5 0.0 copy-start.1
  2.5 10.6 %all-to-all-start = ((bf16[32,16,512]{2,1,0:T(8,128)(2,1)}), bf16[32,16,512]{2,1,0:T(8,128)(2,1)S(1)}, u32[]{:S(2)}, u32[]{:S(2)}) async-start(bf16[32,16,512]{2,1,0:T(8,128)(2,1)} %get-tuple-element.10), calls=%async_computation | async-start | bytes 1048576 | tf_op jit(solution)/shard_map/all_to_all | solution.py:273
  13.1 2.9 %collective-permute-start = (f32[8,128]{1,0:T(8,128)S(1)}, f32[8,128]{1,0:T(8,128)S(1)}, u32[]{:S(2)}, u32[]{:S(2)}) collective-permute-start(f32[8,128]{1,0:T(8,128)S(1)} %get-tuple-element.13), channel_id=1, source_target_pairs={{0,1},{1,0},{2,3},{3,2},{4,5},{5,4},{6,7},{7,6},{8,9},{9,8},{10,11... | collective-permute-start | bytes 12296 | tf_op jit(solution)/shard_map/ppermute | solution.py:280
  16.7 0.1 fusion.5
  16.7 0.1 fusion.2
  16.8 0.1 negate_bitcast_fusion
  16.8 0.0 collective-permute-done
  16.9 10.6 %collective-permute-start.2 = (f32[1,8,128]{2,1,0:T(8,128)S(1)}, f32[1,8,128]{2,1,0:T(8,128)S(1)}, u32[]{:S(2)}, u32[]{:S(2)}) collective-permute-start(f32[1,8,128]{2,1,0:T(8,128)S(1)} %add_bitcast_fusion), channel_id=1, source_target_pairs={{0,10},{1,11},{2,12},{3,13},{4,14},{5,15},{6,0},{7,1},{8,2},{9,3},... | collective-permute-start | bytes 12296 | tf_op jit(solution)/shard_map/ppermute | solution.py:276
  27.5 1.9 %collective-permute-start.1 = (f32[1,8,128]{2,1,0:T(8,128)S(1)}, f32[1,8,128]{2,1,0:T(8,128)S(1)}, u32[]{:S(2)}, u32[]{:S(2)}) collective-permute-start(f32[1,8,128]{2,1,0:T(8,128)S(1)} %add_bitcast_fusion), channel_id=1, source_target_pairs={{0,6},{1,7},{2,8},{3,9},{4,10},{5,11},{6,12},{7,13},{8,14},{9,15},... | collective-permute-start | bytes 12296 | tf_op jit(solution)/shard_map/ppermute | solution.py:276
  29.4 0.1 fusion.4
  29.5 0.0 collective-permute-done.2
  29.5 5.4 %collective-permute-done.1 = f32[1,8,128]{2,1,0:T(8,128)S(1)} collective-permute-done((f32[1,8,128]{2,1,0:T(8,128)S(1)}, f32[1,8,128]{2,1,0:T(8,128)S(1)}, u32[]{:S(2)}, u32[]{:S(2)}) %collective-permute-start.1) | collective-permute-done | bytes 4128 | tf_op jit(solution)/shard_map/ppermute | solution.py:276
  34.9 0.0 all-to-all-done.arrived_ref
  34.9 1.0 %shard_map.105 = (f32[32,16,128]{2,1,0:T(8,128)}, s32[8]{0:T(128)S(4)}) custom-call(s32[8]{0:T(128)S(4)} %get-tuple-element.9.index_ref, bf16[32,16,512]{2,1,0:T(8,128)(2,1)S(1)} %all-to-all-done.arrived_ref, bf16[2,2,4,8192]{3,2,1,0:T(4,128)(2,1)S(1)} %get-tuple-element.11.down_ref, bf16[2,2,4,1024]{3,2,1,0:T(4,128)(2,1)S(1)} %get-tuple-element.12.up_ref, ...), custom_call_target="tpu_custom_call" | custom-call | flops 1000000 | bytes 1000000 | tf_op jit(solution)/shard_map/pallas_call | solution.py:27
  35.8 9.6 %all-to-all-start.1 = ((f32[32,16,128]{2,1,0:T(8,128)}), f32[32,16,128]{2,1,0:T(8,128)S(1)}, u32[]{:S(2)}, u32[]{:S(2)}) async-start(f32[32,16,128]{2,1,0:T(8,128)} %get-tuple-element.14), calls=%async_computation.1 | async-start | bytes 524288 | tf_op jit(solution)/shard_map/all_to_all | solution.py:294
  45.5 0.1 fusion.6
  45.5 0.0 copy-start.2
  45.6 0.1 broadcast_select_fusion
  45.6 0.4 fusion.base_ref
  46.0 3.1 %collective-permute-start.3 = (f32[3,8,128]{2,1,0:T(8,128)S(1)}, f32[3,8,128]{2,1,0:T(8,128)S(1)}, u32[]{:S(2)}, u32[]{:S(2)}) collective-permute-start(f32[3,8,128]{2,1,0:T(8,128)S(1)} %pad_maximum_fusion.spread_ref), channel_id=1, source_target_pairs={{0,2},{1,3},{2,4},{3,5},{4,6},{5,7},{6,8},{7,9},{8,10},{9,11},{10,... | collective-permute-start | bytes 36872 | tf_op jit(solution)/shard_map/ppermute | solution.py:276
  49.2 3.4 %collective-permute-start.4 = (f32[3,8,128]{2,1,0:T(8,128)S(1)}, f32[3,8,128]{2,1,0:T(8,128)S(1)}, u32[]{:S(2)}, u32[]{:S(2)}) collective-permute-start(f32[3,8,128]{2,1,0:T(8,128)S(1)} %pad_maximum_fusion.spread_ref), channel_id=1, source_target_pairs={{0,14},{1,15},{2,0},{3,1},{4,2},{5,3},{6,4},{7,5},{8,6},{9,7},{10,... | collective-permute-start | bytes 36872 | tf_op jit(solution)/shard_map/ppermute | solution.py:276
  52.5 0.1 maximum_bitcast_fusion
  52.6 1.3 %collective-permute-done.4.after_ref = f32[3,8,128]{2,1,0:T(8,128)S(1)} collective-permute-done((f32[3,8,128]{2,1,0:T(8,128)S(1)}, f32[3,8,128]{2,1,0:T(8,128)S(1)}, u32[]{:S(2)}, u32[]{:S(2)}) %collective-permute-start.4) | collective-permute-done | bytes 12320 | tf_op jit(solution)/shard_map/ppermute | solution.py:276
  53.9 0.5 shard_map.106.partial_ref
  54.4 1.5 %all-to-all-done.1.arrived_ref = f32[32,16,128]{2,1,0:T(8,128)S(1)} async-done(((f32[32,16,128]{2,1,0:T(8,128)}), f32[32,16,128]{2,1,0:T(8,128)S(1)}, u32[]{:S(2)}, u32[]{:S(2)}) %all-to-all-start.1) | async-done | bytes 262176 | tf_op jit(solution)/shard_map/all_to_all | solution.py:294
  55.9 0.6 shard_map.107
  56.5 7.5 %all-to-all-start.2 = ((f32[16,8,128]{2,1,0:T(8,128)}), f32[16,8,128]{2,1,0:T(8,128)S(1)}, u32[]{:S(2)}, u32[]{:S(2)}) async-start(f32[16,8,128]{2,1,0:T(8,128)} %shard_map.107), calls=%async_computation.2 | async-start | bytes 131072 | tf_op jit(solution)/shard_map/all_to_all | solution.py:311
  64.0 0.1 maximum_bitcast_fusion.1
  64.1 7.7 %all-to-all-done.2.arrived_ref = f32[16,8,128]{2,1,0:T(8,128)S(1)} async-done(((f32[16,8,128]{2,1,0:T(8,128)}), f32[16,8,128]{2,1,0:T(8,128)S(1)}, u32[]{:S(2)}, u32[]{:S(2)}) %all-to-all-start.2) | async-done | bytes 65568 | tf_op jit(solution)/shard_map/all_to_all | solution.py:311
  71.8 0.9 %shard_map.108 = (bf16[1,128]{1,0:T(2,128)(2,1)}, bf16[1,512]{1,0:T(2,128)(2,1)}) custom-call(f32[4,128]{1,0:T(4,128)S(1)} %pad_maximum_fusion.1.rot_ref, bf16[1,512]{1,0:T(2,128)(2,1)S(1)} %copy-done.3, f32[16,8,128]{2,1,0:T(8,128)S(1)} %all-to-all-done.2.arrived_ref), custom_call_target="tpu_custom_call" | custom-call | flops 100000 | bytes 100000 | tf_op jit(solution)/shard_map/pallas_call | solution.py:27
  (11 shorter events, 0.0 us)
Async XLA Ops:
  0.6 45.0 %copy-start = (bf16[8192,128]{1,0:T(8,128)(2,1)S(1)}, bf16[8192,128]{1,0:T(8,128)(2,1)}, u32[]{:S(2)}) copy-start(bf16[8192,128]{1,0:T(8,128)(2,1)} %param.10) | copy-start | bytes 6291460
  0.6 45.0 %copy-start.4 = (bf16[1,8192]{1,0:T(2,128)(2,1)S(1)}, bf16[1,8192]{1,0:T(2,128)(2,1)}, u32[]{:S(2)}) copy-start(bf16[1,8192]{1,0:T(2,128)(2,1)} %hidden_hbm.1) | copy-start | bytes 49156
  2.5 51.4 %copy-start.1 = (bf16[1,256,1024]{2,1,0:T(8,128)(2,1)S(1)}, bf16[1,256,1024]{2,1,0:T(8,128)(2,1)}, u32[]{:S(2)}) copy-start(bf16[1,256,1024]{2,1,0:T(8,128)(2,1)} %key_ref.1) | copy-start | bytes 1572868
  2.5 32.4 %all-to-all-start = ((bf16[32,16,512]{2,1,0:T(8,128)(2,1)}), bf16[32,16,512]{2,1,0:T(8,128)(2,1)S(1)}, u32[]{:S(2)}, u32[]{:S(2)}) async-start(bf16[32,16,512]{2,1,0:T(8,128)(2,1)} %get-tuple-element.10), calls=%async_computation | async-start | bytes 1048576 | tf_op jit(solution)/shard_map/all_to_all | solution.py:273
  13.1 3.7 %collective-permute-start = (f32[8,128]{1,0:T(8,128)S(1)}, f32[8,128]{1,0:T(8,128)S(1)}, u32[]{:S(2)}, u32[]{:S(2)}) collective-permute-start(f32[8,128]{1,0:T(8,128)S(1)} %get-tuple-element.13), channel_id=1, source_target_pairs={{0,1},{1,0},{2,3},{3,2},{4,5},{5,4},{6,7},{7,6},{8,9},{9,8},{10,11... | collective-permute-start | bytes 12296 | tf_op jit(solution)/shard_map/ppermute | solution.py:280
  16.9 12.6 %collective-permute-start.2 = (f32[1,8,128]{2,1,0:T(8,128)S(1)}, f32[1,8,128]{2,1,0:T(8,128)S(1)}, u32[]{:S(2)}, u32[]{:S(2)}) collective-permute-start(f32[1,8,128]{2,1,0:T(8,128)S(1)} %add_bitcast_fusion), channel_id=1, source_target_pairs={{0,10},{1,11},{2,12},{3,13},{4,14},{5,15},{6,0},{7,1},{8,2},{9,3},... | collective-permute-start | bytes 12296 | tf_op jit(solution)/shard_map/ppermute | solution.py:276
  27.5 7.4 %collective-permute-start.1 = (f32[1,8,128]{2,1,0:T(8,128)S(1)}, f32[1,8,128]{2,1,0:T(8,128)S(1)}, u32[]{:S(2)}, u32[]{:S(2)}) collective-permute-start(f32[1,8,128]{2,1,0:T(8,128)S(1)} %add_bitcast_fusion), channel_id=1, source_target_pairs={{0,6},{1,7},{2,8},{3,9},{4,10},{5,11},{6,12},{7,13},{8,14},{9,15},... | collective-permute-start | bytes 12296 | tf_op jit(solution)/shard_map/ppermute | solution.py:276
  35.8 36.0 %copy-start.3 = (bf16[1,512]{1,0:T(2,128)(2,1)S(1)}, bf16[1,512]{1,0:T(2,128)(2,1)}, u32[]{:S(2)}) copy-start(bf16[1,512]{1,0:T(2,128)(2,1)} %query_ref.1) | copy-start | bytes 3076
  35.8 20.0 %all-to-all-start.1 = ((f32[32,16,128]{2,1,0:T(8,128)}), f32[32,16,128]{2,1,0:T(8,128)S(1)}, u32[]{:S(2)}, u32[]{:S(2)}) async-start(f32[32,16,128]{2,1,0:T(8,128)} %get-tuple-element.14), calls=%async_computation.1 | async-start | bytes 524288 | tf_op jit(solution)/shard_map/all_to_all | solution.py:294
  45.5 8.4 %copy-start.2 = (bf16[1,256,1024]{2,1,0:T(8,128)(2,1)S(1)}, bf16[1,256,1024]{2,1,0:T(8,128)(2,1)}, u32[]{:S(2)}) copy-start(bf16[1,256,1024]{2,1,0:T(8,128)(2,1)} %value_ref.1) | copy-start | bytes 1572868
  46.0 6.6 %collective-permute-start.3 = (f32[3,8,128]{2,1,0:T(8,128)S(1)}, f32[3,8,128]{2,1,0:T(8,128)S(1)}, u32[]{:S(2)}, u32[]{:S(2)}) collective-permute-start(f32[3,8,128]{2,1,0:T(8,128)S(1)} %pad_maximum_fusion.spread_ref), channel_id=1, source_target_pairs={{0,2},{1,3},{2,4},{3,5},{4,6},{5,7},{6,8},{7,9},{8,10},{9,11},{10,... | collective-permute-start | bytes 36872 | tf_op jit(solution)/shard_map/ppermute | solution.py:276
  49.2 4.7 %collective-permute-start.4 = (f32[3,8,128]{2,1,0:T(8,128)S(1)}, f32[3,8,128]{2,1,0:T(8,128)S(1)}, u32[]{:S(2)}, u32[]{:S(2)}) collective-permute-start(f32[3,8,128]{2,1,0:T(8,128)S(1)} %pad_maximum_fusion.spread_ref), channel_id=1, source_target_pairs={{0,14},{1,15},{2,0},{3,1},{4,2},{5,3},{6,4},{7,5},{8,6},{9,7},{10,... | collective-permute-start | bytes 36872 | tf_op jit(solution)/shard_map/ppermute | solution.py:276
  56.5 15.3 %all-to-all-start.2 = ((f32[16,8,128]{2,1,0:T(8,128)}), f32[16,8,128]{2,1,0:T(8,128)S(1)}, u32[]{:S(2)}, u32[]{:S(2)}) async-start(f32[16,8,128]{2,1,0:T(8,128)} %shard_map.107), calls=%async_computation.2 | async-start | bytes 131072 | tf_op jit(solution)/shard_map/all_to_all | solution.py:311

commit v6 on v5

--- a/solution.py
+++ b/solution.py
@@ -20,7 +20,6 @@
 VMEM = pl.BlockSpec(memory_space=pltpu.VMEM)
 SMEM = pl.BlockSpec(memory_space=pltpu.SMEM)
 HBM = pl.BlockSpec(memory_space=pltpu.HBM)
-ANY = pl.BlockSpec(memory_space=pl.ANY)
 
 
 def call(body, out_shape, specs, args, cost):
@@ -32,7 +31,7 @@
             lambda x: SMEM if getattr(x, "memory_space", None) == pltpu.SMEM else VMEM, out_shape
         ),
         cost_estimate=pl.CostEstimate(flops=cost, bytes_accessed=cost, transcendentals=0),
-        compiler_params=pltpu.CompilerParams(vmem_limit_bytes=24 * 1024 * 1024),
+        compiler_params=pltpu.CompilerParams(vmem_limit_bytes=10 * 1024 * 1024),
     )(*args)
 
 
@@ -55,10 +54,10 @@
     out_hbm,
     query_out,
     index_ref,
-    down_out,
-    up_out,
+    shared_ref,
+    own_ref,
+    hidden,
     slot,
-    hidden,
     query,
     chunks,
     sem,
@@ -68,16 +67,40 @@
         pltpu.make_async_copy(hidden_hbm, hidden, sem.at[0]),
         pltpu.make_async_copy(query_hbm, query, sem.at[1]),
         pltpu.make_async_copy(slot_hbm, slot, sem.at[2]),
-        pltpu.make_async_copy(down_hbm, down_out, sem.at[3]),
-        pltpu.make_async_copy(up_hbm, up_out, sem.at[4]),
     ]
-    for copy in copies:
-        copy.start()
     n_sess, rows, lanes = out_hbm.shape
     o = lax.axis_index("sess")
     t = lax.axis_index("tensor")
+    half = rows * lanes
+    start = pl.multiple_of(jnp.bitwise_and(t, 1) * half, half)
+    other = pl.multiple_of(half - start, half)
+    up_width = up_hbm.shape[3]
+    copies.append(
+        pltpu.make_async_copy(
+            down_hbm.at[:, :, :, pl.ds(other, half)],
+            shared_ref.at[:, :, :, pl.ds(0, half)],
+            sem.at[3],
+        )
+    )
+    copies.append(
+        pltpu.make_async_copy(
+            up_hbm, shared_ref.at[:, :, :, pl.ds(half, up_width)], sem.at[4]
+        )
+    )
+    copies.append(
+        pltpu.make_async_copy(
+            down_hbm.at[:, :, :, pl.ds(start, half)],
+            own_ref.at[:, :, :, pl.ds(0, half)],
+            sem.at[5],
+        )
+    )
+    copies.append(
+        pltpu.make_async_copy(up_hbm, own_ref.at[:, :, :, pl.ds(half, up_width)], sem.at[6])
+    )
+    for copy in copies:
+        copy.start()
     copies[0].wait()
-    x = hidden[...].astype(F32)
+    x = hidden[:, pl.ds(start, half)].astype(F32)
     x = jnp.concatenate([x[:, j * lanes : (j + 1) * lanes] for j in range(rows)], axis=0)
     x = x.astype(BF16)
     sends = []
@@ -92,40 +115,55 @@
     q = jnp.concatenate([q[:, j * HD : (j + 1) * HD] for j in range(4)], axis=0)
     even = jnp.bitwise_and(t, 1) == 0
     zero = jnp.zeros_like(q)
-    query_out[...] = jnp.concatenate(
-        [jnp.where(even, q, zero), jnp.where(even, zero, q)], axis=0
-    )
+    upper, lower = jnp.where(even, q, zero), jnp.where(even, zero, q)
+    query_out[...] = jnp.concatenate([upper, lower], axis=0)
+    for a in range(2):
+        shared_ref[a, 0, :, half + up_width :] = upper.astype(BF16)
+        shared_ref[a, 1, :, half + up_width :] = lower.astype(BF16)
     copies[2].wait()
     for a in range(2):
         index, found = holder(slot, 2 * o + a, n_sess)
         index_ref[2 * a] = index
         index_ref[2 * a + 1] = found
     index_ref[4] = lax.shift_right_logical(slot[o], 1)
-    copies[3].wait()
-    copies[4].wait()
+    for copy in copies[3:]:
+        copy.wait()
     for send in sends:
         send.wait()
 
 
-def adapter_kernel(index_ref, arrived_ref, down_ref, up_ref, spread_ref, out_ref, mark_ref):
-    ranks = down_ref.shape[2]
+def reduce_kernel(index_ref, arrived_ref, own_ref, shared_ref, out_ref):
     rows, lanes = arrived_ref.shape[1:]
+    half = rows * lanes
+    for a in range(2):
+        x = arrived_ref[index_ref[2 * a]].astype(F32)
+        for k in range(2):
+            for r, maps in enumerate((own_ref, shared_ref)):
+                d = maps[a, k, :, :half].astype(F32)
+                acc = None
+                for i in range(rows):
+                    term = d[:, i * lanes : (i + 1) * lanes] * x[i : i + 1]
+                    acc = term if acc is None else acc + term
+                value = jnp.sum(acc, axis=1, keepdims=True)
+                out_ref[(a * 2 + k) * 2 + r] = jnp.broadcast_to(value, out_ref.shape[1:])
+
+
+def lift_kernel(index_ref, mine_ref, other_ref, own_ref, shared_ref, out_ref, mark_ref):
+    half = own_ref.shape[3] - KVH * HD
+    k = jnp.bitwise_and(lax.axis_index("tensor"), 1)
     mark_ref[0] = jnp.int32(0)
     out_ref[...] = jnp.zeros(out_ref.shape, out_ref.dtype)
     for a in range(2):
+        lifted = None
+        for r, maps in enumerate((own_ref, shared_ref)):
+            at = (a * 2 + k) * 2
+            reduced = (mine_ref[at + r] + other_ref[at + 1 - r])[:, :1].astype(BF16).astype(F32)
+            u = maps[a, k][:, half : half + KVH * HD].astype(F32)
+            part = jnp.sum(reduced * u, axis=0, keepdims=True)
+            lifted = part if lifted is None else lifted + part
+        heads = [lifted[:, h * HD : (h + 1) * HD] for h in range(KVH)]
+        lifted = jnp.concatenate(heads, axis=0) * ADAPTER_SCALE
         index = index_ref[2 * a]
-        x = arrived_ref[index].astype(F32)
-        heads = []
-        for k in range(2):
-            d = down_ref[a, k].astype(F32)
-            acc = None
-            for i in range(rows):
-                term = d[:, i * lanes : (i + 1) * lanes] * x[i : i + 1]
-                acc = term if acc is None else acc + term
-            reduced = jnp.sum(acc, axis=1, keepdims=True).astype(BF16).astype(F32)
-            lifted = jnp.sum(reduced * up_ref[a, k].astype(F32), axis=0, keepdims=True)
-            heads += [lifted[:, h * HD : (h + 1) * HD] for h in range(KVH)]
-        lifted = (jnp.concatenate(heads, axis=0) * ADAPTER_SCALE).astype(out_ref.dtype)
 
         @pl.when(index_ref[2 * a + 1] == 1)
         def _():
@@ -133,7 +171,7 @@
 
 
 def attention_kernel(
-    length_ref, mark_ref, before_ref, spread_ref, after_ref, key_ref, value_ref, out_ref
+    length_ref, mark_ref, near_ref, far_ref, key_ref, value_ref, out_ref
 ):
     span = key_ref.shape[1]
     t = lax.axis_index("tensor")
@@ -142,14 +180,9 @@
     v = value_ref[0]
     scores = []
     for g in range(KVH):
-        place = jnp.bitwise_and(g - lax.shift_right_logical(t, 1) + 4, 7)
-        row = lax.shift_right_logical(place * 11, 5)
-        part = place - 3 * row
-        q = jnp.where(
-            part == 0,
-            before_ref[row],
-            jnp.where(part == 1, spread_ref[row], after_ref[row]),
-        ).astype(BF16)
+        away = jnp.bitwise_xor(lax.shift_right_logical(t, 1), g)
+        row = lax.shift_right_logical(away, 1)
+        q = jnp.where(jnp.bitwise_and(away, 1) == 0, near_ref[row], far_ref[row]).astype(BF16)
         scores.append(
             lax.dot_general(
                 q,
@@ -181,11 +214,19 @@
             out_ref[2 * g + half] = jnp.concatenate([acc[rows], zero, stat], axis=0)
 
 
+def base_kernel(mark_ref, hidden_ref, weight_ref, out_ref):
+    out_ref[...] = jnp.dot(hidden_ref[...], weight_ref[...], preferred_element_type=F32)
+
+
 def pack_kernel(index_ref, arrived_ref, base_ref, partial_ref, out_ref):
     t = lax.axis_index("tensor")
     owner = index_ref[4]
     row = lax.broadcasted_iota(jnp.int32, (2 * KVH, HD), 0)
-    p = arrived_ref[owner].astype(F32) + jnp.where(row == t, base_ref[...], 0.0)
+    r = arrived_ref[owner]
+    keys = jnp.bitwise_and(t, 1) == 0
+    zero = jnp.zeros_like(r)
+    p = jnp.concatenate([jnp.where(keys, r, zero), jnp.where(keys, zero, r)], axis=0)
+    p = p + jnp.where(row == t, base_ref[...], 0.0)
     out_ref[...] = partial_ref[...]
     for d in range(out_ref.shape[0]):
         g = d // 2
@@ -242,53 +283,69 @@
     t = lax.axis_index("tensor")
     slots, two, ranks, width = adapter_down_maps.shape
     shape = jax.ShapeDtypeStruct
-
-    parts, own_queries, index, down, up = pl.pallas_call(
+    half = width // 2
+
+    parts, own_queries, index, shared, own, hidden = pl.pallas_call(
         spread_kernel,
         out_shape=(
-            pltpu.HBM((n_sess, 16, width // 16), BF16),
+            pltpu.HBM((n_sess, 16, half // 16), BF16),
             shape((8, HD), F32),
             pltpu.SMEM((8,), jnp.int32),
-            shape(adapter_down_maps.shape, BF16),
-            shape(adapter_up_maps.shape, BF16),
+            shape((slots, two, ranks, half + KVH * HD + HD), BF16),
+            shape((slots, two, ranks, half + KVH * HD), BF16),
+            shape(hidden.shape, BF16),
         ),
         in_specs=[HBM] * 5,
-        out_specs=(HBM, VMEM, SMEM, VMEM, VMEM),
+        out_specs=(HBM, VMEM, SMEM, VMEM, VMEM, VMEM),
         scratch_shapes=[
             pltpu.SMEM((n_sess,), jnp.int32),
-            pltpu.VMEM(hidden.shape, BF16),
             pltpu.VMEM(queries.shape, BF16),
-            pltpu.VMEM((n_sess, 16, width // 16), BF16),
-            pltpu.SemaphoreType.DMA((5,)),
+            pltpu.VMEM((n_sess, 16, half // 16), BF16),
+            pltpu.SemaphoreType.DMA((7,)),
             pltpu.SemaphoreType.DMA((4,)),
         ],
         cost_estimate=pl.CostEstimate(flops=10**5, bytes_accessed=10**5, transcendentals=0),
-        compiler_params=pltpu.CompilerParams(vmem_limit_bytes=24 * 1024 * 1024),
+        compiler_params=pltpu.CompilerParams(vmem_limit_bytes=10 * 1024 * 1024),
     )(
         *(
             pltpu.with_memory_space_constraint(x, pltpu.HBM)
-            for x in (session_slot, hidden, queries, adapter_down_maps, adapter_up_maps)
+            for x in (
+                session_slot,
+                hidden,
+                queries,
+                adapter_down_maps,
+                adapter_up_maps,
+            )
         )
     )
     parts = lax.all_to_all(parts, "sess", 0, 0, tiled=True)
 
-    def come(x, distance):
+    def swap(x, distance):
         return lax.ppermute(
-            x, "tensor", [(i, (i - 2 * distance) % n_tensor) for i in range(n_tensor)]
-        )
-
-    pair = own_queries + lax.ppermute(
-        own_queries, "tensor", [(i, i ^ 1) for i in range(n_tensor)]
-    )
+            x, "tensor", [(i, i ^ (2 * distance)) for i in range(n_tensor)]
+        )
+
+    other_core = [(i, i ^ 1) for i in range(n_tensor)]
+    shared = lax.ppermute(shared, "tensor", other_core)
+    pair = own_queries + shared[0, :, :, half + KVH * HD :].reshape(8, HD).astype(F32)
     pair = pair[None]
-    spread = jnp.concatenate([come(pair, -3), pair, come(pair, 3)])
-    before, after = come(spread, -1), come(spread, 1)
-
+    two_groups = jnp.concatenate([pair, swap(pair, 2)])
+    near = jnp.concatenate([two_groups, swap(two_groups, 4)])
+    far = swap(near, 1)
+
+    mine = call(
+        reduce_kernel,
+        shape((slots * two * 2, ranks, HD), F32),
+        [SMEM, VMEM, VMEM, VMEM],
+        [index, parts, own, shared],
+        10**6,
+    )
+    other = lax.ppermute(mine, "tensor", other_core)
     terms, mark = call(
-        adapter_kernel,
-        (pltpu.HBM((n_sess, 2 * KVH, HD), F32), pltpu.SMEM((8,), jnp.int32)),
-        [SMEM, VMEM, VMEM, VMEM, ANY],
-        [index, parts, down, up, spread],
+        lift_kernel,
+        (pltpu.HBM((n_sess, KVH, HD), F32), pltpu.SMEM((8,), jnp.int32)),
+        [SMEM, VMEM, VMEM, VMEM, VMEM],
+        [index, mine, other, own, shared],
         10**6,
     )
     terms = lax.all_to_all(terms, "sess", 0, 0, tiled=True)
@@ -296,22 +353,27 @@
     partial = call(
         attention_kernel,
         shape((n_tensor, 8, HD), F32),
-        [SMEM, SMEM, VMEM, VMEM, VMEM, VMEM, VMEM],
-        [lengths, mark, before, spread, after, cached_key_rows, cached_value_rows],
+        [SMEM, SMEM, VMEM, VMEM, VMEM, VMEM],
+        [lengths, mark, near, far, cached_key_rows, cached_value_rows],
         10**7,
     )
-    base = jnp.dot(hidden, key_value_weight, preferred_element_type=F32)
+    base = call(
+        base_kernel,
+        shape((1, HD), F32),
+        [SMEM, VMEM, VMEM],
+        [mark, hidden, pltpu.with_memory_space_constraint(key_value_weight, pltpu.HBM)],
+        10**4,
+    )
     packed = call(
         pack_kernel,
-        pltpu.HBM((n_tensor, 8, HD), F32),
+        shape((n_tensor, 8, HD), F32),
         [SMEM, VMEM, VMEM, VMEM],
         [index, terms, base, partial],
         10**5,
     )
     packed = lax.all_to_all(packed, "tensor", 0, 0, tiled=True)
 
-    half = HD // 2
-    inverse = jnp.exp(-(2.0 * jnp.arange(half, dtype=F32) / HD) * math.log(ROPE_BASE))
+    inverse = jnp.exp(-(2.0 * jnp.arange(HD // 2, dtype=F32) / HD) * math.log(ROPE_BASE))
     angles = lengths[0].astype(F32) * inverse
     cosine, sine = jnp.cos(angles), jnp.sin(angles)
     cosine = jnp.concatenate([cosine, cosine])

time: 73.3 us -> 72.8 us (level)
  starting transfers between devices: 49.7 us -> 46.5 us
  Pallas kernels: 4.76 us -> 6.6 us
  waiting for transfers between devices: 15.9 us -> 17.1 us
    ppermute x5, starting transfers between devices: 21.9 us -> 32.2 us  [the longest x3 19.5 us: swap(): lax.ppermute(x, 'tensor', [(i, i ^ 2 * distance) for i in range(n_tensor)])]
    ppermute x5, waiting for transfers between devices: 6.67 us -> 0.01 us  [the longest x3 0.01 us: swap(): lax.ppermute(x, 'tensor', [(i, i ^ 2 * distance) for i in range(n_tensor)])]
    all_to_all x1, starting transfers between devices: 10.6 us -> 4.31 us  [local(): parts = lax.all_to_all(parts, 'sess', 0, 0, tiled=True)]
    all_to_all x1, starting transfers between devices: 9.63 us -> 3.85 us  [local(): terms = lax.all_to_all(terms, 'sess', 0, 0, tiled=True)]
    all_to_all x1, waiting for transfers between devices: 0.01 us -> 5.19 us  [local(): parts = lax.all_to_all(parts, 'sess', 0, 0, tiled=True)]
    all_to_all x1, waiting for transfers between devices: 1.51 us -> 4.21 us  [local(): terms = lax.all_to_all(terms, 'sess', 0, 0, tiled=True)]
    pallas_call x4 -> x6, Pallas kernels: 2.95 us -> 4.96 us  [call(): pl.pallas_call(body, out_shape=out_shape, in_specs=specs, out_specs=jax.t...]
    all_to_all x1, starting transfers between devices: 7.5 us -> 6.15 us  [local(): packed = lax.all_to_all(packed, 'tensor', 0, 0, tiled=True)]
  transfers between devices with their start and end apart: 8 -> 8, of which waited for: 4 -> 3; matrix products, arithmetic and copies ran while one was open for 1% -> 1% of each run, Pallas kernels for 1% -> 5%
where the time goes in v6:
time: 72.8 us; the launch traced here: 72.3 us
  starting transfers between devices  46.5 us (64%)
  waiting for transfers between devices  17.1 us (23%)
  Pallas kernels  6.6 us (9%)
  between operations  1.49 us (2%)
    ppermute x3, starting transfers between devices, swap(): lax.ppermute(x, 'tensor', [(i, i ^ 2 * distance) for i in range(n_tensor)])  19.5 us
    ppermute x1, starting transfers between devices, local(): shared = lax.ppermute(shared, 'tensor', other_core)  8.79 us
    all_to_all x1, waiting for transfers between devices, local(): packed = lax.all_to_all(packed, 'tensor', 0, 0, tiled=True)  7.72 us
    all_to_all x1, starting transfers between devices, local(): packed = lax.all_to_all(packed, 'tensor', 0, 0, tiled=True)  6.15 us
    all_to_all x1, waiting for transfers between devices, local(): parts = lax.all_to_all(parts, 'sess', 0, 0, tiled=True)  5.19 us
    pallas_call x6, Pallas kernels, call(): pl.pallas_call(body, out_shape=out_shape, in_specs=specs, out_specs=jax.t...  4.96 us
    all_to_all x1, starting transfers between devices, local(): parts = lax.all_to_all(parts, 'sess', 0, 0, tiled=True)  4.31 us
    all_to_all x1, waiting for transfers between devices, local(): terms = lax.all_to_all(terms, 'sess', 0, 0, tiled=True)  4.21 us
  transfers between devices with their start and end apart: 8, of which 3 were waited for; matrix products, arithmetic and copies ran while one was open for 1% of the time, Pallas kernels for 5%

profile of v6, /device:TPU:1, one launch (start us, length us, event | category | flops | bytes accessed | tf_op | source)
XLA Modules:
  0.0 72.3 jit_solution(1030935466214253784)
XLA Ops:
  0.7 1.6 %shard_map.104 = (bf16[32,16,256]{2,1,0:T(8,128)(2,1)}, f32[8,128]{1,0:T(8,128)S(1)}, s32[8]{0:T(128)S(4)}, bf16[2,2,4,5248]{3,2,1,0:T(4,128)(2,1)S(1)}, bf16[2,...) custom-call(s32[32]{0:T(128)} %slot_hbm.1, bf16[1,8192]{1,0:T(2,128)(2,1)} %hidden_hbm.1, ...), custom_call_target="tpu_custom_call" | custom-call | flops 100000 | bytes 100000 | tf_op jit(solution)/shard_map/pallas_call | solution.py:288
  2.3 8.8 %collective-permute-start = (bf16[2,2,4,5248]{3,2,1,0:T(4,128)(2,1)S(1)}, bf16[2,2,4,5248]{3,2,1,0:T(4,128)(2,1)S(1)}, u32[]{:S(2)}, u32[]{:S(2)}) collective-permute-start(bf16[2,2,4,5248]{3,2,1,0:T(4,128)(2,1)S(1)} %get-tuple-element.13), channel_id=1, source_target_pairs={{0,1},{1,0},{2,3},{3,2},{4,5},{5,4},{6,7},{7,6},{8,9},{9,8},{10,11... | collective-permute-start | bytes 503816 | tf_op jit(solution)/shard_map/ppermute | solution.py:329
  11.1 4.3 %all-to-all-start = ((bf16[32,16,256]{2,1,0:T(8,128)(2,1)}), bf16[32,16,256]{2,1,0:T(8,128)(2,1)S(1)}, u32[]{:S(2)}, u32[]{:S(2)}) async-start(bf16[32,16,256]{2,1,0:T(8,128)(2,1)} %get-tuple-element.11), calls=%async_computation | async-start | bytes 524288 | tf_op jit(solution)/shard_map/all_to_all | solution.py:321
  16.1 0.1 fusion.3
  16.1 0.1 fusion.4
  16.2 0.1 negate_bitcast_fusion
  16.2 0.1 fusion.1
  16.3 0.0 collective-permute-done.shared_ref
  16.3 5.8 %collective-permute-start.2 = (f32[1,8,128]{2,1,0:T(8,128)S(1)}, f32[1,8,128]{2,1,0:T(8,128)S(1)}, u32[]{:S(2)}, u32[]{:S(2)}) collective-permute-start(f32[1,8,128]{2,1,0:T(8,128)S(1)} %fusion), channel_id=1, source_target_pairs={{0,4},{1,5},{2,6},{3,7},{4,0},{5,1},{6,2},{7,3},{8,12},{9,13},{10,... | collective-permute-start | bytes 12296 | tf_op jit(solution)/shard_map/ppermute | solution.py:324
  22.2 0.1 broadcast_select_fusion
  22.2 5.2 %all-to-all-done.arrived_ref = bf16[32,16,256]{2,1,0:T(8,128)(2,1)S(1)} async-done(((bf16[32,16,256]{2,1,0:T(8,128)(2,1)}), bf16[32,16,256]{2,1,0:T(8,128)(2,1)S(1)}, u32[]{:S(2)}, u32[]{:S(2)}) %all-to-all-start) | async-done | bytes 262176 | tf_op jit(solution)/shard_map/all_to_all | solution.py:321
  27.4 0.2 shard_map.105.mine_ref
  27.6 3.9 %collective-permute-start.1 = (f32[8,4,128]{2,1,0:T(4,128)S(1)}, f32[8,4,128]{2,1,0:T(4,128)S(1)}, u32[]{:S(2)}, u32[]{:S(2)}) collective-permute-start(f32[8,4,128]{2,1,0:T(4,128)S(1)} %shard_map.105.mine_ref), channel_id=1, source_target_pairs={{0,1},{1,0},{2,3},{3,2},{4,5},{5,4},{6,7},{7,6},{8,9},{9,8},{10,11... | collective-permute-start | bytes 49160 | tf_op jit(solution)/shard_map/ppermute | solution.py:343
  31.5 0.0 collective-permute-done.2
  31.5 0.0 copy-start.2
  31.5 10.6 %collective-permute-start.3 = (f32[2,8,128]{2,1,0:T(8,128)S(1)}, f32[2,8,128]{2,1,0:T(8,128)S(1)}, u32[]{:S(2)}, u32[]{:S(2)}) collective-permute-start(f32[2,8,128]{2,1,0:T(8,128)S(1)} %pad_maximum_fusion.1), channel_id=1, source_target_pairs={{0,8},{1,9},{2,10},{3,11},{4,12},{5,13},{6,14},{7,15},{8,0},{9,1},... | collective-permute-start | bytes 24584 | tf_op jit(solution)/shard_map/ppermute | solution.py:324
  42.1 0.0 collective-permute-done.1.other_ref
  42.2 0.9 %shard_map.106 = (f32[32,8,128]{2,1,0:T(8,128)}, s32[8]{0:T(128)S(4)}) custom-call(s32[8]{0:T(128)S(4)} %get-tuple-element.10.index_ref, f32[8,4,128]{2,1,0:T(4,128)S(1)} %shard_map.105.mine_ref, f32[8,4,128]{2,1,0:T(4,128)S(1)} %collective-permute-done.1.other_ref, bf16[2,2,4,5120]{3,2,1,0:T(4,128)(2,1)S(1)} %get-tuple-element.12.own_ref, ...), custom_call_target="tpu_custom_call" | custom-call | flops 1000000 | bytes 1000000 | tf_op jit(solution)/shard_map/pallas_call | solution.py:26
  43.0 3.9 %all-to-all-start.1 = ((f32[32,8,128]{2,1,0:T(8,128)}), f32[32,8,128]{2,1,0:T(8,128)S(1)}, u32[]{:S(2)}, u32[]{:S(2)}) async-start(f32[32,8,128]{2,1,0:T(8,128)} %get-tuple-element.14), calls=%async_computation.1 | async-start | bytes 262144 | tf_op jit(solution)/shard_map/all_to_all | solution.py:351
  46.9 0.1 fusion.5
  46.9 3.1 %collective-permute-start.4 = (f32[4,8,128]{2,1,0:T(8,128)S(1)}, f32[4,8,128]{2,1,0:T(8,128)S(1)}, u32[]{:S(2)}, u32[]{:S(2)}) collective-permute-start(f32[4,8,128]{2,1,0:T(8,128)S(1)} %pad_maximum_fusion.near_ref), channel_id=1, source_target_pairs={{0,2},{1,3},{2,0},{3,1},{4,6},{5,7},{6,4},{7,5},{8,10},{9,11},{10,... | collective-permute-start | bytes 49160 | tf_op jit(solution)/shard_map/ppermute | solution.py:324
  50.1 0.1 maximum_bitcast_fusion
  50.1 2.0 %shard_map.107.base_ref = f32[1,128]{1,0:T(1,128)S(1)} custom-call(s32[8]{0:T(128)S(4)} %get-tuple-element.15.mark_ref, bf16[1,8192]{1,0:T(2,128)(2,1)S(1)} %get-tuple-element.16.hidden_ref, bf16[8192,128]{1,0:T(8,128)(2,1)} %weight_ref.1), custom_call_target="tpu_custom_call" | custom-call | flops 10000 | bytes 10000 | tf_op jit(solution)/shard_map/pallas_call | solution.py:26
  52.1 0.0 collective-permute-done.4.far_ref
  52.1 0.0 copy-done
  52.1 0.5 shard_map.108.partial_ref
  52.6 4.2 %all-to-all-done.1.arrived_ref = f32[32,8,128]{2,1,0:T(8,128)S(1)} async-done(((f32[32,8,128]{2,1,0:T(8,128)}), f32[32,8,128]{2,1,0:T(8,128)S(1)}, u32[]{:S(2)}, u32[]{:S(2)}) %all-to-all-start.1) | async-done | bytes 131104 | tf_op jit(solution)/shard_map/all_to_all | solution.py:351
  56.8 0.6 shard_map.109
  57.4 6.2 %all-to-all-start.2 = ((f32[16,8,128]{2,1,0:T(8,128)}), f32[16,8,128]{2,1,0:T(8,128)S(1)}, u32[]{:S(2)}, u32[]{:S(2)}) async-start(f32[16,8,128]{2,1,0:T(8,128)} %shard_map.109), calls=%async_computation.2 | async-start | bytes 131072 | tf_op jit(solution)/shard_map/all_to_all | solution.py:374
  63.6 0.1 maximum_bitcast_fusion.1
  63.7 7.7 %all-to-all-done.2.arrived_ref = f32[16,8,128]{2,1,0:T(8,128)S(1)} async-done(((f32[16,8,128]{2,1,0:T(8,128)}), f32[16,8,128]{2,1,0:T(8,128)S(1)}, u32[]{:S(2)}, u32[]{:S(2)}) %all-to-all-start.2) | async-done | bytes 65568 | tf_op jit(solution)/shard_map/all_to_all | solution.py:374
  71.4 0.9 %shard_map.110 = (bf16[1,128]{1,0:T(2,128)(2,1)}, bf16[1,512]{1,0:T(2,128)(2,1)}) custom-call(f32[4,128]{1,0:T(4,128)S(1)} %pad_maximum_fusion.2.rot_ref, bf16[1,512]{1,0:T(2,128)(2,1)S(1)} %copy-done.2, f32[16,8,128]{2,1,0:T(8,128)S(1)} %all-to-all-done.2.arrived_ref), custom_call_target="tpu_custom_call" | custom-call | flops 100000 | bytes 100000 | tf_op jit(solution)/shard_map/pallas_call | solution.py:26
  (10 shorter events, 0.0 us)
Async XLA Ops:
  0.6 51.5 %copy-start = (bf16[1,256,1024]{2,1,0:T(8,128)(2,1)S(1)}, bf16[1,256,1024]{2,1,0:T(8,128)(2,1)}, u32[]{:S(2)}) copy-start(bf16[1,256,1024]{2,1,0:T(8,128)(2,1)} %key_ref.1) | copy-start | bytes 1572868
  0.6 51.5 %copy-start.1 = (bf16[1,256,1024]{2,1,0:T(8,128)(2,1)S(1)}, bf16[1,256,1024]{2,1,0:T(8,128)(2,1)}, u32[]{:S(2)}) copy-start(bf16[1,256,1024]{2,1,0:T(8,128)(2,1)} %value_ref.1) | copy-start | bytes 1572868
  2.3 14.0 %collective-permute-start = (bf16[2,2,4,5248]{3,2,1,0:T(4,128)(2,1)S(1)}, bf16[2,2,4,5248]{3,2,1,0:T(4,128)(2,1)S(1)}, u32[]{:S(2)}, u32[]{:S(2)}) collective-permute-start(bf16[2,2,4,5248]{3,2,1,0:T(4,128)(2,1)S(1)} %get-tuple-element.13), channel_id=1, source_target_pairs={{0,1},{1,0},{2,3},{3,2},{4,5},{5,4},{6,7},{7,6},{8,9},{9,8},{10,11... | collective-permute-start | bytes 503816 | tf_op jit(solution)/shard_map/ppermute | solution.py:329
  11.1 16.3 %all-to-all-start = ((bf16[32,16,256]{2,1,0:T(8,128)(2,1)}), bf16[32,16,256]{2,1,0:T(8,128)(2,1)S(1)}, u32[]{:S(2)}, u32[]{:S(2)}) async-start(bf16[32,16,256]{2,1,0:T(8,128)(2,1)} %get-tuple-element.11), calls=%async_computation | async-start | bytes 524288 | tf_op jit(solution)/shard_map/all_to_all | solution.py:321
  16.3 15.1 %collective-permute-start.2 = (f32[1,8,128]{2,1,0:T(8,128)S(1)}, f32[1,8,128]{2,1,0:T(8,128)S(1)}, u32[]{:S(2)}, u32[]{:S(2)}) collective-permute-start(f32[1,8,128]{2,1,0:T(8,128)S(1)} %fusion), channel_id=1, source_target_pairs={{0,4},{1,5},{2,6},{3,7},{4,0},{5,1},{6,2},{7,3},{8,12},{9,13},{10,... | collective-permute-start | bytes 12296 | tf_op jit(solution)/shard_map/ppermute | solution.py:324
  27.6 14.6 %collective-permute-start.1 = (f32[8,4,128]{2,1,0:T(4,128)S(1)}, f32[8,4,128]{2,1,0:T(4,128)S(1)}, u32[]{:S(2)}, u32[]{:S(2)}) collective-permute-start(f32[8,4,128]{2,1,0:T(4,128)S(1)} %shard_map.105.mine_ref), channel_id=1, source_target_pairs={{0,1},{1,0},{2,3},{3,2},{4,5},{5,4},{6,7},{7,6},{8,9},{9,8},{10,11... | collective-permute-start | bytes 49160 | tf_op jit(solution)/shard_map/ppermute | solution.py:343
  31.5 39.9 %copy-start.2 = (bf16[1,512]{1,0:T(2,128)(2,1)S(1)}, bf16[1,512]{1,0:T(2,128)(2,1)}, u32[]{:S(2)}) copy-start(bf16[1,512]{1,0:T(2,128)(2,1)} %query_ref.1) | copy-start | bytes 3076
  31.5 15.4 %collective-permute-start.3 = (f32[2,8,128]{2,1,0:T(8,128)S(1)}, f32[2,8,128]{2,1,0:T(8,128)S(1)}, u32[]{:S(2)}, u32[]{:S(2)}) collective-permute-start(f32[2,8,128]{2,1,0:T(8,128)S(1)} %pad_maximum_fusion.1), channel_id=1, source_target_pairs={{0,8},{1,9},{2,10},{3,11},{4,12},{5,13},{6,14},{7,15},{8,0},{9,1},... | collective-permute-start | bytes 24584 | tf_op jit(solution)/shard_map/ppermute | solution.py:324
  43.0 13.8 %all-to-all-start.1 = ((f32[32,8,128]{2,1,0:T(8,128)}), f32[32,8,128]{2,1,0:T(8,128)S(1)}, u32[]{:S(2)}, u32[]{:S(2)}) async-start(f32[32,8,128]{2,1,0:T(8,128)} %get-tuple-element.14), calls=%async_computation.1 | async-start | bytes 262144 | tf_op jit(solution)/shard_map/all_to_all | solution.py:351
  46.9 5.2 %collective-permute-start.4 = (f32[4,8,128]{2,1,0:T(8,128)S(1)}, f32[4,8,128]{2,1,0:T(8,128)S(1)}, u32[]{:S(2)}, u32[]{:S(2)}) collective-permute-start(f32[4,8,128]{2,1,0:T(8,128)S(1)} %pad_maximum_fusion.near_ref), channel_id=1, source_target_pairs={{0,2},{1,3},{2,0},{3,1},{4,6},{5,7},{6,4},{7,5},{8,10},{9,11},{10,... | collective-permute-start | bytes 49160 | tf_op jit(solution)/shard_map/ppermute | solution.py:324
  57.4 14.0 %all-to-all-start.2 = ((f32[16,8,128]{2,1,0:T(8,128)}), f32[16,8,128]{2,1,0:T(8,128)S(1)}, u32[]{:S(2)}, u32[]{:S(2)}) async-start(f32[16,8,128]{2,1,0:T(8,128)} %shard_map.109), calls=%async_computation.2 | async-start | bytes 131072 | tf_op jit(solution)/shard_map/all_to_all | solution.py:374

commit v7 on v6

--- a/solution.py
+++ b/solution.py
@@ -20,6 +20,7 @@
 VMEM = pl.BlockSpec(memory_space=pltpu.VMEM)
 SMEM = pl.BlockSpec(memory_space=pltpu.SMEM)
 HBM = pl.BlockSpec(memory_space=pltpu.HBM)
+ANY = pl.BlockSpec(memory_space=pl.ANY)
 
 
 def call(body, out_shape, specs, args, cost):
@@ -132,7 +133,7 @@
         send.wait()
 
 
-def reduce_kernel(index_ref, arrived_ref, own_ref, shared_ref, out_ref):
+def reduce_kernel(index_ref, arrived_ref, own_ref, shared_ref, groups_ref, out_ref):
     rows, lanes = arrived_ref.shape[1:]
     half = rows * lanes
     for a in range(2):
@@ -336,8 +337,8 @@
     mine = call(
         reduce_kernel,
         shape((slots * two * 2, ranks, HD), F32),
-        [SMEM, VMEM, VMEM, VMEM],
-        [index, parts, own, shared],
+        [SMEM, VMEM, VMEM, VMEM, ANY],
+        [index, parts, own, shared, two_groups],
         10**6,
     )
     other = lax.ppermute(mine, "tensor", other_core)

time: 72.8 us -> 72.7 us (level)
  waiting for transfers between devices: 17.1 us -> 13.1 us
  starting transfers between devices: 46.5 us -> 50.5 us
    all_to_all x1, starting transfers between devices: 4.31 us -> 10.5 us  [local(): parts = lax.all_to_all(parts, 'sess', 0, 0, tiled=True)]
    ppermute x1, starting transfers between devices: 8.79 us -> 2.86 us  [local(): shared = lax.ppermute(shared, 'tensor', other_core)]
    all_to_all x1, waiting for transfers between devices: 5.19 us -> 0.21 us  [local(): parts = lax.all_to_all(parts, 'sess', 0, 0, tiled=True)]
    all_to_all x1, starting transfers between devices: 3.85 us -> 6.51 us  [local(): terms = lax.all_to_all(terms, 'sess', 0, 0, tiled=True)]
    ppermute x3, waiting for transfers between devices: 0.01 us -> 1.22 us  [swap(): lax.ppermute(x, 'tensor', [(i, i ^ 2 * distance) for i in range(n_tensor)])]
  transfers between devices with their start and end apart: 8 -> 8, of which waited for: 3 -> 5; matrix products, arithmetic and copies ran while one was open for 1% -> 1% of each run, Pallas kernels for 5% -> 5%
where the time goes in v7:
time: 72.7 us; the launch traced here: 72.1 us
  starting transfers between devices  50.5 us (69%)
  waiting for transfers between devices  13.1 us (18%)
  Pallas kernels  6.6 us (9%)
  between operations  1.45 us (2%)
    ppermute x3, starting transfers between devices, swap(): lax.ppermute(x, 'tensor', [(i, i ^ 2 * distance) for i in range(n_tensor)])  19.7 us
    all_to_all x1, starting transfers between devices, local(): parts = lax.all_to_all(parts, 'sess', 0, 0, tiled=True)  10.5 us
    all_to_all x1, waiting for transfers between devices, local(): packed = lax.all_to_all(packed, 'tensor', 0, 0, tiled=True)  7.72 us
    all_to_all x1, starting transfers between devices, local(): packed = lax.all_to_all(packed, 'tensor', 0, 0, tiled=True)  6.58 us
    all_to_all x1, starting transfers between devices, local(): terms = lax.all_to_all(terms, 'sess', 0, 0, tiled=True)  6.51 us
    pallas_call x6, Pallas kernels, call(): pl.pallas_call(body, out_shape=out_shape, in_specs=specs, out_specs=jax.t...  4.96 us
    ppermute x1, starting transfers between devices, local(): other = lax.ppermute(mine, 'tensor', other_core)  4.35 us
    all_to_all x1, waiting for transfers between devices, local(): terms = lax.all_to_all(terms, 'sess', 0, 0, tiled=True)  3.73 us
  transfers between devices with their start and end apart: 8, of which 5 were waited for; matrix products, arithmetic and copies ran while one was open for 1% of the time, Pallas kernels for 5%

profile of v7, /device:TPU:1, one launch (start us, length us, event | category | flops | bytes accessed | tf_op | source)
XLA Modules:
  0.0 72.1 jit_solution(864298699005512801)
XLA Ops:
  0.7 1.6 %shard_map.104 = (bf16[32,16,256]{2,1,0:T(8,128)(2,1)}, f32[8,128]{1,0:T(8,128)S(1)}, s32[8]{0:T(128)S(4)}, bf16[2,2,4,5248]{3,2,1,0:T(4,128)(2,1)S(1)}, bf16[2,...) custom-call(s32[32]{0:T(128)} %slot_hbm.1, bf16[1,8192]{1,0:T(2,128)(2,1)} %hidden_hbm.1, ...), custom_call_target="tpu_custom_call" | custom-call | flops 100000 | bytes 100000 | tf_op jit(solution)/shard_map/pallas_call | solution.py:289
  2.3 10.5 %all-to-all-start = ((bf16[32,16,256]{2,1,0:T(8,128)(2,1)}), bf16[32,16,256]{2,1,0:T(8,128)(2,1)S(1)}, u32[]{:S(2)}, u32[]{:S(2)}) async-start(bf16[32,16,256]{2,1,0:T(8,128)(2,1)} %get-tuple-element.11), calls=%async_computation | async-start | bytes 524288 | tf_op jit(solution)/shard_map/all_to_all | solution.py:322
  12.8 2.9 %collective-permute-start = (bf16[2,2,4,5248]{3,2,1,0:T(4,128)(2,1)S(1)}, bf16[2,2,4,5248]{3,2,1,0:T(4,128)(2,1)S(1)}, u32[]{:S(2)}, u32[]{:S(2)}) collective-permute-start(bf16[2,2,4,5248]{3,2,1,0:T(4,128)(2,1)S(1)} %get-tuple-element.13), channel_id=1, source_target_pairs={{0,1},{1,0},{2,3},{3,2},{4,5},{5,4},{6,7},{7,6},{8,9},{9,8},{10,11... | collective-permute-start | bytes 503816 | tf_op jit(solution)/shard_map/ppermute | solution.py:330
  16.3 0.1 fusion.1
  16.4 0.1 fusion.4
  16.5 0.1 negate_bitcast_fusion
  16.5 0.2 collective-permute-done.shared_ref
  16.7 5.8 %collective-permute-start.1 = (f32[1,8,128]{2,1,0:T(8,128)S(1)}, f32[1,8,128]{2,1,0:T(8,128)S(1)}, u32[]{:S(2)}, u32[]{:S(2)}) collective-permute-start(f32[1,8,128]{2,1,0:T(8,128)S(1)} %fusion), channel_id=1, source_target_pairs={{0,4},{1,5},{2,6},{3,7},{4,0},{5,1},{6,2},{7,3},{8,12},{9,13},{10,... | collective-permute-start | bytes 12296 | tf_op jit(solution)/shard_map/ppermute | solution.py:325
  22.5 0.1 fusion.3
  22.6 1.2 %collective-permute-done.1 = f32[1,8,128]{2,1,0:T(8,128)S(1)} collective-permute-done((f32[1,8,128]{2,1,0:T(8,128)S(1)}, f32[1,8,128]{2,1,0:T(8,128)S(1)}, u32[]{:S(2)}, u32[]{:S(2)}) %collective-permute-start.1) | collective-permute-done | bytes 4128 | tf_op jit(solution)/shard_map/ppermute | solution.py:325
  23.8 0.2 all-to-all-done.arrived_ref
  24.0 0.2 shard_map.105.mine_ref
  24.2 4.3 %collective-permute-start.2 = (f32[8,4,128]{2,1,0:T(4,128)S(1)}, f32[8,4,128]{2,1,0:T(4,128)S(1)}, u32[]{:S(2)}, u32[]{:S(2)}) collective-permute-start(f32[8,4,128]{2,1,0:T(4,128)S(1)} %shard_map.105.mine_ref), channel_id=1, source_target_pairs={{0,1},{1,0},{2,3},{3,2},{4,5},{5,4},{6,7},{7,6},{8,9},{9,8},{10,11... | collective-permute-start | bytes 49160 | tf_op jit(solution)/shard_map/ppermute | solution.py:344
  28.5 0.1 broadcast_select_fusion
  28.6 10.8 %collective-permute-start.3 = (f32[2,8,128]{2,1,0:T(8,128)S(1)}, f32[2,8,128]{2,1,0:T(8,128)S(1)}, u32[]{:S(2)}, u32[]{:S(2)}) collective-permute-start(f32[2,8,128]{2,1,0:T(8,128)S(1)} %pad_maximum_fusion.1.groups_ref), channel_id=1, source_target_pairs={{0,8},{1,9},{2,10},{3,11},{4,12},{5,13},{6,14},{7,15},{8,0},{9,1},... | collective-permute-start | bytes 24584 | tf_op jit(solution)/shard_map/ppermute | solution.py:325
  39.4 0.0 collective-permute-done.2.other_ref
  39.4 0.8 %shard_map.106 = (f32[32,8,128]{2,1,0:T(8,128)}, s32[8]{0:T(128)S(4)}) custom-call(s32[8]{0:T(128)S(4)} %get-tuple-element.10.index_ref, f32[8,4,128]{2,1,0:T(4,128)S(1)} %shard_map.105.mine_ref, f32[8,4,128]{2,1,0:T(4,128)S(1)} %collective-permute-done.2.other_ref, bf16[2,2,4,5120]{3,2,1,0:T(4,128)(2,1)S(1)} %get-tuple-element.12.own_ref, ...), custom_call_target="tpu_custom_call" | custom-call | flops 1000000 | bytes 1000000 | tf_op jit(solution)/shard_map/pallas_call | solution.py:27
  40.2 6.5 %all-to-all-start.1 = ((f32[32,8,128]{2,1,0:T(8,128)}), f32[32,8,128]{2,1,0:T(8,128)S(1)}, u32[]{:S(2)}, u32[]{:S(2)}) async-start(f32[32,8,128]{2,1,0:T(8,128)} %get-tuple-element.15), calls=%async_computation.1 | async-start | bytes 262144 | tf_op jit(solution)/shard_map/all_to_all | solution.py:352
  46.8 0.1 fusion.5
  46.8 0.0 collective-permute-done.3
  46.8 3.1 %collective-permute-start.4 = (f32[4,8,128]{2,1,0:T(8,128)S(1)}, f32[4,8,128]{2,1,0:T(8,128)S(1)}, u32[]{:S(2)}, u32[]{:S(2)}) collective-permute-start(f32[4,8,128]{2,1,0:T(8,128)S(1)} %pad_maximum_fusion.near_ref), channel_id=1, source_target_pairs={{0,2},{1,3},{2,0},{3,1},{4,6},{5,7},{6,4},{7,5},{8,10},{9,11},{10,... | collective-permute-start | bytes 49160 | tf_op jit(solution)/shard_map/ppermute | solution.py:325
  49.9 0.1 maximum_bitcast_fusion
  50.0 2.0 %shard_map.107.base_ref = f32[1,128]{1,0:T(1,128)S(1)} custom-call(s32[8]{0:T(128)S(4)} %get-tuple-element.16.mark_ref, bf16[1,8192]{1,0:T(2,128)(2,1)S(1)} %get-tuple-element.17.hidden_ref, bf16[8192,128]{1,0:T(8,128)(2,1)} %weight_ref.1), custom_call_target="tpu_custom_call" | custom-call | flops 10000 | bytes 10000 | tf_op jit(solution)/shard_map/pallas_call | solution.py:27
  52.0 0.0 collective-permute-done.4.far_ref
  52.0 0.0 copy-done.1
  52.0 0.5 shard_map.108.partial_ref
  52.5 3.7 %all-to-all-done.1.arrived_ref = f32[32,8,128]{2,1,0:T(8,128)S(1)} async-done(((f32[32,8,128]{2,1,0:T(8,128)}), f32[32,8,128]{2,1,0:T(8,128)S(1)}, u32[]{:S(2)}, u32[]{:S(2)}) %all-to-all-start.1) | async-done | bytes 131104 | tf_op jit(solution)/shard_map/all_to_all | solution.py:352
  56.2 0.6 shard_map.109
  56.9 6.6 %all-to-all-start.2 = ((f32[16,8,128]{2,1,0:T(8,128)}), f32[16,8,128]{2,1,0:T(8,128)S(1)}, u32[]{:S(2)}, u32[]{:S(2)}) async-start(f32[16,8,128]{2,1,0:T(8,128)} %shard_map.109), calls=%async_computation.2 | async-start | bytes 131072 | tf_op jit(solution)/shard_map/all_to_all | solution.py:375
  63.4 0.1 maximum_bitcast_fusion.1
  63.5 7.7 %all-to-all-done.2.arrived_ref = f32[16,8,128]{2,1,0:T(8,128)S(1)} async-done(((f32[16,8,128]{2,1,0:T(8,128)}), f32[16,8,128]{2,1,0:T(8,128)S(1)}, u32[]{:S(2)}, u32[]{:S(2)}) %all-to-all-start.2) | async-done | bytes 65568 | tf_op jit(solution)/shard_map/all_to_all | solution.py:375
  71.2 0.9 %shard_map.110 = (bf16[1,128]{1,0:T(2,128)(2,1)}, bf16[1,512]{1,0:T(2,128)(2,1)}) custom-call(f32[4,128]{1,0:T(4,128)S(1)} %pad_maximum_fusion.2.rot_ref, bf16[1,512]{1,0:T(2,128)(2,1)S(1)} %copy-done.2, f32[16,8,128]{2,1,0:T(8,128)S(1)} %all-to-all-done.2.arrived_ref), custom_call_target="tpu_custom_call" | custom-call | flops 100000 | bytes 100000 | tf_op jit(solution)/shard_map/pallas_call | solution.py:27
  (10 shorter events, 0.0 us)
Async XLA Ops:
  0.6 51.4 %copy-start.1 = (bf16[1,256,1024]{2,1,0:T(8,128)(2,1)S(1)}, bf16[1,256,1024]{2,1,0:T(8,128)(2,1)}, u32[]{:S(2)}) copy-start(bf16[1,256,1024]{2,1,0:T(8,128)(2,1)} %value_ref.1) | copy-start | bytes 1572868
  0.6 51.4 %copy-start = (bf16[1,256,1024]{2,1,0:T(8,128)(2,1)S(1)}, bf16[1,256,1024]{2,1,0:T(8,128)(2,1)}, u32[]{:S(2)}) copy-start(bf16[1,256,1024]{2,1,0:T(8,128)(2,1)} %key_ref.1) | copy-start | bytes 1572868
  2.3 21.7 %all-to-all-start = ((bf16[32,16,256]{2,1,0:T(8,128)(2,1)}), bf16[32,16,256]{2,1,0:T(8,128)(2,1)S(1)}, u32[]{:S(2)}, u32[]{:S(2)}) async-start(bf16[32,16,256]{2,1,0:T(8,128)(2,1)} %get-tuple-element.11), calls=%async_computation | async-start | bytes 524288 | tf_op jit(solution)/shard_map/all_to_all | solution.py:322
  12.8 3.9 %collective-permute-start = (bf16[2,2,4,5248]{3,2,1,0:T(4,128)(2,1)S(1)}, bf16[2,2,4,5248]{3,2,1,0:T(4,128)(2,1)S(1)}, u32[]{:S(2)}, u32[]{:S(2)}) collective-permute-start(bf16[2,2,4,5248]{3,2,1,0:T(4,128)(2,1)S(1)} %get-tuple-element.13), channel_id=1, source_target_pairs={{0,1},{1,0},{2,3},{3,2},{4,5},{5,4},{6,7},{7,6},{8,9},{9,8},{10,11... | collective-permute-start | bytes 503816 | tf_op jit(solution)/shard_map/ppermute | solution.py:330
  16.7 7.1 %collective-permute-start.1 = (f32[1,8,128]{2,1,0:T(8,128)S(1)}, f32[1,8,128]{2,1,0:T(8,128)S(1)}, u32[]{:S(2)}, u32[]{:S(2)}) collective-permute-start(f32[1,8,128]{2,1,0:T(8,128)S(1)} %fusion), channel_id=1, source_target_pairs={{0,4},{1,5},{2,6},{3,7},{4,0},{5,1},{6,2},{7,3},{8,12},{9,13},{10,... | collective-permute-start | bytes 12296 | tf_op jit(solution)/shard_map/ppermute | solution.py:325
  24.2 15.2 %collective-permute-start.2 = (f32[8,4,128]{2,1,0:T(4,128)S(1)}, f32[8,4,128]{2,1,0:T(4,128)S(1)}, u32[]{:S(2)}, u32[]{:S(2)}) collective-permute-start(f32[8,4,128]{2,1,0:T(4,128)S(1)} %shard_map.105.mine_ref), channel_id=1, source_target_pairs={{0,1},{1,0},{2,3},{3,2},{4,5},{5,4},{6,7},{7,6},{8,9},{9,8},{10,11... | collective-permute-start | bytes 49160 | tf_op jit(solution)/shard_map/ppermute | solution.py:344
  28.6 42.6 %copy-start.2 = (bf16[1,512]{1,0:T(2,128)(2,1)S(1)}, bf16[1,512]{1,0:T(2,128)(2,1)}, u32[]{:S(2)}) copy-start(bf16[1,512]{1,0:T(2,128)(2,1)} %query_ref.1) | copy-start | bytes 3076
  28.6 18.2 %collective-permute-start.3 = (f32[2,8,128]{2,1,0:T(8,128)S(1)}, f32[2,8,128]{2,1,0:T(8,128)S(1)}, u32[]{:S(2)}, u32[]{:S(2)}) collective-permute-start(f32[2,8,128]{2,1,0:T(8,128)S(1)} %pad_maximum_fusion.1.groups_ref), channel_id=1, source_target_pairs={{0,8},{1,9},{2,10},{3,11},{4,12},{5,13},{6,14},{7,15},{8,0},{9,1},... | collective-permute-start | bytes 24584 | tf_op jit(solution)/shard_map/ppermute | solution.py:325
  40.2 16.0 %all-to-all-start.1 = ((f32[32,8,128]{2,1,0:T(8,128)}), f32[32,8,128]{2,1,0:T(8,128)S(1)}, u32[]{:S(2)}, u32[]{:S(2)}) async-start(f32[32,8,128]{2,1,0:T(8,128)} %get-tuple-element.15), calls=%async_computation.1 | async-start | bytes 262144 | tf_op jit(solution)/shard_map/all_to_all | solution.py:352
  46.8 5.2 %collective-permute-start.4 = (f32[4,8,128]{2,1,0:T(8,128)S(1)}, f32[4,8,128]{2,1,0:T(8,128)S(1)}, u32[]{:S(2)}, u32[]{:S(2)}) collective-permute-start(f32[4,8,128]{2,1,0:T(8,128)S(1)} %pad_maximum_fusion.near_ref), channel_id=1, source_target_pairs={{0,2},{1,3},{2,0},{3,1},{4,6},{5,7},{6,4},{7,5},{8,10},{9,11},{10,... | collective-permute-start | bytes 49160 | tf_op jit(solution)/shard_map/ppermute | solution.py:325
  56.9 14.4 %all-to-all-start.2 = ((f32[16,8,128]{2,1,0:T(8,128)}), f32[16,8,128]{2,1,0:T(8,128)S(1)}, u32[]{:S(2)}, u32[]{:S(2)}) async-start(f32[16,8,128]{2,1,0:T(8,128)} %shard_map.109), calls=%async_computation.2 | async-start | bytes 131072 | tf_op jit(solution)/shard_map/all_to_all | solution.py:375

commit v8 on v7

--- a/solution.py
+++ b/solution.py
@@ -182,7 +182,7 @@
     scores = []
     for g in range(KVH):
         away = jnp.bitwise_xor(lax.shift_right_logical(t, 1), g)
-        row = lax.shift_right_logical(away, 1)
+        row = lax.shift_right_logical(away, 2) + jnp.bitwise_and(away, 2)
         q = jnp.where(jnp.bitwise_and(away, 1) == 0, near_ref[row], far_ref[row]).astype(BF16)
         scores.append(
             lax.dot_general(
@@ -330,8 +330,8 @@
     shared = lax.ppermute(shared, "tensor", other_core)
     pair = own_queries + shared[0, :, :, half + KVH * HD :].reshape(8, HD).astype(F32)
     pair = pair[None]
-    two_groups = jnp.concatenate([pair, swap(pair, 2)])
-    near = jnp.concatenate([two_groups, swap(two_groups, 4)])
+    two_groups = jnp.concatenate([pair, swap(pair, 4)])
+    near = jnp.concatenate([two_groups, swap(two_groups, 2)])
     far = swap(near, 1)
 
     mine = call(

time: 72.7 us -> 74.7 us (1.028)
  starting transfers between devices: 50.5 us -> 53 us
    all_to_all x1, starting transfers between devices: 6.51 us -> 9.49 us  [local(): terms = lax.all_to_all(terms, 'sess', 0, 0, tiled=True)]
    all_to_all x1, starting transfers between devices: 6.58 us -> 9.18 us  [local(): packed = lax.all_to_all(packed, 'tensor', 0, 0, tiled=True)]
    ppermute x3, starting transfers between devices: 19.7 us -> 17.9 us  [swap(): lax.ppermute(x, 'tensor', [(i, i ^ 2 * distance) for i in range(n_tensor)])]
    ppermute x1, starting transfers between devices: 4.35 us -> 3.13 us  [local(): other = lax.ppermute(mine, 'tensor', other_core)]
  transfers between devices with their start and end apart: 8 -> 8, of which waited for: 5 -> 4; matrix products, arithmetic and copies ran while one was open for 1% -> 1% of each run, Pallas kernels for 5% -> 4%
where the time goes in v8:
time: 74.7 us; the launch traced here: 74.2 us
  starting transfers between devices  53 us (71%)
  waiting for transfers between devices  12.6 us (17%)
  Pallas kernels  6.6 us (9%)
  between operations  1.45 us (2%)
    ppermute x3, starting transfers between devices, swap(): lax.ppermute(x, 'tensor', [(i, i ^ 2 * distance) for i in range(n_tensor)])  17.9 us
    all_to_all x1, starting transfers between devices, local(): parts = lax.all_to_all(parts, 'sess', 0, 0, tiled=True)  10.5 us
    all_to_all x1, starting transfers between devices, local(): terms = lax.all_to_all(terms, 'sess', 0, 0, tiled=True)  9.49 us
    all_to_all x1, starting transfers between devices, local(): packed = lax.all_to_all(packed, 'tensor', 0, 0, tiled=True)  9.18 us
    all_to_all x1, waiting for transfers between devices, local(): packed = lax.all_to_all(packed, 'tensor', 0, 0, tiled=True)  7.72 us
    pallas_call x6, Pallas kernels, call(): pl.pallas_call(body, out_shape=out_shape, in_specs=specs, out_specs=jax.t...  4.96 us
    all_to_all x1, waiting for transfers between devices, local(): terms = lax.all_to_all(terms, 'sess', 0, 0, tiled=True)  3.76 us
    ppermute x1, starting transfers between devices, local(): other = lax.ppermute(mine, 'tensor', other_core)  3.13 us
  transfers between devices with their start and end apart: 8, of which 4 were waited for; matrix products, arithmetic and copies ran while one was open for 1% of the time, Pallas kernels for 4%

profile of v8, /device:TPU:1, one launch (start us, length us, event | category | flops | bytes accessed | tf_op | source)
XLA Modules:
  0.0 74.2 jit_solution(9894036849108699028)
XLA Ops:
  0.7 1.6 %shard_map.104 = (bf16[32,16,256]{2,1,0:T(8,128)(2,1)}, f32[8,128]{1,0:T(8,128)S(1)}, s32[8]{0:T(128)S(4)}, bf16[2,2,4,5248]{3,2,1,0:T(4,128)(2,1)S(1)}, bf16[2,...) custom-call(s32[32]{0:T(128)} %slot_hbm.1, bf16[1,8192]{1,0:T(2,128)(2,1)} %hidden_hbm.1, ...), custom_call_target="tpu_custom_call" | custom-call | flops 100000 | bytes 100000 | tf_op jit(solution)/shard_map/pallas_call | solution.py:289
  2.3 10.5 %all-to-all-start = ((bf16[32,16,256]{2,1,0:T(8,128)(2,1)}), bf16[32,16,256]{2,1,0:T(8,128)(2,1)S(1)}, u32[]{:S(2)}, u32[]{:S(2)}) async-start(bf16[32,16,256]{2,1,0:T(8,128)(2,1)} %get-tuple-element.11), calls=%async_computation | async-start | bytes 524288 | tf_op jit(solution)/shard_map/all_to_all | solution.py:322
  12.8 2.9 %collective-permute-start = (bf16[2,2,4,5248]{3,2,1,0:T(4,128)(2,1)S(1)}, bf16[2,2,4,5248]{3,2,1,0:T(4,128)(2,1)S(1)}, u32[]{:S(2)}, u32[]{:S(2)}) collective-permute-start(bf16[2,2,4,5248]{3,2,1,0:T(4,128)(2,1)S(1)} %get-tuple-element.13), channel_id=1, source_target_pairs={{0,1},{1,0},{2,3},{3,2},{4,5},{5,4},{6,7},{7,6},{8,9},{9,8},{10,11... | collective-permute-start | bytes 503816 | tf_op jit(solution)/shard_map/ppermute | solution.py:330
  16.3 0.1 fusion.1
  16.4 0.1 fusion.4
  16.5 0.1 negate_bitcast_fusion
  16.5 0.2 collective-permute-done.shared_ref
  16.7 10.6 %collective-permute-start.1 = (f32[1,8,128]{2,1,0:T(8,128)S(1)}, f32[1,8,128]{2,1,0:T(8,128)S(1)}, u32[]{:S(2)}, u32[]{:S(2)}) collective-permute-start(f32[1,8,128]{2,1,0:T(8,128)S(1)} %fusion), channel_id=1, source_target_pairs={{0,8},{1,9},{2,10},{3,11},{4,12},{5,13},{6,14},{7,15},{8,0},{9,1},... | collective-permute-start | bytes 12296 | tf_op jit(solution)/shard_map/ppermute | solution.py:325
  27.4 0.1 fusion.3
  27.4 0.9 %collective-permute-done.1 = f32[1,8,128]{2,1,0:T(8,128)S(1)} collective-permute-done((f32[1,8,128]{2,1,0:T(8,128)S(1)}, f32[1,8,128]{2,1,0:T(8,128)S(1)}, u32[]{:S(2)}, u32[]{:S(2)}) %collective-permute-start.1) | collective-permute-done | bytes 4128 | tf_op jit(solution)/shard_map/ppermute | solution.py:325
  28.3 0.0 all-to-all-done.arrived_ref
  28.3 0.2 shard_map.105.mine_ref
  28.5 3.1 %collective-permute-start.2 = (f32[8,4,128]{2,1,0:T(4,128)S(1)}, f32[8,4,128]{2,1,0:T(4,128)S(1)}, u32[]{:S(2)}, u32[]{:S(2)}) collective-permute-start(f32[8,4,128]{2,1,0:T(4,128)S(1)} %shard_map.105.mine_ref), channel_id=1, source_target_pairs={{0,1},{1,0},{2,3},{3,2},{4,5},{5,4},{6,7},{7,6},{8,9},{9,8},{10,11... | collective-permute-start | bytes 49160 | tf_op jit(solution)/shard_map/ppermute | solution.py:344
  31.6 0.1 broadcast_select_fusion
  31.7 4.2 %collective-permute-start.3 = (f32[2,8,128]{2,1,0:T(8,128)S(1)}, f32[2,8,128]{2,1,0:T(8,128)S(1)}, u32[]{:S(2)}, u32[]{:S(2)}) collective-permute-start(f32[2,8,128]{2,1,0:T(8,128)S(1)} %pad_maximum_fusion.1.groups_ref), channel_id=1, source_target_pairs={{0,4},{1,5},{2,6},{3,7},{4,0},{5,1},{6,2},{7,3},{8,12},{9,13},{10,... | collective-permute-start | bytes 24584 | tf_op jit(solution)/shard_map/ppermute | solution.py:325
  35.9 0.0 collective-permute-done.2.other_ref
  35.9 0.9 %shard_map.106 = (f32[32,8,128]{2,1,0:T(8,128)}, s32[8]{0:T(128)S(4)}) custom-call(s32[8]{0:T(128)S(4)} %get-tuple-element.10.index_ref, f32[8,4,128]{2,1,0:T(4,128)S(1)} %shard_map.105.mine_ref, f32[8,4,128]{2,1,0:T(4,128)S(1)} %collective-permute-done.2.other_ref, bf16[2,2,4,5120]{3,2,1,0:T(4,128)(2,1)S(1)} %get-tuple-element.12.own_ref, ...), custom_call_target="tpu_custom_call" | custom-call | flops 1000000 | bytes 1000000 | tf_op jit(solution)/shard_map/pallas_call | solution.py:27
  36.7 9.5 %all-to-all-start.1 = ((f32[32,8,128]{2,1,0:T(8,128)}), f32[32,8,128]{2,1,0:T(8,128)S(1)}, u32[]{:S(2)}, u32[]{:S(2)}) async-start(f32[32,8,128]{2,1,0:T(8,128)} %get-tuple-element.15), calls=%async_computation.1 | async-start | bytes 262144 | tf_op jit(solution)/shard_map/all_to_all | solution.py:352
  46.2 0.1 fusion.5
  46.3 0.0 collective-permute-done.3
  46.3 3.1 %collective-permute-start.4 = (f32[4,8,128]{2,1,0:T(8,128)S(1)}, f32[4,8,128]{2,1,0:T(8,128)S(1)}, u32[]{:S(2)}, u32[]{:S(2)}) collective-permute-start(f32[4,8,128]{2,1,0:T(8,128)S(1)} %pad_maximum_fusion.near_ref), channel_id=1, source_target_pairs={{0,2},{1,3},{2,0},{3,1},{4,6},{5,7},{6,4},{7,5},{8,10},{9,11},{10,... | collective-permute-start | bytes 49160 | tf_op jit(solution)/shard_map/ppermute | solution.py:325
  49.4 0.1 maximum_bitcast_fusion
  49.5 2.0 %shard_map.107.base_ref = f32[1,128]{1,0:T(1,128)S(1)} custom-call(s32[8]{0:T(128)S(4)} %get-tuple-element.16.mark_ref, bf16[1,8192]{1,0:T(2,128)(2,1)S(1)} %get-tuple-element.17.hidden_ref, bf16[8192,128]{1,0:T(8,128)(2,1)} %weight_ref.1), custom_call_target="tpu_custom_call" | custom-call | flops 10000 | bytes 10000 | tf_op jit(solution)/shard_map/pallas_call | solution.py:27
  51.5 0.0 collective-permute-done.4.far_ref
  51.5 0.0 copy-done.1
  51.5 0.5 shard_map.108.partial_ref
  51.9 3.8 %all-to-all-done.1.arrived_ref = f32[32,8,128]{2,1,0:T(8,128)S(1)} async-done(((f32[32,8,128]{2,1,0:T(8,128)}), f32[32,8,128]{2,1,0:T(8,128)S(1)}, u32[]{:S(2)}, u32[]{:S(2)}) %all-to-all-start.1) | async-done | bytes 131104 | tf_op jit(solution)/shard_map/all_to_all | solution.py:352
  55.7 0.6 shard_map.109
  56.3 9.2 %all-to-all-start.2 = ((f32[16,8,128]{2,1,0:T(8,128)}), f32[16,8,128]{2,1,0:T(8,128)S(1)}, u32[]{:S(2)}, u32[]{:S(2)}) async-start(f32[16,8,128]{2,1,0:T(8,128)} %shard_map.109), calls=%async_computation.2 | async-start | bytes 131072 | tf_op jit(solution)/shard_map/all_to_all | solution.py:375
  65.5 0.1 maximum_bitcast_fusion.1
  65.6 7.7 %all-to-all-done.2.arrived_ref = f32[16,8,128]{2,1,0:T(8,128)S(1)} async-done(((f32[16,8,128]{2,1,0:T(8,128)}), f32[16,8,128]{2,1,0:T(8,128)S(1)}, u32[]{:S(2)}, u32[]{:S(2)}) %all-to-all-start.2) | async-done | bytes 65568 | tf_op jit(solution)/shard_map/all_to_all | solution.py:375
  73.3 0.9 %shard_map.110 = (bf16[1,128]{1,0:T(2,128)(2,1)}, bf16[1,512]{1,0:T(2,128)(2,1)}) custom-call(f32[4,128]{1,0:T(4,128)S(1)} %pad_maximum_fusion.2.rot_ref, bf16[1,512]{1,0:T(2,128)(2,1)S(1)} %copy-done.2, f32[16,8,128]{2,1,0:T(8,128)S(1)} %all-to-all-done.2.arrived_ref), custom_call_target="tpu_custom_call" | custom-call | flops 100000 | bytes 100000 | tf_op jit(solution)/shard_map/pallas_call | solution.py:27
  (10 shorter events, 0.0 us)
Async XLA Ops:
  0.6 50.8 %copy-start.1 = (bf16[1,256,1024]{2,1,0:T(8,128)(2,1)S(1)}, bf16[1,256,1024]{2,1,0:T(8,128)(2,1)}, u32[]{:S(2)}) copy-start(bf16[1,256,1024]{2,1,0:T(8,128)(2,1)} %value_ref.1) | copy-start | bytes 1572868
  0.6 50.8 %copy-start = (bf16[1,256,1024]{2,1,0:T(8,128)(2,1)S(1)}, bf16[1,256,1024]{2,1,0:T(8,128)(2,1)}, u32[]{:S(2)}) copy-start(bf16[1,256,1024]{2,1,0:T(8,128)(2,1)} %key_ref.1) | copy-start | bytes 1572868
  2.3 26.0 %all-to-all-start = ((bf16[32,16,256]{2,1,0:T(8,128)(2,1)}), bf16[32,16,256]{2,1,0:T(8,128)(2,1)S(1)}, u32[]{:S(2)}, u32[]{:S(2)}) async-start(bf16[32,16,256]{2,1,0:T(8,128)(2,1)} %get-tuple-element.11), calls=%async_computation | async-start | bytes 524288 | tf_op jit(solution)/shard_map/all_to_all | solution.py:322
  12.8 3.9 %collective-permute-start = (bf16[2,2,4,5248]{3,2,1,0:T(4,128)(2,1)S(1)}, bf16[2,2,4,5248]{3,2,1,0:T(4,128)(2,1)S(1)}, u32[]{:S(2)}, u32[]{:S(2)}) collective-permute-start(bf16[2,2,4,5248]{3,2,1,0:T(4,128)(2,1)S(1)} %get-tuple-element.13), channel_id=1, source_target_pairs={{0,1},{1,0},{2,3},{3,2},{4,5},{5,4},{6,7},{7,6},{8,9},{9,8},{10,11... | collective-permute-start | bytes 503816 | tf_op jit(solution)/shard_map/ppermute | solution.py:330
  16.7 11.6 %collective-permute-start.1 = (f32[1,8,128]{2,1,0:T(8,128)S(1)}, f32[1,8,128]{2,1,0:T(8,128)S(1)}, u32[]{:S(2)}, u32[]{:S(2)}) collective-permute-start(f32[1,8,128]{2,1,0:T(8,128)S(1)} %fusion), channel_id=1, source_target_pairs={{0,8},{1,9},{2,10},{3,11},{4,12},{5,13},{6,14},{7,15},{8,0},{9,1},... | collective-permute-start | bytes 12296 | tf_op jit(solution)/shard_map/ppermute | solution.py:325
  28.5 7.4 %collective-permute-start.2 = (f32[8,4,128]{2,1,0:T(4,128)S(1)}, f32[8,4,128]{2,1,0:T(4,128)S(1)}, u32[]{:S(2)}, u32[]{:S(2)}) collective-permute-start(f32[8,4,128]{2,1,0:T(4,128)S(1)} %shard_map.105.mine_ref), channel_id=1, source_target_pairs={{0,1},{1,0},{2,3},{3,2},{4,5},{5,4},{6,7},{7,6},{8,9},{9,8},{10,11... | collective-permute-start | bytes 49160 | tf_op jit(solution)/shard_map/ppermute | solution.py:344
  31.7 41.6 %copy-start.2 = (bf16[1,512]{1,0:T(2,128)(2,1)S(1)}, bf16[1,512]{1,0:T(2,128)(2,1)}, u32[]{:S(2)}) copy-start(bf16[1,512]{1,0:T(2,128)(2,1)} %query_ref.1) | copy-start | bytes 3076
  31.7 14.6 %collective-permute-start.3 = (f32[2,8,128]{2,1,0:T(8,128)S(1)}, f32[2,8,128]{2,1,0:T(8,128)S(1)}, u32[]{:S(2)}, u32[]{:S(2)}) collective-permute-start(f32[2,8,128]{2,1,0:T(8,128)S(1)} %pad_maximum_fusion.1.groups_ref), channel_id=1, source_target_pairs={{0,4},{1,5},{2,6},{3,7},{4,0},{5,1},{6,2},{7,3},{8,12},{9,13},{10,... | collective-permute-start | bytes 24584 | tf_op jit(solution)/shard_map/ppermute | solution.py:325
  36.7 19.0 %all-to-all-start.1 = ((f32[32,8,128]{2,1,0:T(8,128)}), f32[32,8,128]{2,1,0:T(8,128)S(1)}, u32[]{:S(2)}, u32[]{:S(2)}) async-start(f32[32,8,128]{2,1,0:T(8,128)} %get-tuple-element.15), calls=%async_computation.1 | async-start | bytes 262144 | tf_op jit(solution)/shard_map/all_to_all | solution.py:352
  46.3 5.1 %collective-permute-start.4 = (f32[4,8,128]{2,1,0:T(8,128)S(1)}, f32[4,8,128]{2,1,0:T(8,128)S(1)}, u32[]{:S(2)}, u32[]{:S(2)}) collective-permute-start(f32[4,8,128]{2,1,0:T(8,128)S(1)} %pad_maximum_fusion.near_ref), channel_id=1, source_target_pairs={{0,2},{1,3},{2,0},{3,1},{4,6},{5,7},{6,4},{7,5},{8,10},{9,11},{10,... | collective-permute-start | bytes 49160 | tf_op jit(solution)/shard_map/ppermute | solution.py:325
  56.3 17.0 %all-to-all-start.2 = ((f32[16,8,128]{2,1,0:T(8,128)}), f32[16,8,128]{2,1,0:T(8,128)S(1)}, u32[]{:S(2)}, u32[]{:S(2)}) async-start(f32[16,8,128]{2,1,0:T(8,128)} %shard_map.109), calls=%async_computation.2 | async-start | bytes 131072 | tf_op jit(solution)/shard_map/all_to_all | solution.py:375

commit v9 on v8

--- a/solution.py
+++ b/solution.py
@@ -133,7 +133,7 @@
         send.wait()
 
 
-def reduce_kernel(index_ref, arrived_ref, own_ref, shared_ref, groups_ref, out_ref):
+def reduce_kernel(index_ref, arrived_ref, own_ref, shared_ref, near_ref, out_ref):
     rows, lanes = arrived_ref.shape[1:]
     half = rows * lanes
     for a in range(2):
@@ -172,7 +172,7 @@
 
 
 def attention_kernel(
-    length_ref, mark_ref, near_ref, far_ref, key_ref, value_ref, out_ref
+    length_ref, mark_ref, before_ref, near_ref, after_ref, key_ref, value_ref, out_ref
 ):
     span = key_ref.shape[1]
     t = lax.axis_index("tensor")
@@ -181,9 +181,14 @@
     v = value_ref[0]
     scores = []
     for g in range(KVH):
-        away = jnp.bitwise_xor(lax.shift_right_logical(t, 1), g)
-        row = lax.shift_right_logical(away, 2) + jnp.bitwise_and(away, 2)
-        q = jnp.where(jnp.bitwise_and(away, 1) == 0, near_ref[row], far_ref[row]).astype(BF16)
+        place = jnp.bitwise_and(g - lax.shift_right_logical(t, 1) + 4, 7)
+        row = lax.shift_right_logical(place * 11, 5)
+        part = place - 3 * row
+        q = jnp.where(
+            part == 0,
+            before_ref[row],
+            jnp.where(part == 1, near_ref[row], after_ref[row]),
+        ).astype(BF16)
         scores.append(
             lax.dot_general(
                 q,
@@ -321,24 +326,23 @@
     )
     parts = lax.all_to_all(parts, "sess", 0, 0, tiled=True)
 
-    def swap(x, distance):
-        return lax.ppermute(
-            x, "tensor", [(i, i ^ (2 * distance)) for i in range(n_tensor)]
-        )
-
     other_core = [(i, i ^ 1) for i in range(n_tensor)]
     shared = lax.ppermute(shared, "tensor", other_core)
     pair = own_queries + shared[0, :, :, half + KVH * HD :].reshape(8, HD).astype(F32)
     pair = pair[None]
-    two_groups = jnp.concatenate([pair, swap(pair, 4)])
-    near = jnp.concatenate([two_groups, swap(two_groups, 2)])
-    far = swap(near, 1)
+    def come(x, distance):
+        return lax.ppermute(
+            x, "tensor", [(i, (i - 2 * distance) % n_tensor) for i in range(n_tensor)]
+        )
+
+    near = jnp.concatenate([come(pair, -3), pair, come(pair, 3)])
+    before, after = come(near, -1), come(near, 1)
 
     mine = call(
         reduce_kernel,
         shape((slots * two * 2, ranks, HD), F32),
         [SMEM, VMEM, VMEM, VMEM, ANY],
-        [index, parts, own, shared, two_groups],
+        [index, parts, own, shared, near],
         10**6,
     )
     other = lax.ppermute(mine, "tensor", other_core)
@@ -354,8 +358,8 @@
     partial = call(
         attention_kernel,
         shape((n_tensor, 8, HD), F32),
-        [SMEM, SMEM, VMEM, VMEM, VMEM, VMEM],
-        [lengths, mark, near, far, cached_key_rows, cached_value_rows],
+        [SMEM, SMEM, VMEM, VMEM, VMEM, VMEM, VMEM],
+        [lengths, mark, before, near, after, cached_key_rows, cached_value_rows],
         10**7,
     )
     base = call(

time: 74.7 us -> 74.9 us (level)
  waiting for transfers between devices: 12.6 us -> 15.5 us
  starting transfers between devices: 53 us -> 50.2 us
    ppermute x3 -> x4, waiting for transfers between devices: 0.93 us -> 5.9 us  [come(): lax.ppermute(x, 'tensor', [(i, (i - 2 * distance) % n_tensor) for i in ra...]
    all_to_all x1, starting transfers between devices: 9.18 us -> 5.83 us  [local(): packed = lax.all_to_all(packed, 'tensor', 0, 0, tiled=True)]
    all_to_all x1, waiting for transfers between devices: 3.76 us -> 0.88 us  [local(): terms = lax.all_to_all(terms, 'sess', 0, 0, tiled=True)]
    ppermute x3 -> x4, starting transfers between devices: 17.9 us -> 17.8 us  [come(): lax.ppermute(x, 'tensor', [(i, (i - 2 * distance) % n_tensor) for i in ra...]
  transfers between devices with their start and end apart: 8 -> 9, of which waited for: 4 -> 6; matrix products, arithmetic and copies ran while one was open for 1% -> 1% of each run, Pallas kernels for 4% -> 3%
where the time goes in v9:
time: 74.9 us; the launch traced here: 74.3 us
  starting transfers between devices  50.2 us (67%)
  waiting for transfers between devices  15.5 us (21%)
  Pallas kernels  6.64 us (9%)
  between operations  1.43 us (2%)
    ppermute x4, starting transfers between devices, come(): lax.ppermute(x, 'tensor', [(i, (i - 2 * distance) % n_tensor) for i in ra...  17.8 us
    all_to_all x1, starting transfers between devices, local(): parts = lax.all_to_all(parts, 'sess', 0, 0, tiled=True)  10.5 us
    all_to_all x1, starting transfers between devices, local(): terms = lax.all_to_all(terms, 'sess', 0, 0, tiled=True)  9.49 us
    all_to_all x1, waiting for transfers between devices, local(): packed = lax.all_to_all(packed, 'tensor', 0, 0, tiled=True)  7.72 us
    ppermute x4, waiting for transfers between devices, come(): lax.ppermute(x, 'tensor', [(i, (i - 2 * distance) % n_tensor) for i in ra...  5.9 us
    all_to_all x1, starting transfers between devices, local(): packed = lax.all_to_all(packed, 'tensor', 0, 0, tiled=True)  5.83 us
    pallas_call x6, Pallas kernels, call(): pl.pallas_call(body, out_shape=out_shape, in_specs=specs, out_specs=jax.t...  4.97 us
    ppermute x1, starting transfers between devices, local(): other = lax.ppermute(mine, 'tensor', other_core)  3.69 us
  transfers between devices with their start and end apart: 9, of which 6 were waited for; matrix products, arithmetic and copies ran while one was open for 1% of the time, Pallas kernels for 3%

profile of v9, /device:TPU:1, one launch (start us, length us, event | category | flops | bytes accessed | tf_op | source)
XLA Modules:
  0.0 74.3 jit_solution(16755421080082247894)
XLA Ops:
  0.7 1.7 %shard_map.104 = (bf16[32,16,256]{2,1,0:T(8,128)(2,1)}, f32[8,128]{1,0:T(8,128)S(1)}, s32[8]{0:T(128)S(4)}, bf16[2,2,4,5248]{3,2,1,0:T(4,128)(2,1)S(1)}, bf16[2,...) custom-call(s32[32]{0:T(128)} %slot_hbm.1, bf16[1,8192]{1,0:T(2,128)(2,1)} %hidden_hbm.1, ...), custom_call_target="tpu_custom_call" | custom-call | flops 100000 | bytes 100000 | tf_op jit(solution)/shard_map/pallas_call | solution.py:294
  2.3 10.5 %all-to-all-start = ((bf16[32,16,256]{2,1,0:T(8,128)(2,1)}), bf16[32,16,256]{2,1,0:T(8,128)(2,1)S(1)}, u32[]{:S(2)}, u32[]{:S(2)}) async-start(bf16[32,16,256]{2,1,0:T(8,128)(2,1)} %get-tuple-element.11), calls=%async_computation | async-start | bytes 524288 | tf_op jit(solution)/shard_map/all_to_all | solution.py:327
  12.8 2.9 %collective-permute-start = (bf16[2,2,4,5248]{3,2,1,0:T(4,128)(2,1)S(1)}, bf16[2,2,4,5248]{3,2,1,0:T(4,128)(2,1)S(1)}, u32[]{:S(2)}, u32[]{:S(2)}) collective-permute-start(bf16[2,2,4,5248]{3,2,1,0:T(4,128)(2,1)S(1)} %get-tuple-element.13), channel_id=1, source_target_pairs={{0,1},{1,0},{2,3},{3,2},{4,5},{5,4},{6,7},{7,6},{8,9},{9,8},{10,11... | collective-permute-start | bytes 503816 | tf_op jit(solution)/shard_map/ppermute | solution.py:330
  16.4 0.1 fusion.1
  16.4 0.1 fusion.4
  16.5 0.2 collective-permute-done.shared_ref
  16.7 10.6 %collective-permute-start.2 = (f32[1,8,128]{2,1,0:T(8,128)S(1)}, f32[1,8,128]{2,1,0:T(8,128)S(1)}, u32[]{:S(2)}, u32[]{:S(2)}) collective-permute-start(f32[1,8,128]{2,1,0:T(8,128)S(1)} %fusion), channel_id=1, source_target_pairs={{0,10},{1,11},{2,12},{3,13},{4,14},{5,15},{6,0},{7,1},{8,2},{9,3},... | collective-permute-start | bytes 12296 | tf_op jit(solution)/shard_map/ppermute | solution.py:334
  27.4 1.9 %collective-permute-start.1 = (f32[1,8,128]{2,1,0:T(8,128)S(1)}, f32[1,8,128]{2,1,0:T(8,128)S(1)}, u32[]{:S(2)}, u32[]{:S(2)}) collective-permute-start(f32[1,8,128]{2,1,0:T(8,128)S(1)} %fusion), channel_id=1, source_target_pairs={{0,6},{1,7},{2,8},{3,9},{4,10},{5,11},{6,12},{7,13},{8,14},{9,15},... | collective-permute-start | bytes 12296 | tf_op jit(solution)/shard_map/ppermute | solution.py:334
  29.3 0.1 negate_bitcast_fusion
  29.4 0.0 collective-permute-done.2
  29.4 5.4 %collective-permute-done.1 = f32[1,8,128]{2,1,0:T(8,128)S(1)} collective-permute-done((f32[1,8,128]{2,1,0:T(8,128)S(1)}, f32[1,8,128]{2,1,0:T(8,128)S(1)}, u32[]{:S(2)}, u32[]{:S(2)}) %collective-permute-start.1) | collective-permute-done | bytes 4128 | tf_op jit(solution)/shard_map/ppermute | solution.py:334
  34.7 0.2 shard_map.105.mine_ref
  34.9 3.7 %collective-permute-start.3 = (f32[8,4,128]{2,1,0:T(4,128)S(1)}, f32[8,4,128]{2,1,0:T(4,128)S(1)}, u32[]{:S(2)}, u32[]{:S(2)}) collective-permute-start(f32[8,4,128]{2,1,0:T(4,128)S(1)} %shard_map.105.mine_ref), channel_id=1, source_target_pairs={{0,1},{1,0},{2,3},{3,2},{4,5},{5,4},{6,7},{7,6},{8,9},{9,8},{10,11... | collective-permute-start | bytes 49160 | tf_op jit(solution)/shard_map/ppermute | solution.py:348
  38.6 0.1 fusion.3
  38.7 0.0 copy-start.2
  38.7 0.8 %collective-permute-done.3.other_ref = f32[8,4,128]{2,1,0:T(4,128)S(1)} collective-permute-done((f32[8,4,128]{2,1,0:T(4,128)S(1)}, f32[8,4,128]{2,1,0:T(4,128)S(1)}, u32[]{:S(2)}, u32[]{:S(2)}) %collective-permute-start.3) | collective-permute-done | bytes 16416 | tf_op jit(solution)/shard_map/ppermute | solution.py:348
  39.4 0.9 %shard_map.106 = (f32[32,8,128]{2,1,0:T(8,128)}, s32[8]{0:T(128)S(4)}) custom-call(s32[8]{0:T(128)S(4)} %get-tuple-element.10.index_ref, f32[8,4,128]{2,1,0:T(4,128)S(1)} %shard_map.105.mine_ref, f32[8,4,128]{2,1,0:T(4,128)S(1)} %collective-permute-done.3.other_ref, bf16[2,2,4,5120]{3,2,1,0:T(4,128)(2,1)S(1)} %get-tuple-element.12.own_ref, ...), custom_call_target="tpu_custom_call" | custom-call | flops 1000000 | bytes 1000000 | tf_op jit(solution)/shard_map/pallas_call | solution.py:27
  40.3 9.5 %all-to-all-start.1 = ((f32[32,8,128]{2,1,0:T(8,128)}), f32[32,8,128]{2,1,0:T(8,128)S(1)}, u32[]{:S(2)}, u32[]{:S(2)}) async-start(f32[32,8,128]{2,1,0:T(8,128)} %get-tuple-element.15), calls=%async_computation.1 | async-start | bytes 262144 | tf_op jit(solution)/shard_map/all_to_all | solution.py:356
  49.8 0.1 fusion.5
  49.9 0.1 broadcast_select_fusion
  49.9 1.9 %collective-permute-start.5 = (f32[3,8,128]{2,1,0:T(8,128)S(1)}, f32[3,8,128]{2,1,0:T(8,128)S(1)}, u32[]{:S(2)}, u32[]{:S(2)}) collective-permute-start(f32[3,8,128]{2,1,0:T(8,128)S(1)} %pad_maximum_fusion.near_ref), channel_id=1, source_target_pairs={{0,14},{1,15},{2,0},{3,1},{4,2},{5,3},{6,4},{7,5},{8,6},{9,7},{10,... | collective-permute-start | bytes 36872 | tf_op jit(solution)/shard_map/ppermute | solution.py:334
  51.9 3.4 %collective-permute-start.4 = (f32[3,8,128]{2,1,0:T(8,128)S(1)}, f32[3,8,128]{2,1,0:T(8,128)S(1)}, u32[]{:S(2)}, u32[]{:S(2)}) collective-permute-start(f32[3,8,128]{2,1,0:T(8,128)S(1)} %pad_maximum_fusion.near_ref), channel_id=1, source_target_pairs={{0,2},{1,3},{2,4},{3,5},{4,6},{5,7},{6,8},{7,9},{8,10},{9,11},{10,... | collective-permute-start | bytes 36872 | tf_op jit(solution)/shard_map/ppermute | solution.py:334
  55.2 0.1 maximum_bitcast_fusion
  55.3 2.0 %shard_map.107.base_ref = f32[1,128]{1,0:T(1,128)S(1)} custom-call(s32[8]{0:T(128)S(4)} %get-tuple-element.16.mark_ref, bf16[1,8192]{1,0:T(2,128)(2,1)S(1)} %get-tuple-element.17.hidden_ref, bf16[8192,128]{1,0:T(8,128)(2,1)} %weight_ref.1), custom_call_target="tpu_custom_call" | custom-call | flops 10000 | bytes 10000 | tf_op jit(solution)/shard_map/pallas_call | solution.py:27
  57.3 0.5 collective-permute-done.4.before_ref
  57.8 0.5 shard_map.108.partial_ref
  58.3 0.9 %all-to-all-done.1.arrived_ref = f32[32,8,128]{2,1,0:T(8,128)S(1)} async-done(((f32[32,8,128]{2,1,0:T(8,128)}), f32[32,8,128]{2,1,0:T(8,128)S(1)}, u32[]{:S(2)}, u32[]{:S(2)}) %all-to-all-start.1) | async-done | bytes 131104 | tf_op jit(solution)/shard_map/all_to_all | solution.py:356
  59.1 0.7 shard_map.109
  59.8 5.8 %all-to-all-start.2 = ((f32[16,8,128]{2,1,0:T(8,128)}), f32[16,8,128]{2,1,0:T(8,128)S(1)}, u32[]{:S(2)}, u32[]{:S(2)}) async-start(f32[16,8,128]{2,1,0:T(8,128)} %shard_map.109), calls=%async_computation.2 | async-start | bytes 131072 | tf_op jit(solution)/shard_map/all_to_all | solution.py:379
  65.6 0.1 maximum_bitcast_fusion.1
  65.7 7.7 %all-to-all-done.2.arrived_ref = f32[16,8,128]{2,1,0:T(8,128)S(1)} async-done(((f32[16,8,128]{2,1,0:T(8,128)}), f32[16,8,128]{2,1,0:T(8,128)S(1)}, u32[]{:S(2)}, u32[]{:S(2)}) %all-to-all-start.2) | async-done | bytes 65568 | tf_op jit(solution)/shard_map/all_to_all | solution.py:379
  73.4 0.9 %shard_map.110 = (bf16[1,128]{1,0:T(2,128)(2,1)}, bf16[1,512]{1,0:T(2,128)(2,1)}) custom-call(f32[4,128]{1,0:T(4,128)S(1)} %pad_maximum_fusion.1.rot_ref, bf16[1,512]{1,0:T(2,128)(2,1)S(1)} %copy-done.2, f32[16,8,128]{2,1,0:T(8,128)S(1)} %all-to-all-done.2.arrived_ref), custom_call_target="tpu_custom_call" | custom-call | flops 100000 | bytes 100000 | tf_op jit(solution)/shard_map/pallas_call | solution.py:27
  (11 shorter events, 0.0 us)
Async XLA Ops:
  0.6 57.2 %copy-start.1 = (bf16[1,256,1024]{2,1,0:T(8,128)(2,1)S(1)}, bf16[1,256,1024]{2,1,0:T(8,128)(2,1)}, u32[]{:S(2)}) copy-start(bf16[1,256,1024]{2,1,0:T(8,128)(2,1)} %value_ref.1) | copy-start | bytes 1572868
  0.6 57.2 %copy-start = (bf16[1,256,1024]{2,1,0:T(8,128)(2,1)S(1)}, bf16[1,256,1024]{2,1,0:T(8,128)(2,1)}, u32[]{:S(2)}) copy-start(bf16[1,256,1024]{2,1,0:T(8,128)(2,1)} %key_ref.1) | copy-start | bytes 1572868
  2.3 32.4 %all-to-all-start = ((bf16[32,16,256]{2,1,0:T(8,128)(2,1)}), bf16[32,16,256]{2,1,0:T(8,128)(2,1)S(1)}, u32[]{:S(2)}, u32[]{:S(2)}) async-start(bf16[32,16,256]{2,1,0:T(8,128)(2,1)} %get-tuple-element.11), calls=%async_computation | async-start | bytes 524288 | tf_op jit(solution)/shard_map/all_to_all | solution.py:327
  12.8 3.9 %collective-permute-start = (bf16[2,2,4,5248]{3,2,1,0:T(4,128)(2,1)S(1)}, bf16[2,2,4,5248]{3,2,1,0:T(4,128)(2,1)S(1)}, u32[]{:S(2)}, u32[]{:S(2)}) collective-permute-start(bf16[2,2,4,5248]{3,2,1,0:T(4,128)(2,1)S(1)} %get-tuple-element.13), channel_id=1, source_target_pairs={{0,1},{1,0},{2,3},{3,2},{4,5},{5,4},{6,7},{7,6},{8,9},{9,8},{10,11... | collective-permute-start | bytes 503816 | tf_op jit(solution)/shard_map/ppermute | solution.py:330
  16.7 12.6 %collective-permute-start.2 = (f32[1,8,128]{2,1,0:T(8,128)S(1)}, f32[1,8,128]{2,1,0:T(8,128)S(1)}, u32[]{:S(2)}, u32[]{:S(2)}) collective-permute-start(f32[1,8,128]{2,1,0:T(8,128)S(1)} %fusion), channel_id=1, source_target_pairs={{0,10},{1,11},{2,12},{3,13},{4,14},{5,15},{6,0},{7,1},{8,2},{9,3},... | collective-permute-start | bytes 12296 | tf_op jit(solution)/shard_map/ppermute | solution.py:334
  27.4 7.4 %collective-permute-start.1 = (f32[1,8,128]{2,1,0:T(8,128)S(1)}, f32[1,8,128]{2,1,0:T(8,128)S(1)}, u32[]{:S(2)}, u32[]{:S(2)}) collective-permute-start(f32[1,8,128]{2,1,0:T(8,128)S(1)} %fusion), channel_id=1, source_target_pairs={{0,6},{1,7},{2,8},{3,9},{4,10},{5,11},{6,12},{7,13},{8,14},{9,15},... | collective-permute-start | bytes 12296 | tf_op jit(solution)/shard_map/ppermute | solution.py:334
  34.9 4.5 %collective-permute-start.3 = (f32[8,4,128]{2,1,0:T(4,128)S(1)}, f32[8,4,128]{2,1,0:T(4,128)S(1)}, u32[]{:S(2)}, u32[]{:S(2)}) collective-permute-start(f32[8,4,128]{2,1,0:T(4,128)S(1)} %shard_map.105.mine_ref), channel_id=1, source_target_pairs={{0,1},{1,0},{2,3},{3,2},{4,5},{5,4},{6,7},{7,6},{8,9},{9,8},{10,11... | collective-permute-start | bytes 49160 | tf_op jit(solution)/shard_map/ppermute | solution.py:348
  38.7 34.8 %copy-start.2 = (bf16[1,512]{1,0:T(2,128)(2,1)S(1)}, bf16[1,512]{1,0:T(2,128)(2,1)}, u32[]{:S(2)}) copy-start(bf16[1,512]{1,0:T(2,128)(2,1)} %query_ref.1) | copy-start | bytes 3076
  40.3 18.8 %all-to-all-start.1 = ((f32[32,8,128]{2,1,0:T(8,128)}), f32[32,8,128]{2,1,0:T(8,128)S(1)}, u32[]{:S(2)}, u32[]{:S(2)}) async-start(f32[32,8,128]{2,1,0:T(8,128)} %get-tuple-element.15), calls=%async_computation.1 | async-start | bytes 262144 | tf_op jit(solution)/shard_map/all_to_all | solution.py:356
  49.9 7.3 %collective-permute-start.5 = (f32[3,8,128]{2,1,0:T(8,128)S(1)}, f32[3,8,128]{2,1,0:T(8,128)S(1)}, u32[]{:S(2)}, u32[]{:S(2)}) collective-permute-start(f32[3,8,128]{2,1,0:T(8,128)S(1)} %pad_maximum_fusion.near_ref), channel_id=1, source_target_pairs={{0,14},{1,15},{2,0},{3,1},{4,2},{5,3},{6,4},{7,5},{8,6},{9,7},{10,... | collective-permute-start | bytes 36872 | tf_op jit(solution)/shard_map/ppermute | solution.py:334
  51.9 5.9 %collective-permute-start.4 = (f32[3,8,128]{2,1,0:T(8,128)S(1)}, f32[3,8,128]{2,1,0:T(8,128)S(1)}, u32[]{:S(2)}, u32[]{:S(2)}) collective-permute-start(f32[3,8,128]{2,1,0:T(8,128)S(1)} %pad_maximum_fusion.near_ref), channel_id=1, source_target_pairs={{0,2},{1,3},{2,4},{3,5},{4,6},{5,7},{6,8},{7,9},{8,10},{9,11},{10,... | collective-permute-start | bytes 36872 | tf_op jit(solution)/shard_map/ppermute | solution.py:334
  59.8 13.6 %all-to-all-start.2 = ((f32[16,8,128]{2,1,0:T(8,128)}), f32[16,8,128]{2,1,0:T(8,128)S(1)}, u32[]{:S(2)}, u32[]{:S(2)}) async-start(f32[16,8,128]{2,1,0:T(8,128)} %shard_map.109), calls=%async_computation.2 | async-start | bytes 131072 | tf_op jit(solution)/shard_map/all_to_all | solution.py:379
